TPU v7x, 256 devices: a whole 4x4x8 slice. The times are simulated.
256 devices in a mesh: grp: 4 (over x_lo, core), blk: 64 (over x_hi, z, y).
Axes of the slice: x: 4 (x_hi: 2, x_lo: 2; x = x_hi * 2 + x_lo), y: 4, z: 8, core: 2. Of those that a mesh axis runs over, the one named last changes fastest.
Arguments:
- masses: bfloat16 [64, 2, 256, 256], P('blk'), may hold values from -3 to 3
- spins: int32 [64, 256], P('blk'), may hold values from 0 to 1
- shift_table: int32 [256, 256], P('blk'), may hold values from 0 to 255, as said below
- flip_table: int32 [256, 256], P('blk'), may hold values from 0 to 255, as said below
- ph_in: float32 [2, 256, 256, 256], P(None, 'blk', 'grp'), may hold values from -6 to 6
- pp_in: float32 [2, 256, 256, 256], P(None, 'blk', 'grp'), may hold values from -6 to 6
Outputs:
- ph_out: float32 [2, 256, 256, 256], P(None, 'blk', 'grp')
- pp_out: float32 [2, 256, 256, 256], P(None, 'blk', 'grp')
Inputs may be any that keep to these rules, and one draw needn't show every extreme that they name: Row t of shift_table maps w * 16 + k to ((w + n_t) mod 16) * 16 + (k + q_t) mod 16 for some integers n_t, q_t of the transfer; every row is a permutation. Row t of flip_table maps w * 16 + k to ((n_t - w - 1) mod 16) * 16 + (q_t - k) mod 16 with the same n_t, q_t as shift_table's row t.
All inputs are finite; a program needn't handle non-finite values.
Results may differ from a plain program's by a relative error of at most 0.0064.
Values may be sent and summed in bfloat16 or wider, within the bound.
No kernel may reach another device: no remote copies, remote signals or barrier semaphores. Data moves between devices by JAX's collectives and lax.ppermute only.
A program may use at most 128 MiB of HBM per device.

v0:
```python
import math

import jax
import jax.numpy as jnp
from jax import lax
from jax.sharding import PartitionSpec as P

NW = 16
NK = 16


COUPLING = 0.5


def shifted(value, axis, steps):
    count = lax.axis_size(axis)
    pairs = [(source, (source + steps) % count) for source in range(count)]
    return lax.ppermute(value, axis, pairs)


def dft_tables():
    index = jnp.arange(NW * NK, dtype=jnp.int32)
    frequency = index // NK
    momentum = index % NK
    numerator = (
        (2 * frequency[:, None] + 1) * frequency[None, :] * NK
        - 2 * momentum[:, None] * momentum[None, :] * NW
    ) % (2 * NW * NK)
    phase = numerator.astype(jnp.float32) * (math.pi / (NW * NK))
    norm_scale = 1.0 / math.sqrt(NW * NK)
    return (
        (jnp.cos(phase) * norm_scale).astype(jnp.bfloat16),
        (jnp.sin(phase) * norm_scale).astype(jnp.bfloat16),
    )


def build_band(masses, spins, rows_real, rows_imag, real_table, imag_table):
    signed = (2 * spins - 1).astype(jnp.float32)
    factors = jnp.stack([jnp.exp(COUPLING * signed), jnp.exp(-COUPLING * signed)], 1)
    scaled = (masses.astype(jnp.float32) * factors[:, :, None, :]).astype(jnp.bfloat16)
    first_real = jnp.einsum(
        "ri,wsij->wsrj", rows_real, scaled, preferred_element_type=jnp.float32
    ).astype(jnp.bfloat16)
    first_imag = jnp.einsum(
        "ri,wsij->wsrj", rows_imag, scaled, preferred_element_type=jnp.float32
    ).astype(jnp.bfloat16)
    joined = jnp.concatenate([first_real, first_imag], -1)
    big_table = jnp.concatenate(
        [
            jnp.concatenate([real_table.T, -imag_table.T], 1),
            jnp.concatenate([imag_table.T, real_table.T], 1),
        ],
        0,
    )
    second = jnp.einsum("wsri,ij->wsrj", joined, big_table, preferred_element_type=jnp.float32)
    order = real_table.shape[1]
    return jnp.stack([second[..., :order], second[..., order:]], 2).astype(jnp.bfloat16)


def window_walkers(payload):
    reach = min(8, lax.axis_size("blk") - 1)
    visits = [payload]
    current = payload
    for offset in range(1, reach + 1):
        current = shifted(current, "blk", 1)
        visits.append(current)
    return visits


def cyclic_window(grid, start, length, axis):
    doubled = jnp.concatenate([grid, grid], axis)
    return lax.dynamic_slice_in_dim(doubled, start, length, axis)


def moved_band(view, freq_move, mom_move, first_freq, band_freq):
    rank = view.ndim
    result = cyclic_window(view, mom_move, NK, rank - 1)
    result = cyclic_window(result, freq_move, NW, rank - 2)
    result = cyclic_window(result, mom_move, NK, rank - 3)
    result = cyclic_window(result, first_freq + freq_move, band_freq, rank - 4)
    lead = view.shape[: rank - 4]
    return result.reshape(lead + (band_freq * NK, NW * NK))


def absorb(increment, full, first_row, height, shift_starts, flip_starts):
    band_freq = height // NK
    first_freq = first_row // NK
    propagator = full[0]
    columns = lax.dynamic_slice_in_dim(propagator, first_row, height, 3)
    mirrored = jnp.swapaxes(columns, 2, 3).astype(jnp.float32)
    upper = lax.dynamic_slice_in_dim(propagator[0], first_row, height, 1).astype(jnp.float32)
    view = propagator.reshape(2, 2, NW, NK, NW, NK)
    reversed_lower = view[1, :, ::-1, ::-1, ::-1, ::-1]

    def one_transfer(starts):
        shift_start, flip_start = starts
        shift_freq = shift_start // NK
        shift_mom = shift_start % NK
        flip_freq = (NW - 1 - flip_start // NK) % NW
        flip_mom = (NK - 1 - flip_start % NK) % NK
        moved = moved_band(view, shift_freq, shift_mom, first_freq, band_freq).astype(jnp.float32)
        ph_real = jnp.sum(mirrored[:, 0] * moved[:, 0] - mirrored[:, 1] * moved[:, 1], axis=0)
        ph_imag = jnp.sum(mirrored[:, 0] * moved[:, 1] + mirrored[:, 1] * moved[:, 0], axis=0)
        lowered = moved_band(reversed_lower, flip_freq, flip_mom, first_freq, band_freq).astype(
            jnp.float32
        )
        pp_real = upper[0] * lowered[0] - upper[1] * lowered[1]
        pp_imag = upper[0] * lowered[1] + upper[1] * lowered[0]
        return (jnp.stack([ph_real, ph_imag]), jnp.stack([pp_real, pp_imag]))

    ph_step, pp_step = lax.map(one_transfer, (shift_starts, flip_starts))
    increment = (increment[0] + ph_step, increment[1] + pp_step)
    return increment


def on_device(masses, spins, shift_table, flip_table, ph_in, pp_in):
    groups = lax.axis_size("grp")
    order = masses.shape[-1]
    height = order // groups
    first_row = lax.axis_index("grp") * height
    real_table, imag_table = dft_tables()
    shift_starts = shift_table[:, 0]
    flip_starts = flip_table[:, 0]
    trans_count = shift_table.shape[0]
    empty = jnp.zeros((trans_count, 2, height, order), jnp.float32)
    increment = (empty, empty)
    rows_real = lax.dynamic_slice_in_dim(real_table, first_row, height, 0)
    rows_imag = lax.dynamic_slice_in_dim(imag_table, first_row, height, 0)
    band = build_band(masses, spins, rows_real, rows_imag, real_table, imag_table)
    full = lax.all_gather(band, "grp", axis=3, tiled=True)
    for visit in window_walkers(full):
        increment = absorb(increment, visit, first_row, height, shift_starts, flip_starts)
    return (ph_in + jnp.swapaxes(increment[0], 0, 1), pp_in + jnp.swapaxes(increment[1], 0, 1))


def solution(mesh):
    placed = (
        P("blk", None, None, None),
        P("blk", None),
        P("blk", None),
        P("blk", None),
        P(None, "blk", "grp", None),
        P(None, "blk", "grp", None),
    )
    return jax.shard_map(
        on_device,
        mesh=mesh,
        in_specs=placed,
        out_specs=(P(None, "blk", "grp", None), P(None, "blk", "grp", None)),
        check_vma=False,
    )
```

profile of v0, /device:TPU:1, one launch (start us, length us, event | category | flops | bytes accessed | tf_op | source)
XLA Modules:
  0.0 1240.9 jit_solution(3988342460509089059)
XLA Ops:
  6.8 9.6 all_gather.3
  40.0 109.9 %while.135 = (s32[]{:T(128)}, f32[4,2,64,256]{3,2,0,1:T(8,128)}, f32[4,2,64,256]{3,2,0,1:T(8,128)}, f32[2,2,64,256]{3,2,1,0:T(8,128)S(1)}, s32[4]{0:T(128)S(1)},...) while((s32[]{:T(128)}, f32[4,2,64,256]{3,2,0,1:T(8,128)}, ...), condition=%wide.region_3.4_spmd, body=%wide.region_0.3_spmd.sunk | while | flops 3342420 | bytes 7472173 | solution.py:111
  47.1 8.8 fusion.252
  74.4 8.8 fusion.252
  101.7 8.9 fusion.252
  129.1 8.9 fusion.252
  177.8 111.4 %while.136 = (s32[]{:T(128)}, f32[4,2,64,256]{3,2,0,1:T(8,128)}, f32[4,2,64,256]{3,2,0,1:T(8,128)}, f32[2,2,64,256]{3,2,1,0:T(8,128)S(1)}, s32[4]{0:T(128)S(1)},...) while((s32[]{:T(128)}, f32[4,2,64,256]{3,2,0,1:T(8,128)}, ...), condition=%wide.region_7.8_spmd, body=%wide.region_4.7_spmd.sunk | while | flops 3342420 | bytes 7472173 | solution.py:111
  184.7 8.8 fusion.261
  212.5 8.8 fusion.261
  240.3 8.9 fusion.261
  268.2 8.9 fusion.261
  293.7 7.3 pad_maximum_fusion.2
  313.9 109.7 %while.137 = (s32[]{:T(128)}, f32[4,2,64,256]{3,2,0,1:T(8,128)}, f32[4,2,64,256]{3,2,0,1:T(8,128)}, f32[2,2,64,256]{3,2,1,0:T(8,128)S(1)}, s32[4]{0:T(128)S(1)},...) while((s32[]{:T(128)}, f32[4,2,64,256]{3,2,0,1:T(8,128)}, ...), condition=%wide.region_11.12_spmd, body=%wide.region_8.11_spmd.sunk | while | flops 3342420 | bytes 7472173 | solution.py:111
  320.6 8.8 fusion.270
  348.0 8.8 fusion.270
  375.4 8.9 fusion.270
  402.8 8.9 fusion.270
  451.6 111.0 %while.138 = (s32[]{:T(128)}, f32[4,2,64,256]{3,2,0,1:T(8,128)}, f32[4,2,64,256]{3,2,0,1:T(8,128)}, f32[2,2,64,256]{3,2,1,0:T(8,128)S(1)}, s32[4]{0:T(128)S(1)},...) while((s32[]{:T(128)}, f32[4,2,64,256]{3,2,0,1:T(8,128)}, ...), condition=%wide.region_15.16_spmd, body=%wide.region_12.15_spmd.sunk | while | flops 3342420 | bytes 7472173 | solution.py:111
  458.5 8.8 fusion.279
  486.2 8.8 fusion.279
  513.9 8.9 fusion.279
  541.7 8.9 fusion.279
  567.2 7.3 pad_maximum_fusion.4
  587.6 108.4 %while.139 = (s32[]{:T(128)}, f32[4,2,64,256]{3,2,0,1:T(8,128)}, f32[4,2,64,256]{3,2,0,1:T(8,128)}, f32[2,2,64,256]{3,2,1,0:T(8,128)S(1)}, s32[4]{0:T(128)S(1)},...) while((s32[]{:T(128)}, f32[4,2,64,256]{3,2,0,1:T(8,128)}, ...), condition=%wide.region_19.20_spmd, body=%wide.region_16.19_spmd.sunk | while | flops 3342420 | bytes 7472173 | solution.py:111
  594.1 8.8 fusion.288
  621.2 8.8 fusion.288
  648.3 8.9 fusion.288
  675.4 8.9 fusion.288
  724.0 109.6 %while.140 = (s32[]{:T(128)}, f32[4,2,64,256]{3,2,0,1:T(8,128)}, f32[4,2,64,256]{3,2,0,1:T(8,128)}, f32[2,2,64,256]{3,2,1,0:T(8,128)S(1)}, s32[4]{0:T(128)S(1)},...) while((s32[]{:T(128)}, f32[4,2,64,256]{3,2,0,1:T(8,128)}, ...), condition=%wide.region_23.24_spmd, body=%wide.region_20.23_spmd.sunk | while | flops 3342420 | bytes 7472173 | solution.py:111
  730.7 8.8 fusion.297
  758.0 8.8 fusion.297
  785.4 8.9 fusion.297
  812.8 8.9 fusion.297
  858.3 108.3 %while.141 = (s32[]{:T(128)}, f32[4,2,64,256]{3,2,0,1:T(8,128)}, f32[4,2,64,256]{3,2,0,1:T(8,128)}, f32[2,2,64,256]{3,2,1,0:T(8,128)S(1)}, s32[4]{0:T(128)S(1)},...) while((s32[]{:T(128)}, f32[4,2,64,256]{3,2,0,1:T(8,128)}, ...), condition=%wide.region_27.28_spmd, body=%wide.region_24.27_spmd.sunk | while | flops 3342420 | bytes 7472173 | solution.py:111
  864.8 8.8 fusion.306
  891.8 8.8 fusion.306
  918.9 8.9 fusion.306
  946.0 8.9 fusion.306
  994.6 109.2 %while.142 = (s32[]{:T(128)}, f32[4,2,64,256]{3,2,0,1:T(8,128)}, f32[4,2,64,256]{3,2,0,1:T(8,128)}, f32[2,2,64,256]{3,2,1,0:T(8,128)S(1)}, s32[4]{0:T(128)S(1)},...) while((s32[]{:T(128)}, f32[4,2,64,256]{3,2,0,1:T(8,128)}, ...), condition=%wide.region_31.32_spmd, body=%wide.region_28.31_spmd.sunk | while | flops 3342420 | bytes 7472173 | solution.py:111
  1001.2 8.8 fusion.315
  1028.4 8.8 fusion.315
  1055.7 8.9 fusion.315
  1083.0 8.9 fusion.315
  1126.3 109.0 %while.143 = (s32[]{:T(128)}, f32[4,2,64,256]{3,2,0,1:T(8,128)S(1)}, f32[4,2,64,256]{3,2,0,1:T(8,128)}, f32[2,2,64,256]{3,2,1,0:T(8,128)S(1)}, s32[4]{0:T(128)S(...) while((s32[]{:T(128)}, f32[4,2,64,256]{3,2,0,1:T(8,128)S(1)}, ...), condition=%wide.region_35.36_spmd, body=%wide.region_32.35_spmd.sunk | while | flops 3342420 | bytes 7472173 | solution.py:111
  1133.0 8.8 fusion.324
  1160.2 8.8 fusion.324
  1187.4 8.9 fusion.324
  1214.7 8.9 fusion.324
  (691 shorter events, 704.6 us)
Async XLA Ops:
  16.3 133.5 %collective-permute-start = (bf16[1,2,2,256,256]{4,3,1,2,0:T(8,128)(2,1)S(1)}, bf16[1,2,2,256,256]{4,3,1,2,0:T(8,128)(2,1)}, u32[]{:S(2)}, u32[]{:S(2)}) collective-permute-start(bf16[1,2,2,256,256]{4,3,1,2,0:T(8,128)(2,1)S(1)} %all_gather.3), channel_id=1, source_target_pairs={{0,1},{1,2},{2,3},{3,4},{4,5},{5,6},{6,7},{7,8},{8,9},{9,10},{10,1... | collective-permute-start | bytes 1572872 | tf_op jit(solution)/shard_map/ppermute | solution.py:18
  29.5 8.6 copy-start.10
  29.5 8.6 copy-start.11
  174.8 114.5 %collective-permute-start.1 = (bf16[1,2,2,256,256]{4,3,1,2,0:T(8,128)(2,1)}, bf16[1,2,2,256,256]{4,3,1,2,0:T(8,128)(2,1)S(1)}, u32[]{:S(2)}, u32[]{:S(2)}) collective-permute-start(bf16[1,2,2,256,256]{4,3,1,2,0:T(8,128)(2,1)} %collective-permute-done), channel_id=1, source_target_pairs={{0,1},{1,2},{2,3},{3,4},{4,5},{5,6},{6,7},{7,8},{8,9},{9,10},{10,1... | collective-permute-start | bytes 1572872 | tf_op jit(solution)/shard_map/ppermute | solution.py:18
  311.1 112.5 %collective-permute-start.2 = (bf16[1,2,2,256,256]{4,3,1,2,0:T(8,128)(2,1)S(1)}, bf16[1,2,2,256,256]{4,3,1,2,0:T(8,128)(2,1)}, u32[]{:S(2)}, u32[]{:S(2)}) collective-permute-start(bf16[1,2,2,256,256]{4,3,1,2,0:T(8,128)(2,1)S(1)} %collective-permute-done.1), channel_id=1, source_target_pairs={{0,1},{1,2},{2,3},{3,4},{4,5},{5,6},{6,7},{7,8},{8,9},{9,10},{10,1... | collective-permute-start | bytes 1572872 | tf_op jit(solution)/shard_map/ppermute | solution.py:18
  448.5 114.1 %collective-permute-start.3 = (bf16[1,2,2,256,256]{4,3,1,2,0:T(8,128)(2,1)}, bf16[1,2,2,256,256]{4,3,1,2,0:T(8,128)(2,1)S(1)}, u32[]{:S(2)}, u32[]{:S(2)}) collective-permute-start(bf16[1,2,2,256,256]{4,3,1,2,0:T(8,128)(2,1)} %collective-permute-done.2), channel_id=1, source_target_pairs={{0,1},{1,2},{2,3},{3,4},{4,5},{5,6},{6,7},{7,8},{8,9},{9,10},{10,1... | collective-permute-start | bytes 1572872 | tf_op jit(solution)/shard_map/ppermute | solution.py:18
  584.6 111.5 %collective-permute-start.4 = (bf16[1,2,2,256,256]{4,3,1,2,0:T(8,128)(2,1)S(1)}, bf16[1,2,2,256,256]{4,3,1,2,0:T(8,128)(2,1)}, u32[]{:S(2)}, u32[]{:S(2)}) collective-permute-start(bf16[1,2,2,256,256]{4,3,1,2,0:T(8,128)(2,1)S(1)} %collective-permute-done.3), channel_id=1, source_target_pairs={{0,1},{1,2},{2,3},{3,4},{4,5},{5,6},{6,7},{7,8},{8,9},{9,10},{10,1... | collective-permute-start | bytes 1572872 | tf_op jit(solution)/shard_map/ppermute | solution.py:18
  720.9 112.7 %collective-permute-start.5 = (bf16[1,2,2,256,256]{4,3,1,2,0:T(8,128)(2,1)}, bf16[1,2,2,256,256]{4,3,1,2,0:T(8,128)(2,1)S(1)}, u32[]{:S(2)}, u32[]{:S(2)}) collective-permute-start(bf16[1,2,2,256,256]{4,3,1,2,0:T(8,128)(2,1)} %collective-permute-done.4), channel_id=1, source_target_pairs={{0,1},{1,2},{2,3},{3,4},{4,5},{5,6},{6,7},{7,8},{8,9},{9,10},{10,1... | collective-permute-start | bytes 1572872 | tf_op jit(solution)/shard_map/ppermute | solution.py:18
  855.5 111.1 %collective-permute-start.6 = (bf16[1,2,2,256,256]{4,3,1,2,0:T(8,128)(2,1)S(1)}, bf16[1,2,2,256,256]{4,3,1,2,0:T(8,128)(2,1)}, u32[]{:S(2)}, u32[]{:S(2)}) collective-permute-start(bf16[1,2,2,256,256]{4,3,1,2,0:T(8,128)(2,1)S(1)} %collective-permute-done.5), channel_id=1, source_target_pairs={{0,1},{1,2},{2,3},{3,4},{4,5},{5,6},{6,7},{7,8},{8,9},{9,10},{10,1... | collective-permute-start | bytes 1572872 | tf_op jit(solution)/shard_map/ppermute | solution.py:18
  991.5 112.3 %collective-permute-start.7 = (bf16[1,2,2,256,256]{4,3,1,2,0:T(8,128)(2,1)}, bf16[1,2,2,256,256]{4,3,1,2,0:T(8,128)(2,1)S(1)}, u32[]{:S(2)}, u32[]{:S(2)}) collective-permute-start(bf16[1,2,2,256,256]{4,3,1,2,0:T(8,128)(2,1)} %collective-permute-done.6), channel_id=1, source_target_pairs={{0,1},{1,2},{2,3},{3,4},{4,5},{5,6},{6,7},{7,8},{8,9},{9,10},{10,1... | collective-permute-start | bytes 1572872 | tf_op jit(solution)/shard_map/ppermute | solution.py:18
  1235.3 3.7 copy-start
  1235.3 3.7 copy-start.1
  1235.3 3.7 copy-start.2
  1235.3 3.7 copy-start.3
  1235.3 3.7 copy-start.4
  1235.3 3.7 copy-start.5
  1235.4 3.7 copy-start.6
  1235.4 3.7 copy-start.7
  1235.4 3.7 copy-start.8
  1235.4 3.9 copy-start.9
where the time goes:
time: 1260 us; the launch traced here: 1240 us
  other arithmetic  610 us (48%)
  local copies, waits for them, and re-layouts  416 us (33%)
  loops' own time  191 us (15%)
    concatenate x126, other arithmetic, cyclic_window(): doubled = jnp.concatenate([grid, grid], axis)  536 us
    dynamic_slice x72, local copies, waits for them, and re-layouts, cyclic_window(): return lax.dynamic_slice_in_dim(doubled, start, length, axis)  205 us
    another operation x9, loops' own time, absorb(): ph_step, pp_step = lax.map(one_transfer, (shift_starts, flip_starts))  191 us
    dynamic_slice x72, local copies, waits for them, and re-layouts, absorb(): ph_step, pp_step = lax.map(one_transfer, (shift_starts, flip_starts))  45.4 us
    another operation x9, local copies, waits for them, and re-layouts, absorb(): view = propagator.reshape(2, 2, NW, NK, NW, NK)  42.6 us
    rev x9, local copies, waits for them, and re-layouts, absorb(): reversed_lower = view[1, :, ::-1, ::-1, ::-1, ::-1]  34.6 us
    convert_element_type x36, local copies, waits for them, and re-layouts, one_transfer(): moved_band(view, shift_freq, shift_mom, first_freq, band_freq)  33.8 us
    dynamic_update_slice x36, other arithmetic, absorb(): ph_step, pp_step = lax.map(one_transfer, (shift_starts, flip_starts))  26.4 us
  transfers between devices with their start and end apart: 8, of which 0 were waited for; matrix products, arithmetic and copies ran while one was open for 60% of the time, Pallas kernels for 0%

commit v1 on v0

v1 whole, which is shorter than its diff:
```python
import functools
import math

import jax
import jax.numpy as jnp
from jax import lax
from jax.experimental import pallas as pl
from jax.experimental.pallas import tpu as pltpu
from jax.sharding import PartitionSpec as P

NK = 16
ORDER = 256
BAND = 64
TRANS = 4
COUPLING = 0.5
BF = jnp.bfloat16
F32 = jnp.float32
MIB = 1 << 20


def wave(freq, mom, tau, site):
    turns = ((2 * freq + 1) * tau - 2 * mom * site) & 31
    phase = turns.astype(F32) * (math.pi / 16.0)
    return (jnp.cos(phase) * 0.0625).astype(BF), (jnp.sin(phase) * 0.0625).astype(BF)


def table_kernel(place_ref, shift_ref, flip_ref, cols_ref, rows_ref):
    square = (ORDER, ORDER)
    sub = lax.broadcasted_iota(jnp.int32, square, 0)
    lane = lax.broadcasted_iota(jnp.int32, square, 1)
    re, im = wave(lane >> 4, lane & 15, sub >> 4, sub & 15)
    cols_ref[2 * TRANS, :ORDER] = re
    cols_ref[2 * TRANS, ORDER:] = im
    re, im = wave(sub >> 4, sub & 15, lane >> 4, lane & 15)
    base = jnp.concatenate([re, im], 1)
    band_row = lax.broadcasted_iota(jnp.int32, (BAND, ORDER), 0) + place_ref[0] * BAND
    band_lane = lax.broadcasted_iota(jnp.int32, (BAND, ORDER), 1)

    def put_rows(slot, target):
        pick = jnp.where(band_lane == target, 1.0, 0.0).astype(BF)
        out = jnp.dot(pick, base, preferred_element_type=F32).astype(BF)
        rows_ref[2 * BAND * slot : 2 * BAND * slot + BAND] = out[:, :ORDER]
        rows_ref[2 * BAND * slot + BAND : 2 * BAND * (slot + 1)] = out[:, ORDER:]

    def put_cols(slot, target):
        pick = jnp.where(sub == target, 1.0, 0.0).astype(BF)
        cols_ref[slot] = jnp.dot(cols_ref[2 * TRANS], pick, preferred_element_type=F32).astype(BF)

    put_rows(0, band_row)
    for t in range(TRANS):
        freq, mom = shift_ref[t, 0] >> 4, shift_ref[t, 0] & 15

        def moved(i, freq=freq, mom=mom):
            return ((((i >> 4) + freq) & 15) << 4) + (((i & 15) + mom) & 15)

        put_rows(1 + t, moved(band_row))
        put_cols(t, moved(lane))
        freq, mom = flip_ref[t, 0] >> 4, flip_ref[t, 0] & 15

        def turned(i, freq=freq, mom=mom):
            return (((freq - (i >> 4)) & 15) << 4) + ((mom - (i & 15)) & 15)

        put_rows(1 + TRANS + t, turned(band_row))
        put_cols(TRANS + t, turned(lane))


def tables(place, shift, flip):
    return pl.pallas_call(
        table_kernel,
        out_shape=(
            jax.ShapeDtypeStruct((2 * TRANS + 1, 2 * ORDER, ORDER), BF),
            jax.ShapeDtypeStruct(((2 * TRANS + 1) * 2 * BAND, ORDER), BF),
        ),
        in_specs=[pl.BlockSpec(memory_space=pltpu.SMEM)] * 3,
        out_specs=(pl.BlockSpec(memory_space=pltpu.VMEM),) * 2,
        cost_estimate=pl.CostEstimate(flops=2 * 10**9, bytes_accessed=3 * 10**6, transcendentals=0),
        compiler_params=pltpu.CompilerParams(vmem_limit_bytes=20 * MIB),
        name="tables",
    )(place, shift, flip)


def paired(re, im):
    return jnp.concatenate(
        [jnp.concatenate([re, im], 1), jnp.concatenate([im, -re], 1)], 0
    )


def halves(ref, begin):
    return paired(ref[begin : begin + BAND], ref[begin + BAND : begin + 2 * BAND])


def one_walker(up, down, cols, rows, ph, pp, first_up, first_down, plain):
    step = 2 * BAND
    first_up[...] = jnp.dot(rows[: step * (TRANS + 1)], up, preferred_element_type=F32).astype(BF)
    first_down[...] = jnp.dot(rows[step:], down, preferred_element_type=F32).astype(BF)
    across = (((1,), (1,)), ((), ()))
    turned_up = lax.dot_general(rows[:step], up, across, preferred_element_type=F32).astype(BF)
    turned_down = lax.dot_general(rows[:step], down, across, preferred_element_type=F32).astype(BF)
    left = jnp.concatenate(
        [halves(turned_up, 0), halves(turned_down, 0), halves(first_up, 0)], 0
    )
    plain[...] = jnp.dot(left, cols[2 * TRANS], preferred_element_type=F32)
    for t in range(TRANS):
        left = jnp.concatenate([halves(first_up, step * (1 + t)), halves(first_down, step * t)], 0)
        moved = jnp.dot(left, cols[t], preferred_element_type=F32)
        real, imag = 0.0, 0.0
        for s in range(2):
            nr, ni = plain[step * s : step * s + BAND], plain[step * s + BAND : step * (s + 1)]
            mr, mi = moved[step * s : step * s + BAND], moved[step * s + BAND : step * (s + 1)]
            real = real + (nr * mr + ni * mi)
            imag = imag + (nr * mi - ni * mr)
        ph[0, t] += real
        ph[1, t] += imag
        low = jnp.dot(
            halves(first_down, step * (TRANS + t)), cols[TRANS + t], preferred_element_type=F32
        )
        nr, ni = plain[2 * step : 2 * step + BAND], plain[2 * step + BAND : 3 * step]
        pp[0, t] += nr * low[:BAND] - ni * low[BAND:]
        pp[1, t] += nr * low[BAND:] + ni * low[:BAND]


def absorb_kernel(count, *refs):
    place = refs[0]
    mine, theirs = refs[1 : 1 + count], refs[1 + count : 1 + 2 * count]
    cols, rows, ph_in, pp_in, ph, pp = refs[1 + 2 * count : 7 + 2 * count]
    hold, first_up, first_down, plain, sems = refs[7 + 2 * count :]
    core = place[0] & 1
    for i in range(count):
        pltpu.make_async_copy(mine[i], hold.at[i, core], sems.at[i, 0]).start()
        pltpu.make_async_copy(theirs[i], hold.at[i, 1 - core], sems.at[i, 1]).start()
    ph[...] = ph_in[...]
    pp[...] = pp_in[...]
    for i in range(count):
        pltpu.make_async_copy(mine[i], hold.at[i, core], sems.at[i, 0]).wait()
        pltpu.make_async_copy(theirs[i], hold.at[i, 1 - core], sems.at[i, 1]).wait()

    def step(i, carry):
        one_walker(hold[i, 0], hold[i, 1], cols, rows, ph, pp, first_up, first_down, plain)
        return carry

    lax.fori_loop(0, count, step, 0)


def absorb(place, mine, theirs, cols, rows, ph, pp, fresh):
    count = len(mine)
    return pl.pallas_call(
        functools.partial(absorb_kernel, count),
        out_shape=(jax.ShapeDtypeStruct(ph.shape, F32), jax.ShapeDtypeStruct(pp.shape, F32)),
        in_specs=[pl.BlockSpec(memory_space=pltpu.SMEM)]
        + [pl.BlockSpec(memory_space=pl.ANY)] * (2 * count)
        + [pl.BlockSpec(memory_space=pltpu.VMEM)] * 4,
        out_specs=(pl.BlockSpec(memory_space=pltpu.VMEM),) * 2,
        scratch_shapes=[
            pltpu.VMEM((count, 2, ORDER, ORDER), BF),
            pltpu.VMEM((2 * BAND * (TRANS + 1), ORDER), BF),
            pltpu.VMEM((2 * BAND * 2 * TRANS, ORDER), BF),
            pltpu.VMEM((6 * BAND, ORDER), F32),
            pltpu.SemaphoreType.DMA((count, 2)),
        ],
        input_output_aliases={} if fresh else {3 + 2 * count: 0, 4 + 2 * count: 1},
        cost_estimate=pl.CostEstimate(
            flops=count * 10**9, bytes_accessed=4 * 10**6, transcendentals=0
        ),
        compiler_params=pltpu.CompilerParams(vmem_limit_bytes=24 * MIB),
        name="absorb",
    )(place, *mine, *theirs, cols, rows, ph, pp)


def along_ring(value, steps):
    return lax.ppermute(value, "blk", [(s, (s + steps) % 64) for s in range(64)])


def along_y(value, steps):
    return lax.ppermute(value, "blk", [(s, s // 4 * 4 + (s + steps) % 4) for s in range(64)])


def other_core(value):
    return lax.ppermute(value, "grp", [(s, s ^ 1) for s in range(4)])


def on_device(masses, spins, shift_table, flip_table, ph_in, pp_in):
    grp = lax.axis_index("grp")
    y = lax.axis_index("blk") % 4
    place = grp.reshape(1).astype(jnp.int32)
    signed = (2 * spins[0] - 1).astype(F32)
    core = grp % 2
    signs = jnp.stack([1 - 2 * core, 2 * core - 1]).astype(F32) * COUPLING

    def scaled(spin, sign):
        matrix = lax.dynamic_index_in_dim(masses[0], spin, 0, keepdims=False)
        return (matrix.astype(F32) * jnp.exp(sign * signed)[None, :]).astype(BF)

    own, own_other = scaled(core, signs[0]), scaled(1 - core, signs[1])
    near = along_ring(own, 4)
    far = along_ring(own, 8)
    cols, rows = tables(place, shift_table, flip_table)
    ph, pp = absorb(place, [own], [own_other], cols, rows, ph_in, pp_in, True)
    aside = [along_y(near, d) for d in (1, 3, 2)]
    wrapped = [along_y(jnp.where(y + d >= 4, far, own), d) for d in (1, 3, 2)]
    early = [near, far] + aside
    early_other = [other_core(v) for v in early]
    late_other = [other_core(v) for v in wrapped]
    ph, pp = absorb(place, early, early_other, cols, rows, ph, pp, False)
    ph, pp = absorb(place, wrapped, late_other, cols, rows, ph, pp, False)
    return ph, pp


def solution(mesh):
    placed = (
        P("blk", None, None, None),
        P("blk", None),
        P("blk", None),
        P("blk", None),
        P(None, "blk", "grp", None),
        P(None, "blk", "grp", None),
    )
    return jax.shard_map(
        on_device,
        mesh=mesh,
        in_specs=placed,
        out_specs=(P(None, "blk", "grp", None), P(None, "blk", "grp", None)),
        check_vma=False,
    )
```

time: 1260 us -> 59.1 us (0.05); the launches traced: 1240 us -> 58.8 us
  other arithmetic: 610 us -> 3.11 us
  local copies, waits for them, and re-layouts: 416 us -> 1.97 us
  loops' own time: 191 us -> 0 us
  Pallas kernels: 0 us -> 22.3 us
  starting transfers between devices: 9.3 us -> 23.9 us
    concatenate x126 -> x0, other arithmetic: 536 us -> none  [cyclic_window(): doubled = jnp.concatenate([grid, grid], axis)]
    dynamic_slice x144 -> x0, local copies, waits for them, and re-layouts: 250 us -> none  [the longest x72 205 us: cyclic_window(): return lax.dynamic_slice_in_dim(doubled, start, length, axis)]
    another operation x9 -> x0, loops' own time: 191 us -> none  [absorb(): ph_step, pp_step = lax.map(one_transfer, (shift_starts, flip_starts))]
    another operation x28 -> x0, local copies, waits for them, and re-layouts: 57.1 us -> none  [the longest x9 42.6 us: absorb(): view = propagator.reshape(2, 2, NW, NK, NW, NK)]
    slice x127 -> x1, local copies, waits for them, and re-layouts: 38.6 us -> 0.59 us  [on_device(): own, own_other = (scaled(core, signs[0]), scaled(1 - core, signs[1]))]
    convert_element_type x90 -> x1, other arithmetic: 37.6 us -> 1.02 us  [scaled(): return (matrix.astype(F32) * jnp.exp(sign * signed)[None, :]).astype(BF)]
    rev x9 -> x0, local copies, waits for them, and re-layouts: 34.6 us -> none  [absorb(): reversed_lower = view[1, :, ::-1, ::-1, ::-1, ::-1]]
    convert_element_type x36 -> x0, local copies, waits for them, and re-layouts: 33.8 us -> none  [one_transfer(): moved_band(view, shift_freq, shift_mom, first_freq, band_freq)]
  transfers between devices with their start and end apart: 8 -> 16, of which waited for: 0 -> 1; matrix products, arithmetic and copies ran while one was open for 60% -> 0% of each run, Pallas kernels for 0% -> 27%
where the time goes in v1:
time: 59.1 us; the launch traced here: 58.8 us
  starting transfers between devices  23.9 us (40%)
  Pallas kernels  22.3 us (38%)
  waiting for transfers between devices  6.67 us (11%)
  other arithmetic  3.11 us (5%)
  local copies, waits for them, and re-layouts  1.97 us (3%)
  between operations  0.93 us (2%)
    pallas_call x3, Pallas kernels, absorb(): pl.pallas_call(functools.partial(absorb_kernel, count), out_shape=(jax.Sh...  18.5 us
    ppermute x8, starting transfers between devices, other_core(): return lax.ppermute(value, 'grp', [(s, s ^ 1) for s in range(4)])  10.6 us
    ppermute x6, starting transfers between devices, along_y(): lax.ppermute(value, 'blk', [(s, s // 4 * 4 + (s + steps) % 4) for s in ra...  7.68 us
    ppermute x2, waiting for transfers between devices, along_ring(): lax.ppermute(value, 'blk', [(s, (s + steps) % 64) for s in range(64)])  6.63 us
    ppermute x2, starting transfers between devices, along_ring(): lax.ppermute(value, 'blk', [(s, (s + steps) % 64) for s in range(64)])  5.53 us
    pallas_call x1, Pallas kernels, tables(): pl.pallas_call(table_kernel, out_shape=(jax.ShapeDtypeStruct((2 * TRANS +...  3.76 us
    exp x1, other arithmetic, scaled(): return (matrix.astype(F32) * jnp.exp(sign * signed)[None, :]).astype(BF)  1.98 us
    unnamed x8, local copies, waits for them, and re-layouts  1.38 us
  transfers between devices with their start and end apart: 16, of which 1 were waited for; matrix products, arithmetic and copies ran while one was open for 0% of the time, Pallas kernels for 27%

profile of v1, /device:TPU:1, one launch (start us, length us, event | category | flops | bytes accessed | tf_op | source)
XLA Modules:
  0.0 58.8 jit_solution(17710387893365355888)
XLA Ops:
  0.7 0.1 fusion.2
  0.7 0.6 fusion.3
  1.3 2.0 %multiply_exponential_fusion = (f32[1,256]{1,0:T(1,128)S(1)}, f32[1,256]{1,0:T(1,128)S(1)}) fusion(f32[]{:T(128)} %bitcast.7, s32[1,256]{1,0:T(1,128)} %param.7, f32[]{:T(128)} %bitcast.4), kind=kLoop, calls=%fused_computation.7 | loop fusion | flops 1280 | bytes 3080 | tf_op jit(solution)/shard_map/exp | solution.py:191
  3.3 1.0 %fusion = (bf16[256,256]{1,0:T(8,128)(2,1)S(1)}, bf16[256,256]{1,0:T(8,128)(2,1)S(1)}) fusion(f32[256]{0:T(256)S(1)} %bitcast.13, bf16[1,2,256,256]{3,2,1,0:T(8,128)(2,1)} %param.6, s32[]{:T(128)S(6)} %select_n.47, f32[256]{0:T(256)S(1)} %bitcast.14, s32[]{:T(128)S(6)} %select_n.41), kind=kLoop, calls=%fused_computation.1 | loop fusion | flops 393216 | bytes 526344 | tf_op jit(solution)/shard_map/convert_element_type | solution.py:191
  4.3 2.5 %collective-permute-start.7 = (bf16[256,256]{1,0:T(8,128)(2,1)S(1)}, bf16[256,256]{1,0:T(8,128)(2,1)S(1)}, u32[]{:S(2)}, u32[]{:S(2)}) collective-permute-start(bf16[256,256]{1,0:T(8,128)(2,1)S(1)} %get-tuple-element.15.refs_1_), channel_id=1, source_target_pairs={{0,4},{1,5},{2,6},{3,7},{4,8},{5,9},{6,10},{7,11},{8,12},{9,13},{1... | collective-permute-start | bytes 393224 | tf_op jit(solution)/shard_map/ppermute | solution.py:170
  6.9 3.0 %collective-permute-start = (bf16[256,256]{1,0:T(8,128)(2,1)S(1)}, bf16[256,256]{1,0:T(8,128)(2,1)S(1)}, u32[]{:S(2)}, u32[]{:S(2)}) collective-permute-start(bf16[256,256]{1,0:T(8,128)(2,1)S(1)} %get-tuple-element.15.refs_1_), channel_id=1, source_target_pairs={{0,8},{1,9},{2,10},{3,11},{4,12},{5,13},{6,14},{7,15},{8,16},{9,17... | collective-permute-start | bytes 393224 | tf_op jit(solution)/shard_map/ppermute | solution.py:170
  9.9 6.6 %collective-permute-done.7.refs_1_ = bf16[256,256]{1,0:T(8,128)(2,1)S(1)} collective-permute-done((bf16[256,256]{1,0:T(8,128)(2,1)S(1)}, bf16[256,256]{1,0:T(8,128)(2,1)S(1)}, u32[]{:S(2)}, u32[]{:S(2)}) %collective-permute-start.7) | collective-permute-done | bytes 131104 | tf_op jit(solution)/shard_map/ppermute | solution.py:170
  16.5 1.3 %collective-permute-start.8 = (bf16[256,256]{1,0:T(8,128)(2,1)S(1)}, bf16[256,256]{1,0:T(8,128)(2,1)S(1)}, u32[]{:S(2)}, u32[]{:S(2)}) collective-permute-start(bf16[256,256]{1,0:T(8,128)(2,1)S(1)} %collective-permute-done.7.refs_1_), channel_id=1, source_target_pairs={{0,1},{1,2},{2,3},{3,0},{4,5},{5,6},{6,7},{7,4},{8,9},{9,10},{10,1... | collective-permute-start | bytes 393224 | tf_op jit(solution)/shard_map/ppermute | solution.py:174
  17.8 1.4 %collective-permute-start.9 = (bf16[256,256]{1,0:T(8,128)(2,1)S(1)}, bf16[256,256]{1,0:T(8,128)(2,1)S(1)}, u32[]{:S(2)}, u32[]{:S(2)}) collective-permute-start(bf16[256,256]{1,0:T(8,128)(2,1)S(1)} %collective-permute-done.7.refs_1_), channel_id=1, source_target_pairs={{0,3},{1,0},{2,1},{3,2},{4,7},{5,4},{6,5},{7,6},{8,11},{9,8},{10,9... | collective-permute-start | bytes 393224 | tf_op jit(solution)/shard_map/ppermute | solution.py:174
  19.2 1.6 %collective-permute-start.10 = (bf16[256,256]{1,0:T(8,128)(2,1)S(1)}, bf16[256,256]{1,0:T(8,128)(2,1)S(1)}, u32[]{:S(2)}, u32[]{:S(2)}) collective-permute-start(bf16[256,256]{1,0:T(8,128)(2,1)S(1)} %collective-permute-done.7.refs_1_), channel_id=1, source_target_pairs={{0,2},{1,3},{2,0},{3,1},{4,6},{5,7},{6,4},{7,5},{8,10},{9,11},{10,... | collective-permute-start | bytes 393224 | tf_op jit(solution)/shard_map/ppermute | solution.py:174
  20.9 3.4 %collective-permute-start.11 = (bf16[256,256]{1,0:T(8,128)(2,1)S(1)}, bf16[256,256]{1,0:T(8,128)(2,1)S(1)}, u32[]{:S(2)}, u32[]{:S(2)}) collective-permute-start(bf16[256,256]{1,0:T(8,128)(2,1)S(1)} %collective-permute-done.7.refs_1_), channel_id=1, source_target_pairs={{0,64},{64,0},{128,192},{192,128},{1,65},{65,1},{129,193},{193,129... | collective-permute-start | bytes 393224 | tf_op jit(solution)/shard_map/ppermute | solution.py:178
  24.2 0.0 collective-permute-done.refs_2_
  24.2 0.0 collective-permute-start.12
  24.3 0.0 collective-permute-done.8.refs_3_
  24.3 0.5 collective-permute-start.1
  24.8 0.0 collective-permute-done.9.refs_4_
  24.8 2.3 %collective-permute-start.2 = (bf16[256,256]{1,0:T(8,128)(2,1)S(1)}, bf16[256,256]{1,0:T(8,128)(2,1)S(1)}, u32[]{:S(2)}, u32[]{:S(2)}) collective-permute-start(bf16[256,256]{1,0:T(8,128)(2,1)S(1)} %get-tuple-element.17), channel_id=1, source_target_pairs={{0,3},{1,0},{2,1},{3,2},{4,7},{5,4},{6,5},{7,6},{8,11},{9,8},{10,9... | collective-permute-start | bytes 393224 | tf_op jit(solution)/shard_map/ppermute | solution.py:174
  27.1 0.0 collective-permute-done.10.refs_5_
  27.1 0.6 collective-permute-start.3
  27.6 0.0 collective-permute-done.11.refs_6_
  27.6 4.3 %collective-permute-start.13 = (bf16[256,256]{1,0:T(8,128)(2,1)S(1)}, bf16[256,256]{1,0:T(8,128)(2,1)S(1)}, u32[]{:S(2)}, u32[]{:S(2)}) collective-permute-start(bf16[256,256]{1,0:T(8,128)(2,1)S(1)} %collective-permute-done.8.refs_3_), channel_id=1, source_target_pairs={{0,64},{64,0},{128,192},{192,128},{1,65},{65,1},{129,193},{193,129... | collective-permute-start | bytes 393224 | tf_op jit(solution)/shard_map/ppermute | solution.py:178
  31.9 0.0 collective-permute-done.12.refs_7_
  31.9 0.1 collective-permute-start.14
  32.0 0.0 collective-permute-done.1.refs_1_
  32.0 2.2 %collective-permute-start.15 = (bf16[256,256]{1,0:T(8,128)(2,1)S(1)}, bf16[256,256]{1,0:T(8,128)(2,1)S(1)}, u32[]{:S(2)}, u32[]{:S(2)}) collective-permute-start(bf16[256,256]{1,0:T(8,128)(2,1)S(1)} %collective-permute-done.10.refs_5_), channel_id=1, source_target_pairs={{0,64},{64,0},{128,192},{192,128},{1,65},{65,1},{129,193},{193,129... | collective-permute-start | bytes 393224 | tf_op jit(solution)/shard_map/ppermute | solution.py:178
  34.2 0.0 copy-start.2
  34.2 0.7 %copy-done.2 = s32[4,256]{1,0:T(4,128)S(1)} copy-done((s32[4,256]{1,0:T(4,128)S(1)}, s32[4,256]{1,0:T(4,128)}, u32[]{:S(2)}) %copy-start.2) | copy-done | bytes 4120
  34.9 0.0 copy-start.3
  34.9 0.7 %copy-done.3 = s32[4,256]{1,0:T(4,128)S(1)} copy-done((s32[4,256]{1,0:T(4,128)S(1)}, s32[4,256]{1,0:T(4,128)}, u32[]{:S(2)}) %copy-start.3) | copy-done | bytes 4120
  35.6 0.0 copy-start
  35.6 0.0 copy-start.1
  35.6 3.8 %tables.1 = (bf16[9,512,256]{2,1,0:T(8,128)(2,1)S(1)}, bf16[1152,256]{1,0:T(8,128)(2,1)S(1)}) custom-call(s32[1]{0:T(128)} %bitcast.place_ref.refs_0_, s32[4,256]{1,0:T(4,128)S(1)} %copy-done.2, s32[4,256]{1,0:T(4,128)S(1)} %copy-done.3), custom_call_target="tpu_custom_call" | custom-call | flops 2000000000 | bytes 3000000 | tf_op jit(solution)/shard_map/tables/pallas_call | solution.py:68
  39.3 0.0 copy-done
  39.3 0.0 copy-done.1
  39.4 2.5 %absorb.3 = (f32[2,4,64,256]{3,2,1,0:T(8,128)}, f32[2,4,64,256]{3,2,1,0:T(8,128)}) custom-call(s32[1]{0:T(128)} %bitcast.place_ref.refs_0_, bf16[256,256]{1,0:T(8,128)(2,1)S(1)} %get-tuple-element.15.refs_1_, bf16[256,256]{1,0:T(8,128)(2,1)S(1)} %get-tuple-element.14.refs_2_, bf16[9,512,256]{2,1,0:T(8,128)(2,1)S(1)} %get-tuple-element.8.refs_3_.refs_11_.refs_7_, ...), custom_call_target="tpu_custom_call" | custom-call | flops 1000000000 | bytes 4000000 | tf_op jit(solution)/shard_map/absorb/pallas_call | solution.py:146
  41.8 0.0 collective-permute-done.2.refs_2_
  41.8 0.1 collective-permute-start.4
  41.9 0.0 collective-permute-done.3.refs_3_
  41.9 0.5 collective-permute-start.5
  42.4 0.0 collective-permute-done.13.refs_8_
  42.4 0.1 collective-permute-start.6
  42.5 0.0 collective-permute-done.14.refs_9_
  42.5 0.0 collective-permute-done.15.refs_10_
  42.5 9.5 %absorb.4 = (f32[2,4,64,256]{3,2,1,0:T(8,128)}, f32[2,4,64,256]{3,2,1,0:T(8,128)}) custom-call(s32[1]{0:T(128)} %bitcast.place_ref.refs_0_, bf16[256,256]{1,0:T(8,128)(2,1)S(1)} %collective-permute-done.7.refs_1_, bf16[256,256]{1,0:T(8,128)(2,1)S(1)} %collective-permute-done.refs_2_, ...), custom_call_target="tpu_custom_call", output_to_operand_aliasing={{0}: (13, {}), {1}: (14, {})} | custom-call | flops 5000000000 | bytes 4000000 | tf_op jit(solution)/shard_map/absorb/pallas_call | solution.py:146
  52.1 0.0 collective-permute-done.4.refs_4_
  52.1 0.0 collective-permute-done.5.refs_5_
  52.1 0.0 collective-permute-done.6.refs_6_
  52.1 6.6 %absorb.5 = (f32[2,4,64,256]{3,2,1,0:T(8,128)}, f32[2,4,64,256]{3,2,1,0:T(8,128)}) custom-call(s32[1]{0:T(128)} %bitcast.place_ref.refs_0_, bf16[256,256]{1,0:T(8,128)(2,1)S(1)} %collective-permute-done.1.refs_1_, bf16[256,256]{1,0:T(8,128)(2,1)S(1)} %collective-permute-done.2.refs_2_, ...), custom_call_target="tpu_custom_call", output_to_operand_aliasing={{0}: (9, {}), {1}: (10, {})} | custom-call | flops 3000000000 | bytes 4000000 | tf_op jit(solution)/shard_map/absorb/pallas_call | solution.py:146
  (1 shorter events, 0.0 us)
Async XLA Ops:
  4.3 12.2 %collective-permute-start.7 = (bf16[256,256]{1,0:T(8,128)(2,1)S(1)}, bf16[256,256]{1,0:T(8,128)(2,1)S(1)}, u32[]{:S(2)}, u32[]{:S(2)}) collective-permute-start(bf16[256,256]{1,0:T(8,128)(2,1)S(1)} %get-tuple-element.15.refs_1_), channel_id=1, source_target_pairs={{0,4},{1,5},{2,6},{3,7},{4,8},{5,9},{6,10},{7,11},{8,12},{9,13},{1... | collective-permute-start | bytes 393224 | tf_op jit(solution)/shard_map/ppermute | solution.py:170
  6.9 17.4 %collective-permute-start = (bf16[256,256]{1,0:T(8,128)(2,1)S(1)}, bf16[256,256]{1,0:T(8,128)(2,1)S(1)}, u32[]{:S(2)}, u32[]{:S(2)}) collective-permute-start(bf16[256,256]{1,0:T(8,128)(2,1)S(1)} %get-tuple-element.15.refs_1_), channel_id=1, source_target_pairs={{0,8},{1,9},{2,10},{3,11},{4,12},{5,13},{6,14},{7,15},{8,16},{9,17... | collective-permute-start | bytes 393224 | tf_op jit(solution)/shard_map/ppermute | solution.py:170
  16.5 7.8 %collective-permute-start.8 = (bf16[256,256]{1,0:T(8,128)(2,1)S(1)}, bf16[256,256]{1,0:T(8,128)(2,1)S(1)}, u32[]{:S(2)}, u32[]{:S(2)}) collective-permute-start(bf16[256,256]{1,0:T(8,128)(2,1)S(1)} %collective-permute-done.7.refs_1_), channel_id=1, source_target_pairs={{0,1},{1,2},{2,3},{3,0},{4,5},{5,6},{6,7},{7,4},{8,9},{9,10},{10,1... | collective-permute-start | bytes 393224 | tf_op jit(solution)/shard_map/ppermute | solution.py:174
  17.8 7.0 %collective-permute-start.9 = (bf16[256,256]{1,0:T(8,128)(2,1)S(1)}, bf16[256,256]{1,0:T(8,128)(2,1)S(1)}, u32[]{:S(2)}, u32[]{:S(2)}) collective-permute-start(bf16[256,256]{1,0:T(8,128)(2,1)S(1)} %collective-permute-done.7.refs_1_), channel_id=1, source_target_pairs={{0,3},{1,0},{2,1},{3,2},{4,7},{5,4},{6,5},{7,6},{8,11},{9,8},{10,9... | collective-permute-start | bytes 393224 | tf_op jit(solution)/shard_map/ppermute | solution.py:174
  19.2 7.8 %collective-permute-start.10 = (bf16[256,256]{1,0:T(8,128)(2,1)S(1)}, bf16[256,256]{1,0:T(8,128)(2,1)S(1)}, u32[]{:S(2)}, u32[]{:S(2)}) collective-permute-start(bf16[256,256]{1,0:T(8,128)(2,1)S(1)} %collective-permute-done.7.refs_1_), channel_id=1, source_target_pairs={{0,2},{1,3},{2,0},{3,1},{4,6},{5,7},{6,4},{7,5},{8,10},{9,11},{10,... | collective-permute-start | bytes 393224 | tf_op jit(solution)/shard_map/ppermute | solution.py:174
  20.9 6.7 %collective-permute-start.11 = (bf16[256,256]{1,0:T(8,128)(2,1)S(1)}, bf16[256,256]{1,0:T(8,128)(2,1)S(1)}, u32[]{:S(2)}, u32[]{:S(2)}) collective-permute-start(bf16[256,256]{1,0:T(8,128)(2,1)S(1)} %collective-permute-done.7.refs_1_), channel_id=1, source_target_pairs={{0,64},{64,0},{128,192},{192,128},{1,65},{65,1},{129,193},{193,129... | collective-permute-start | bytes 393224 | tf_op jit(solution)/shard_map/ppermute | solution.py:178
  24.2 7.6 %collective-permute-start.12 = (bf16[256,256]{1,0:T(8,128)(2,1)S(1)}, bf16[256,256]{1,0:T(8,128)(2,1)S(1)}, u32[]{:S(2)}, u32[]{:S(2)}) collective-permute-start(bf16[256,256]{1,0:T(8,128)(2,1)S(1)} %collective-permute-done.refs_2_), channel_id=1, source_target_pairs={{0,64},{64,0},{128,192},{192,128},{1,65},{65,1},{129,193},{193,129... | collective-permute-start | bytes 393224 | tf_op jit(solution)/shard_map/ppermute | solution.py:178
  24.3 7.7 %collective-permute-start.1 = (bf16[256,256]{1,0:T(8,128)(2,1)S(1)}, bf16[256,256]{1,0:T(8,128)(2,1)S(1)}, u32[]{:S(2)}, u32[]{:S(2)}) collective-permute-start(bf16[256,256]{1,0:T(8,128)(2,1)S(1)} %get-tuple-element.18), channel_id=1, source_target_pairs={{0,1},{1,2},{2,3},{3,0},{4,5},{5,6},{6,7},{7,4},{8,9},{9,10},{10,1... | collective-permute-start | bytes 393224 | tf_op jit(solution)/shard_map/ppermute | solution.py:174
  24.8 17.0 %collective-permute-start.2 = (bf16[256,256]{1,0:T(8,128)(2,1)S(1)}, bf16[256,256]{1,0:T(8,128)(2,1)S(1)}, u32[]{:S(2)}, u32[]{:S(2)}) collective-permute-start(bf16[256,256]{1,0:T(8,128)(2,1)S(1)} %get-tuple-element.17), channel_id=1, source_target_pairs={{0,3},{1,0},{2,1},{3,2},{4,7},{5,4},{6,5},{7,6},{8,11},{9,8},{10,9... | collective-permute-start | bytes 393224 | tf_op jit(solution)/shard_map/ppermute | solution.py:174
  27.1 14.9 %collective-permute-start.3 = (bf16[256,256]{1,0:T(8,128)(2,1)S(1)}, bf16[256,256]{1,0:T(8,128)(2,1)S(1)}, u32[]{:S(2)}, u32[]{:S(2)}) collective-permute-start(bf16[256,256]{1,0:T(8,128)(2,1)S(1)} %get-tuple-element.16), channel_id=1, source_target_pairs={{0,2},{1,3},{2,0},{3,1},{4,6},{5,7},{6,4},{7,5},{8,10},{9,11},{10,... | collective-permute-start | bytes 393224 | tf_op jit(solution)/shard_map/ppermute | solution.py:174
  27.6 14.8 %collective-permute-start.13 = (bf16[256,256]{1,0:T(8,128)(2,1)S(1)}, bf16[256,256]{1,0:T(8,128)(2,1)S(1)}, u32[]{:S(2)}, u32[]{:S(2)}) collective-permute-start(bf16[256,256]{1,0:T(8,128)(2,1)S(1)} %collective-permute-done.8.refs_3_), channel_id=1, source_target_pairs={{0,64},{64,0},{128,192},{192,128},{1,65},{65,1},{129,193},{193,129... | collective-permute-start | bytes 393224 | tf_op jit(solution)/shard_map/ppermute | solution.py:178
  31.9 10.7 %collective-permute-start.14 = (bf16[256,256]{1,0:T(8,128)(2,1)S(1)}, bf16[256,256]{1,0:T(8,128)(2,1)S(1)}, u32[]{:S(2)}, u32[]{:S(2)}) collective-permute-start(bf16[256,256]{1,0:T(8,128)(2,1)S(1)} %collective-permute-done.9.refs_4_), channel_id=1, source_target_pairs={{0,64},{64,0},{128,192},{192,128},{1,65},{65,1},{129,193},{193,129... | collective-permute-start | bytes 393224 | tf_op jit(solution)/shard_map/ppermute | solution.py:178
  32.0 10.6 %collective-permute-start.15 = (bf16[256,256]{1,0:T(8,128)(2,1)S(1)}, bf16[256,256]{1,0:T(8,128)(2,1)S(1)}, u32[]{:S(2)}, u32[]{:S(2)}) collective-permute-start(bf16[256,256]{1,0:T(8,128)(2,1)S(1)} %collective-permute-done.10.refs_5_), channel_id=1, source_target_pairs={{0,64},{64,0},{128,192},{192,128},{1,65},{65,1},{129,193},{193,129... | collective-permute-start | bytes 393224 | tf_op jit(solution)/shard_map/ppermute | solution.py:178
  34.2 0.7 %copy-start.2 = (s32[4,256]{1,0:T(4,128)S(1)}, s32[4,256]{1,0:T(4,128)}, u32[]{:S(2)}) copy-start(s32[4,256]{1,0:T(4,128)} %shift_ref.1) | copy-start | bytes 12292
  34.9 0.7 %copy-start.3 = (s32[4,256]{1,0:T(4,128)S(1)}, s32[4,256]{1,0:T(4,128)}, u32[]{:S(2)}) copy-start(s32[4,256]{1,0:T(4,128)} %flip_ref.1) | copy-start | bytes 12292
  35.6 3.8 %copy-start = (f32[2,4,64,256]{3,2,1,0:T(8,128)S(1)}, f32[2,4,64,256]{3,2,1,0:T(8,128)}, u32[]{:S(2)}) copy-start(f32[2,4,64,256]{3,2,1,0:T(8,128)} %refs_5_.1) | copy-start | bytes 1572868
  35.6 3.8 %copy-start.1 = (f32[2,4,64,256]{3,2,1,0:T(8,128)S(1)}, f32[2,4,64,256]{3,2,1,0:T(8,128)}, u32[]{:S(2)}) copy-start(f32[2,4,64,256]{3,2,1,0:T(8,128)} %refs_6_.1) | copy-start | bytes 1572868
  41.8 10.2 %collective-permute-start.4 = (bf16[256,256]{1,0:T(8,128)(2,1)S(1)}, bf16[256,256]{1,0:T(8,128)(2,1)S(1)}, u32[]{:S(2)}, u32[]{:S(2)}) collective-permute-start(bf16[256,256]{1,0:T(8,128)(2,1)S(1)} %collective-permute-done.1.refs_1_), channel_id=1, source_target_pairs={{0,64},{64,0},{128,192},{192,128},{1,65},{65,1},{129,193},{193,129... | collective-permute-start | bytes 393224 | tf_op jit(solution)/shard_map/ppermute | solution.py:178
  41.9 10.1 %collective-permute-start.5 = (bf16[256,256]{1,0:T(8,128)(2,1)S(1)}, bf16[256,256]{1,0:T(8,128)(2,1)S(1)}, u32[]{:S(2)}, u32[]{:S(2)}) collective-permute-start(bf16[256,256]{1,0:T(8,128)(2,1)S(1)} %collective-permute-done.2.refs_2_), channel_id=1, source_target_pairs={{0,64},{64,0},{128,192},{192,128},{1,65},{65,1},{129,193},{193,129... | collective-permute-start | bytes 393224 | tf_op jit(solution)/shard_map/ppermute | solution.py:178
  42.4 9.6 %collective-permute-start.6 = (bf16[256,256]{1,0:T(8,128)(2,1)S(1)}, bf16[256,256]{1,0:T(8,128)(2,1)S(1)}, u32[]{:S(2)}, u32[]{:S(2)}) collective-permute-start(bf16[256,256]{1,0:T(8,128)(2,1)S(1)} %collective-permute-done.3.refs_3_), channel_id=1, source_target_pairs={{0,64},{64,0},{128,192},{192,128},{1,65},{65,1},{129,193},{193,129... | collective-permute-start | bytes 393224 | tf_op jit(solution)/shard_map/ppermute | solution.py:178

commit v2 on v1

--- a/solution.py
+++ b/solution.py
@@ -1,4 +1,3 @@
-import functools
 import math
 
 import jax
@@ -16,6 +15,7 @@
 BF = jnp.bfloat16
 F32 = jnp.float32
 MIB = 1 << 20
+TINY = pl.CostEstimate(flops=1, bytes_accessed=1, transcendentals=0)
 
 
 def wave(freq, mom, tau, site):
@@ -73,7 +73,7 @@
         ),
         in_specs=[pl.BlockSpec(memory_space=pltpu.SMEM)] * 3,
         out_specs=(pl.BlockSpec(memory_space=pltpu.VMEM),) * 2,
-        cost_estimate=pl.CostEstimate(flops=2 * 10**9, bytes_accessed=3 * 10**6, transcendentals=0),
+        cost_estimate=TINY,
         compiler_params=pltpu.CompilerParams(vmem_limit_bytes=20 * MIB),
         name="tables",
     )(place, shift, flip)
@@ -119,89 +119,112 @@
         pp[1, t] += nr * low[BAND:] + ni * low[:BAND]
 
 
-def absorb_kernel(count, *refs):
-    place = refs[0]
-    mine, theirs = refs[1 : 1 + count], refs[1 + count : 1 + 2 * count]
-    cols, rows, ph_in, pp_in, ph, pp = refs[1 + 2 * count : 7 + 2 * count]
-    hold, first_up, first_down, plain, sems = refs[7 + 2 * count :]
-    core = place[0] & 1
-    for i in range(count):
-        pltpu.make_async_copy(mine[i], hold.at[i, core], sems.at[i, 0]).start()
-        pltpu.make_async_copy(theirs[i], hold.at[i, 1 - core], sems.at[i, 1]).start()
+def absorb_kernel(pieces, cols, rows, ph_in, pp_in, ph, pp, first_up, first_down, plain):
     ph[...] = ph_in[...]
     pp[...] = pp_in[...]
-    for i in range(count):
-        pltpu.make_async_copy(mine[i], hold.at[i, core], sems.at[i, 0]).wait()
-        pltpu.make_async_copy(theirs[i], hold.at[i, 1 - core], sems.at[i, 1]).wait()
-
-    def step(i, carry):
-        one_walker(hold[i, 0], hold[i, 1], cols, rows, ph, pp, first_up, first_down, plain)
-        return carry
-
-    lax.fori_loop(0, count, step, 0)
-
-
-def absorb(place, mine, theirs, cols, rows, ph, pp, fresh):
-    count = len(mine)
-    return pl.pallas_call(
-        functools.partial(absorb_kernel, count),
+    for i in range(pieces.shape[0]):
+        one_walker(pieces[i, 0], pieces[i, 1], cols, rows, ph, pp, first_up, first_down, plain)
+
+
+def absorb(pieces, cols, rows, ph, pp, fresh):
+    return pl.pallas_call(
+        absorb_kernel,
         out_shape=(jax.ShapeDtypeStruct(ph.shape, F32), jax.ShapeDtypeStruct(pp.shape, F32)),
-        in_specs=[pl.BlockSpec(memory_space=pltpu.SMEM)]
-        + [pl.BlockSpec(memory_space=pl.ANY)] * (2 * count)
-        + [pl.BlockSpec(memory_space=pltpu.VMEM)] * 4,
+        in_specs=[pl.BlockSpec(memory_space=pltpu.VMEM)] * 5,
         out_specs=(pl.BlockSpec(memory_space=pltpu.VMEM),) * 2,
         scratch_shapes=[
-            pltpu.VMEM((count, 2, ORDER, ORDER), BF),
             pltpu.VMEM((2 * BAND * (TRANS + 1), ORDER), BF),
             pltpu.VMEM((2 * BAND * 2 * TRANS, ORDER), BF),
             pltpu.VMEM((6 * BAND, ORDER), F32),
-            pltpu.SemaphoreType.DMA((count, 2)),
         ],
-        input_output_aliases={} if fresh else {3 + 2 * count: 0, 4 + 2 * count: 1},
-        cost_estimate=pl.CostEstimate(
-            flops=count * 10**9, bytes_accessed=4 * 10**6, transcendentals=0
-        ),
+        input_output_aliases={} if fresh else {3: 0, 4: 1},
+        cost_estimate=TINY,
         compiler_params=pltpu.CompilerParams(vmem_limit_bytes=24 * MIB),
         name="absorb",
-    )(place, *mine, *theirs, cols, rows, ph, pp)
-
-
-def along_ring(value, steps):
-    return lax.ppermute(value, "blk", [(s, (s + steps) % 64) for s in range(64)])
+    )(pieces, cols, rows, ph, pp)
+
+
+def scale_kernel(masses, spins, out):
+    signed = (2 * spins[...] - 1).astype(F32)
+    for spin, sign in enumerate((COUPLING, -COUPLING)):
+        factor = jnp.exp(sign * signed)
+        out[spin] = (masses[0, spin].astype(F32) * factor).astype(BF)
+
+
+def scale(masses, spins):
+    return pl.pallas_call(
+        scale_kernel,
+        out_shape=jax.ShapeDtypeStruct((2, ORDER, ORDER), BF),
+        in_specs=[pl.BlockSpec(memory_space=pltpu.VMEM)] * 2,
+        out_specs=pl.BlockSpec(memory_space=pltpu.VMEM),
+        cost_estimate=TINY,
+        name="scale",
+    )(masses, spins)
+
+
+def route_kernel(place, y_ref, own, got, token, *outs):
+    core = place[0] & 1
+    for step, out in zip(Y_STEPS, outs):
+        keep = (core == 0) | (y_ref[0] + step >= 4)
+
+        @pl.when(keep)
+        def _():
+            out[...] = got[...]
+
+        @pl.when(jnp.logical_not(keep))
+        def _():
+            out[...] = own[...]
+
+
+def route(place, y, own, got, token):
+    return pl.pallas_call(
+        route_kernel,
+        out_shape=(jax.ShapeDtypeStruct(own.shape, BF),) * 3,
+        in_specs=[pl.BlockSpec(memory_space=pltpu.SMEM)] * 2
+        + [pl.BlockSpec(memory_space=pltpu.VMEM)] * 2
+        + [pl.BlockSpec(memory_space=pl.ANY)],
+        out_specs=(pl.BlockSpec(memory_space=pltpu.VMEM),) * 3,
+        cost_estimate=TINY,
+        name="route",
+    )(place, y, own, got, token)
+
+
+Y_STEPS = (2, 1, 3)
+PLANE = 4
+BLOCKS = 64
+
+
+def planes_back(value):
+    pairs = [
+        (g * BLOCKS + b, g * BLOCKS + (b + PLANE * (1 + g % 2)) % BLOCKS)
+        for g in range(4)
+        for b in range(BLOCKS)
+    ]
+    return lax.ppermute(value, ("grp", "blk"), pairs)
 
 
 def along_y(value, steps):
-    return lax.ppermute(value, "blk", [(s, s // 4 * 4 + (s + steps) % 4) for s in range(64)])
-
-
-def other_core(value):
-    return lax.ppermute(value, "grp", [(s, s ^ 1) for s in range(4)])
+    return lax.ppermute(value, "blk", [(s, s // 4 * 4 + (s + steps) % 4) for s in range(BLOCKS)])
+
+
+def both_cores(value):
+    return lax.all_gather(value, "grp", axis=0, axis_index_groups=[[0, 1], [2, 3]])
 
 
 def on_device(masses, spins, shift_table, flip_table, ph_in, pp_in):
-    grp = lax.axis_index("grp")
-    y = lax.axis_index("blk") % 4
-    place = grp.reshape(1).astype(jnp.int32)
-    signed = (2 * spins[0] - 1).astype(F32)
-    core = grp % 2
-    signs = jnp.stack([1 - 2 * core, 2 * core - 1]).astype(F32) * COUPLING
-
-    def scaled(spin, sign):
-        matrix = lax.dynamic_index_in_dim(masses[0], spin, 0, keepdims=False)
-        return (matrix.astype(F32) * jnp.exp(sign * signed)[None, :]).astype(BF)
-
-    own, own_other = scaled(core, signs[0]), scaled(1 - core, signs[1])
-    near = along_ring(own, 4)
-    far = along_ring(own, 8)
+    place = lax.axis_index("grp").reshape(1).astype(jnp.int32)
+    y = (lax.axis_index("blk") % PLANE).reshape(1).astype(jnp.int32)
+    own = scale(masses, spins)
+    got = planes_back(own)
     cols, rows = tables(place, shift_table, flip_table)
-    ph, pp = absorb(place, [own], [own_other], cols, rows, ph_in, pp_in, True)
-    aside = [along_y(near, d) for d in (1, 3, 2)]
-    wrapped = [along_y(jnp.where(y + d >= 4, far, own), d) for d in (1, 3, 2)]
-    early = [near, far] + aside
-    early_other = [other_core(v) for v in early]
-    late_other = [other_core(v) for v in wrapped]
-    ph, pp = absorb(place, early, early_other, cols, rows, ph, pp, False)
-    ph, pp = absorb(place, wrapped, late_other, cols, rows, ph, pp, False)
+    ph, pp = absorb(own[None], cols, rows, ph_in, pp_in, True)
+    got, ph, pp = lax.optimization_barrier((got, ph, pp))
+    sent = route(place, y, own, got, ph)
+    across = [along_y(v, d) for v, d in zip(sent, Y_STEPS)]
+    ph, pp = absorb(both_cores(got), cols, rows, ph, pp, False)
+    for piece in across:
+        piece, ph, pp = lax.optimization_barrier((piece, ph, pp))
+        ph, pp = absorb(both_cores(piece), cols, rows, ph, pp, False)
     return ph, pp
 
 

time: 59.1 us -> 55 us (0.931)
  starting transfers between devices: 23.9 us -> 8.2 us
  blocking collectives: 0 us -> 13 us
  waiting for transfers between devices: 6.67 us -> 1.72 us
  Pallas kernels: 22.3 us -> 25.8 us
  local copies, waits for them, and re-layouts: 1.97 us -> 5.1 us
  other arithmetic: 3.11 us -> 0 us
    all_gather x0 -> x4, blocking collectives: none -> 13 us  [both_cores(): lax.all_gather(value, 'grp', axis=0, axis_index_groups=[[0, 1], [2, 3]])]
    ppermute x10 -> x1, starting transfers between devices: 16.2 us -> 3.82 us  [planes_back(): return lax.ppermute(value, ('grp', 'blk'), pairs)]
    ppermute x10 -> x1, waiting for transfers between devices: 6.65 us -> 1.71 us  [planes_back(): return lax.ppermute(value, ('grp', 'blk'), pairs)]
    unnamed x8 -> x12, local copies, waits for them, and re-layouts: 1.38 us -> 5.1 us
    pallas_call x3 -> x7, Pallas kernels: 18.5 us -> 22.1 us  [the longest x5 18.4 us: absorb(): pl.pallas_call(absorb_kernel, out_shape=(jax.ShapeDtypeStruct(ph.shape, F...]
    ppermute x6 -> x3, starting transfers between devices: 7.68 us -> 4.38 us  [along_y(): lax.ppermute(value, 'blk', [(s, s // 4 * 4 + (s + steps) % 4) for s in ra...]
    exp x1 -> x0, other arithmetic: 1.98 us -> none  [scaled(): return (matrix.astype(F32) * jnp.exp(sign * signed)[None, :]).astype(BF)]
    convert_element_type x1 -> x0, other arithmetic: 1.02 us -> none  [scaled(): return (matrix.astype(F32) * jnp.exp(sign * signed)[None, :]).astype(BF)]
  transfers between devices with their start and end apart: 16 -> 4, of which waited for: 1 -> 1; matrix products, arithmetic and copies ran while one was open for 0% -> 0% of each run, Pallas kernels for 27% -> 33%
where the time goes in v2:
time: 55 us; the launch traced here: 54.5 us
  Pallas kernels  25.8 us (47%)
  blocking collectives  13 us (24%)
  starting transfers between devices  8.2 us (15%)
  local copies, waits for them, and re-layouts  5.1 us (9%)
  waiting for transfers between devices  1.72 us (3%)
  between operations  0.66 us (1%)
    pallas_call x5, Pallas kernels, absorb(): pl.pallas_call(absorb_kernel, out_shape=(jax.ShapeDtypeStruct(ph.shape, F...  18.4 us
    all_gather x4, blocking collectives, both_cores(): lax.all_gather(value, 'grp', axis=0, axis_index_groups=[[0, 1], [2, 3]])  13 us
    unnamed x12, local copies, waits for them, and re-layouts  5.1 us
    ppermute x3, starting transfers between devices, along_y(): lax.ppermute(value, 'blk', [(s, s // 4 * 4 + (s + steps) % 4) for s in ra...  4.38 us
    ppermute x1, starting transfers between devices, planes_back(): return lax.ppermute(value, ('grp', 'blk'), pairs)  3.82 us
    pallas_call x1, Pallas kernels, tables(): pl.pallas_call(table_kernel, out_shape=(jax.ShapeDtypeStruct((2 * TRANS +...  3.75 us
    pallas_call x1, Pallas kernels, route(): pl.pallas_call(route_kernel, out_shape=(jax.ShapeDtypeStruct(own.shape, B...  2 us
    ppermute x1, waiting for transfers between devices, planes_back(): return lax.ppermute(value, ('grp', 'blk'), pairs)  1.71 us
  transfers between devices with their start and end apart: 4, of which 1 were waited for; matrix products, arithmetic and copies ran while one was open for 0% of the time, Pallas kernels for 33%

profile of v2, /device:TPU:1, one launch (start us, length us, event | category | flops | bytes accessed | tf_op | source)
XLA Modules:
  0.0 54.5 jit_solution(10582879546783869299)
XLA Ops:
  0.6 1.7 %scale.1.own = bf16[2,256,256]{2,1,0:T(8,128)(2,1)} custom-call(bf16[1,2,256,256]{3,2,1,0:T(8,128)(2,1)} %masses.1, s32[1,256]{1,0:T(1,128)} %spins.1), custom_call_target="tpu_custom_call" | custom-call | flops 1 | bytes 1 | tf_op jit(solution)/shard_map/scale/pallas_call | solution.py:155
  2.3 3.8 %collective-permute-start = (bf16[2,256,256]{2,1,0:T(8,128)(2,1)}, bf16[2,256,256]{2,1,0:T(8,128)(2,1)S(1)}, u32[]{:S(2)}, u32[]{:S(2)}) collective-permute-start(bf16[2,256,256]{2,1,0:T(8,128)(2,1)} %scale.1.own), channel_id=1, source_target_pairs={{0,4},{1,5},{2,6},{3,7},{4,8},{5,9},{6,10},{7,11},{8,12},{9,13},{1... | collective-permute-start | bytes 786440 | tf_op jit(solution)/shard_map/ppermute | solution.py:203
  6.2 0.0 copy-start.3
  6.2 0.7 %copy-done.3 = s32[4,256]{1,0:T(4,128)S(1)} copy-done((s32[4,256]{1,0:T(4,128)S(1)}, s32[4,256]{1,0:T(4,128)}, u32[]{:S(2)}) %copy-start.3) | copy-done | bytes 4120
  6.8 0.0 copy-start.4
  6.8 0.7 %copy-done.4 = s32[4,256]{1,0:T(4,128)S(1)} copy-done((s32[4,256]{1,0:T(4,128)S(1)}, s32[4,256]{1,0:T(4,128)}, u32[]{:S(2)}) %copy-start.4) | copy-done | bytes 4120
  7.5 3.7 %tables.1 = (bf16[9,512,256]{2,1,0:T(8,128)(2,1)S(1)}, bf16[1152,256]{1,0:T(8,128)(2,1)S(1)}) custom-call(s32[1]{0:T(128)} %bitcast.place_ref.place, s32[4,256]{1,0:T(4,128)S(1)} %copy-done.3, s32[4,256]{1,0:T(4,128)S(1)} %copy-done.4), custom_call_target="tpu_custom_call" | custom-call | flops 1 | bytes 1 | tf_op jit(solution)/shard_map/tables/pallas_call | solution.py:68
  11.3 0.0 copy-start
  11.3 0.9 %copy-done = bf16[2,256,256]{2,1,0:T(8,128)(2,1)S(1)} copy-done((bf16[2,256,256]{2,1,0:T(8,128)(2,1)S(1)}, bf16[2,256,256]{2,1,0:T(8,128)(2,1)}, u32[]{:S(2)}) %copy-start) | copy-done | bytes 262168
  12.2 0.0 copy-start.1
  12.2 1.0 %copy-done.1 = f32[2,4,64,256]{3,2,1,0:T(8,128)S(1)} copy-done((f32[2,4,64,256]{3,2,1,0:T(8,128)S(1)}, f32[2,4,64,256]{3,2,1,0:T(8,128)}, u32[]{:S(2)}) %copy-start.1) | copy-done | bytes 524312
  13.3 0.0 copy-start.2
  13.3 1.0 %copy-done.2 = f32[2,4,64,256]{3,2,1,0:T(8,128)S(1)} copy-done((f32[2,4,64,256]{3,2,1,0:T(8,128)S(1)}, f32[2,4,64,256]{3,2,1,0:T(8,128)}, u32[]{:S(2)}) %copy-start.2) | copy-done | bytes 524312
  14.3 2.0 %absorb.5 = (f32[2,4,64,256]{3,2,1,0:T(8,128)}, f32[2,4,64,256]{3,2,1,0:T(8,128)}) custom-call(bf16[1,2,256,256]{3,2,1,0:T(8,128)(2,1)S(1)} %bitcast.7, bf16[9,512,256]{2,1,0:T(8,128)(2,1)S(1)} %get-tuple-element.27.cols, bf16[1152,256]{1,0:T(8,128)(2,1)S(1)} %get-tuple-element.28.rows, f32[2,4,64,256]{3,2,1,0:T(8,128)S(1)} %copy-done.1, ...), custom_call_target="tpu_custom_call" | custom-call | flops 1 | bytes 1 | tf_op jit(solution)/shard_map/absorb/pallas_call | solution.py:130
  16.3 1.7 %collective-permute-done.got = bf16[2,256,256]{2,1,0:T(8,128)(2,1)S(1)} collective-permute-done((bf16[2,256,256]{2,1,0:T(8,128)(2,1)}, bf16[2,256,256]{2,1,0:T(8,128)(2,1)S(1)}, u32[]{:S(2)}, u32[]{:S(2)}) %collective-permute-start) | collective-permute-done | bytes 262176 | tf_op jit(solution)/shard_map/ppermute | solution.py:203
  18.0 0.0 copy-start.5
  18.0 0.7 %copy-done.5 = bf16[2,256,256]{2,1,0:T(8,128)(2,1)} copy-done((bf16[2,256,256]{2,1,0:T(8,128)(2,1)}, bf16[2,256,256]{2,1,0:T(8,128)(2,1)S(1)}, u32[]{:S(2)}) %copy-start.5) | copy-done | bytes 262168
  18.7 2.0 %route.1 = (bf16[2,256,256]{2,1,0:T(8,128)(2,1)}, bf16[2,256,256]{2,1,0:T(8,128)(2,1)}, bf16[2,256,256]{2,1,0:T(8,128)(2,1)}) custom-call(s32[1]{0:T(128)} %bitcast.place_ref.place, s32[1]{0:T(128)} %bitcast.1.y_ref, bf16[2,256,256]{2,1,0:T(8,128)(2,1)} %scale.1.own, bf16[2,256,256]{2,1,0:T(8,128)(2,1)} %copy-done.5, ...), custom_call_target="tpu_custom_call" | custom-call | flops 1 | bytes 1 | tf_op jit(solution)/shard_map/route/pallas_call | solution.py:180
  20.7 2.9 %collective-permute-start.3 = (bf16[2,256,256]{2,1,0:T(8,128)(2,1)}, bf16[2,256,256]{2,1,0:T(8,128)(2,1)S(1)}, u32[]{:S(2)}, u32[]{:S(2)}) collective-permute-start(bf16[2,256,256]{2,1,0:T(8,128)(2,1)} %get-tuple-element.35), channel_id=1, source_target_pairs={{0,2},{1,3},{2,0},{3,1},{4,6},{5,7},{6,4},{7,5},{8,10},{9,11},{10,... | collective-permute-start | bytes 786440 | tf_op jit(solution)/shard_map/ppermute | solution.py:207
  23.6 0.8 %collective-permute-start.1 = (bf16[2,256,256]{2,1,0:T(8,128)(2,1)}, bf16[2,256,256]{2,1,0:T(8,128)(2,1)S(1)}, u32[]{:S(2)}, u32[]{:S(2)}) collective-permute-start(bf16[2,256,256]{2,1,0:T(8,128)(2,1)} %get-tuple-element.33), channel_id=1, source_target_pairs={{0,3},{1,0},{2,1},{3,2},{4,7},{5,4},{6,5},{7,6},{8,11},{9,8},{10,9... | collective-permute-start | bytes 786440 | tf_op jit(solution)/shard_map/ppermute | solution.py:207
  24.4 0.7 %collective-permute-start.2 = (bf16[2,256,256]{2,1,0:T(8,128)(2,1)}, bf16[2,256,256]{2,1,0:T(8,128)(2,1)S(1)}, u32[]{:S(2)}, u32[]{:S(2)}) collective-permute-start(bf16[2,256,256]{2,1,0:T(8,128)(2,1)} %get-tuple-element.34), channel_id=1, source_target_pairs={{0,1},{1,2},{2,3},{3,0},{4,5},{5,6},{6,7},{7,4},{8,9},{9,10},{10,1... | collective-permute-start | bytes 786440 | tf_op jit(solution)/shard_map/ppermute | solution.py:207
  25.1 6.3 %all-gather = bf16[4,256,256]{2,1,0:T(8,128)(2,1)S(1)} all-gather(bf16[2,256,256]{2,1,0:T(8,128)(2,1)} %copy-done.5), channel_id=2, replica_groups={{0,64},{128,192},{1,65},{129,193},{2,66},{130,194},{3,67},{131,195},{4,..., dimensions={0}, use_global_device_ids=true | all-gather | bytes 786432 | tf_op jit(solution)/shard_map/all_gather | solution.py:211
  31.4 4.1 %absorb.6 = (f32[2,4,64,256]{3,2,1,0:T(8,128)}, f32[2,4,64,256]{3,2,1,0:T(8,128)}) custom-call(bf16[2,2,256,256]{3,2,1,0:T(8,128)(2,1)S(1)} %bitcast.9, bf16[9,512,256]{2,1,0:T(8,128)(2,1)S(1)} %get-tuple-element.27.cols, bf16[1152,256]{1,0:T(8,128)(2,1)S(1)} %get-tuple-element.28.rows, ...), custom_call_target="tpu_custom_call", output_to_operand_aliasing={{0}: (3, {}), {1}: (4, {})} | custom-call | flops 1 | bytes 1 | tf_op jit(solution)/shard_map/absorb/pallas_call | solution.py:130
  35.5 0.0 collective-permute-done.3
  35.5 2.2 %all-gather.1 = bf16[4,256,256]{2,1,0:T(8,128)(2,1)S(1)} all-gather(bf16[2,256,256]{2,1,0:T(8,128)(2,1)S(1)} %collective-permute-done.3), channel_id=3, replica_groups={{0,64},{128,192},{1,65},{129,193},{2,66},{130,194},{3,67},{131,195},{4,..., dimensions={0}, use_global_device_ids=true | all-gather | bytes 786432 | tf_op jit(solution)/shard_map/all_gather | solution.py:211
  37.7 4.1 %absorb.7 = (f32[2,4,64,256]{3,2,1,0:T(8,128)}, f32[2,4,64,256]{3,2,1,0:T(8,128)}) custom-call(bf16[2,2,256,256]{3,2,1,0:T(8,128)(2,1)S(1)} %bitcast.10, bf16[9,512,256]{2,1,0:T(8,128)(2,1)S(1)} %get-tuple-element.27.cols, bf16[1152,256]{1,0:T(8,128)(2,1)S(1)} %get-tuple-element.28.rows, ...), custom_call_target="tpu_custom_call", output_to_operand_aliasing={{0}: (3, {}), {1}: (4, {})} | custom-call | flops 1 | bytes 1 | tf_op jit(solution)/shard_map/absorb/pallas_call | solution.py:130
  41.8 0.0 collective-permute-done.2
  41.8 2.4 %all-gather.2 = bf16[4,256,256]{2,1,0:T(8,128)(2,1)S(1)} all-gather(bf16[2,256,256]{2,1,0:T(8,128)(2,1)S(1)} %collective-permute-done.2), channel_id=4, replica_groups={{0,64},{128,192},{1,65},{129,193},{2,66},{130,194},{3,67},{131,195},{4,..., dimensions={0}, use_global_device_ids=true | all-gather | bytes 786432 | tf_op jit(solution)/shard_map/all_gather | solution.py:211
  44.1 4.1 %absorb.8 = (f32[2,4,64,256]{3,2,1,0:T(8,128)}, f32[2,4,64,256]{3,2,1,0:T(8,128)}) custom-call(bf16[2,2,256,256]{3,2,1,0:T(8,128)(2,1)S(1)} %bitcast.11, bf16[9,512,256]{2,1,0:T(8,128)(2,1)S(1)} %get-tuple-element.27.cols, bf16[1152,256]{1,0:T(8,128)(2,1)S(1)} %get-tuple-element.28.rows, ...), custom_call_target="tpu_custom_call", output_to_operand_aliasing={{0}: (3, {}), {1}: (4, {})} | custom-call | flops 1 | bytes 1 | tf_op jit(solution)/shard_map/absorb/pallas_call | solution.py:130
  48.3 0.0 collective-permute-done.1
  48.3 2.2 %all-gather.3 = bf16[4,256,256]{2,1,0:T(8,128)(2,1)S(1)} all-gather(bf16[2,256,256]{2,1,0:T(8,128)(2,1)S(1)} %collective-permute-done.1), channel_id=5, replica_groups={{0,64},{128,192},{1,65},{129,193},{2,66},{130,194},{3,67},{131,195},{4,..., dimensions={0}, use_global_device_ids=true | all-gather | bytes 786432 | tf_op jit(solution)/shard_map/all_gather | solution.py:211
  50.4 4.1 %absorb.9 = (f32[2,4,64,256]{3,2,1,0:T(8,128)}, f32[2,4,64,256]{3,2,1,0:T(8,128)}) custom-call(bf16[2,2,256,256]{3,2,1,0:T(8,128)(2,1)S(1)} %bitcast.8, bf16[9,512,256]{2,1,0:T(8,128)(2,1)S(1)} %get-tuple-element.27.cols, bf16[1152,256]{1,0:T(8,128)(2,1)S(1)} %get-tuple-element.28.rows, ...), custom_call_target="tpu_custom_call", output_to_operand_aliasing={{0}: (3, {}), {1}: (4, {})} | custom-call | flops 1 | bytes 1 | tf_op jit(solution)/shard_map/absorb/pallas_call | solution.py:130
Async XLA Ops:
  2.3 15.7 %collective-permute-start = (bf16[2,256,256]{2,1,0:T(8,128)(2,1)}, bf16[2,256,256]{2,1,0:T(8,128)(2,1)S(1)}, u32[]{:S(2)}, u32[]{:S(2)}) collective-permute-start(bf16[2,256,256]{2,1,0:T(8,128)(2,1)} %scale.1.own), channel_id=1, source_target_pairs={{0,4},{1,5},{2,6},{3,7},{4,8},{5,9},{6,10},{7,11},{8,12},{9,13},{1... | collective-permute-start | bytes 786440 | tf_op jit(solution)/shard_map/ppermute | solution.py:203
  6.2 0.7 %copy-start.3 = (s32[4,256]{1,0:T(4,128)S(1)}, s32[4,256]{1,0:T(4,128)}, u32[]{:S(2)}) copy-start(s32[4,256]{1,0:T(4,128)} %shift_ref.1) | copy-start | bytes 12292
  6.8 0.7 %copy-start.4 = (s32[4,256]{1,0:T(4,128)S(1)}, s32[4,256]{1,0:T(4,128)}, u32[]{:S(2)}) copy-start(s32[4,256]{1,0:T(4,128)} %flip_ref.1) | copy-start | bytes 12292
  11.3 1.0 %copy-start = (bf16[2,256,256]{2,1,0:T(8,128)(2,1)S(1)}, bf16[2,256,256]{2,1,0:T(8,128)(2,1)}, u32[]{:S(2)}) copy-start(bf16[2,256,256]{2,1,0:T(8,128)(2,1)} %scale.1.own) | copy-start | bytes 786436
  12.2 1.0 %copy-start.1 = (f32[2,4,64,256]{3,2,1,0:T(8,128)S(1)}, f32[2,4,64,256]{3,2,1,0:T(8,128)}, u32[]{:S(2)}) copy-start(f32[2,4,64,256]{3,2,1,0:T(8,128)} %ph_in.1) | copy-start | bytes 1572868
  13.3 1.0 %copy-start.2 = (f32[2,4,64,256]{3,2,1,0:T(8,128)S(1)}, f32[2,4,64,256]{3,2,1,0:T(8,128)}, u32[]{:S(2)}) copy-start(f32[2,4,64,256]{3,2,1,0:T(8,128)} %pp_in.1) | copy-start | bytes 1572868
  18.0 0.7 %copy-start.5 = (bf16[2,256,256]{2,1,0:T(8,128)(2,1)}, bf16[2,256,256]{2,1,0:T(8,128)(2,1)S(1)}, u32[]{:S(2)}) copy-start(bf16[2,256,256]{2,1,0:T(8,128)(2,1)S(1)} %collective-permute-done.got) | copy-start | bytes 786436
  20.7 14.8 %collective-permute-start.3 = (bf16[2,256,256]{2,1,0:T(8,128)(2,1)}, bf16[2,256,256]{2,1,0:T(8,128)(2,1)S(1)}, u32[]{:S(2)}, u32[]{:S(2)}) collective-permute-start(bf16[2,256,256]{2,1,0:T(8,128)(2,1)} %get-tuple-element.35), channel_id=1, source_target_pairs={{0,2},{1,3},{2,0},{3,1},{4,6},{5,7},{6,4},{7,5},{8,10},{9,11},{10,... | collective-permute-start | bytes 786440 | tf_op jit(solution)/shard_map/ppermute | solution.py:207
  23.6 24.6 %collective-permute-start.1 = (bf16[2,256,256]{2,1,0:T(8,128)(2,1)}, bf16[2,256,256]{2,1,0:T(8,128)(2,1)S(1)}, u32[]{:S(2)}, u32[]{:S(2)}) collective-permute-start(bf16[2,256,256]{2,1,0:T(8,128)(2,1)} %get-tuple-element.33), channel_id=1, source_target_pairs={{0,3},{1,0},{2,1},{3,2},{4,7},{5,4},{6,5},{7,6},{8,11},{9,8},{10,9... | collective-permute-start | bytes 786440 | tf_op jit(solution)/shard_map/ppermute | solution.py:207
  24.4 17.4 %collective-permute-start.2 = (bf16[2,256,256]{2,1,0:T(8,128)(2,1)}, bf16[2,256,256]{2,1,0:T(8,128)(2,1)S(1)}, u32[]{:S(2)}, u32[]{:S(2)}) collective-permute-start(bf16[2,256,256]{2,1,0:T(8,128)(2,1)} %get-tuple-element.34), channel_id=1, source_target_pairs={{0,1},{1,2},{2,3},{3,0},{4,5},{5,6},{6,7},{7,4},{8,9},{9,10},{10,1... | collective-permute-start | bytes 786440 | tf_op jit(solution)/shard_map/ppermute | solution.py:207

commit v3 on v2

v3 whole, which is shorter than its diff:
```python
import functools
import math

import jax
import jax.numpy as jnp
from jax import lax
from jax.experimental import pallas as pl
from jax.experimental.pallas import tpu as pltpu
from jax.sharding import PartitionSpec as P

NK = 16
ORDER = 256
BAND = 64
TRANS = 4
COUPLING = 0.5
BF = jnp.bfloat16
F32 = jnp.float32
MIB = 1 << 20
TINY = pl.CostEstimate(flops=1, bytes_accessed=1, transcendentals=0)


def wave(freq, mom, tau, site):
    turns = ((2 * freq + 1) * tau - 2 * mom * site) & 31
    phase = turns.astype(F32) * (math.pi / 16.0)
    return (jnp.cos(phase) * 0.0625).astype(BF), (jnp.sin(phase) * 0.0625).astype(BF)


def table_kernel(place_ref, shift_in, flip_in, cols_ref, rows_ref, shift_ref, flip_ref, sems):
    fetch = [
        pltpu.make_async_copy(shift_in, shift_ref, sems.at[0]),
        pltpu.make_async_copy(flip_in, flip_ref, sems.at[1]),
    ]
    for copy in fetch:
        copy.start()
    square = (ORDER, ORDER)
    sub = lax.broadcasted_iota(jnp.int32, square, 0)
    lane = lax.broadcasted_iota(jnp.int32, square, 1)
    re, im = wave(lane >> 4, lane & 15, sub >> 4, sub & 15)
    cols_ref[2 * TRANS, :ORDER] = re
    cols_ref[2 * TRANS, ORDER:] = im
    re, im = wave(sub >> 4, sub & 15, lane >> 4, lane & 15)
    base = jnp.concatenate([re, im], 1)
    band_row = lax.broadcasted_iota(jnp.int32, (BAND, ORDER), 0) + place_ref[0] * BAND
    band_lane = lax.broadcasted_iota(jnp.int32, (BAND, ORDER), 1)

    def put_rows(slot, target):
        pick = jnp.where(band_lane == target, 1.0, 0.0).astype(BF)
        out = jnp.dot(pick, base, preferred_element_type=F32).astype(BF)
        rows_ref[2 * BAND * slot : 2 * BAND * slot + BAND] = out[:, :ORDER]
        rows_ref[2 * BAND * slot + BAND : 2 * BAND * (slot + 1)] = out[:, ORDER:]

    def put_cols(slot, target):
        pick = jnp.where(sub == target, 1.0, 0.0).astype(BF)
        cols_ref[slot] = jnp.dot(cols_ref[2 * TRANS], pick, preferred_element_type=F32).astype(BF)

    put_rows(0, band_row)
    for copy in fetch:
        copy.wait()
    for t in range(TRANS):
        freq, mom = shift_ref[t, 0] >> 4, shift_ref[t, 0] & 15

        def moved(i, freq=freq, mom=mom):
            return ((((i >> 4) + freq) & 15) << 4) + (((i & 15) + mom) & 15)

        put_rows(1 + t, moved(band_row))
        put_cols(t, moved(lane))
        freq, mom = flip_ref[t, 0] >> 4, flip_ref[t, 0] & 15

        def turned(i, freq=freq, mom=mom):
            return (((freq - (i >> 4)) & 15) << 4) + ((mom - (i & 15)) & 15)

        put_rows(1 + TRANS + t, turned(band_row))
        put_cols(TRANS + t, turned(lane))


def tables(place, shift, flip):
    return pl.pallas_call(
        table_kernel,
        out_shape=(
            jax.ShapeDtypeStruct((2 * TRANS + 1, 2 * ORDER, ORDER), BF),
            jax.ShapeDtypeStruct(((2 * TRANS + 1) * 2 * BAND, ORDER), BF),
        ),
        in_specs=[
            pl.BlockSpec(memory_space=pltpu.SMEM),
            pl.BlockSpec(memory_space=pltpu.HBM),
            pl.BlockSpec(memory_space=pltpu.HBM),
        ],
        out_specs=(pl.BlockSpec(memory_space=pltpu.VMEM),) * 2,
        scratch_shapes=[
            pltpu.SMEM((TRANS, ORDER), jnp.int32),
            pltpu.SMEM((TRANS, ORDER), jnp.int32),
            pltpu.SemaphoreType.DMA((2,)),
        ],
        cost_estimate=pl.CostEstimate(flops=4 * 10**9, bytes_accessed=1, transcendentals=0),
        compiler_params=pltpu.CompilerParams(vmem_limit_bytes=12 * MIB),
        name="tables",
    )(place, shift, flip)


def paired(re, im):
    return jnp.concatenate(
        [jnp.concatenate([re, im], 1), jnp.concatenate([im, -re], 1)], 0
    )


def halves(ref, begin):
    return paired(ref[begin : begin + BAND], ref[begin + BAND : begin + 2 * BAND])


def one_walker(up, down, cols, rows, first_up, first_down, plain, ready, put):
    step = 2 * BAND
    first_up[...] = jnp.dot(rows[: step * (TRANS + 1)], up, preferred_element_type=F32).astype(BF)
    first_down[...] = jnp.dot(rows[step:], down, preferred_element_type=F32).astype(BF)
    across = (((1,), (1,)), ((), ()))
    turned_up = lax.dot_general(rows[:step], up, across, preferred_element_type=F32).astype(BF)
    turned_down = lax.dot_general(rows[:step], down, across, preferred_element_type=F32).astype(BF)
    left = jnp.concatenate(
        [halves(turned_up, 0), halves(turned_down, 0), halves(first_up, 0)], 0
    )
    plain[...] = jnp.dot(left, cols[2 * TRANS], preferred_element_type=F32)
    ready()
    for t in range(TRANS):
        left = jnp.concatenate([halves(first_up, step * (1 + t)), halves(first_down, step * t)], 0)
        moved = jnp.dot(left, cols[t], preferred_element_type=F32)
        real, imag = 0.0, 0.0
        for s in range(2):
            nr, ni = plain[step * s : step * s + BAND], plain[step * s + BAND : step * (s + 1)]
            mr, mi = moved[step * s : step * s + BAND], moved[step * s + BAND : step * (s + 1)]
            real = real + (nr * mr + ni * mi)
            imag = imag + (nr * mi - ni * mr)
        put(0, 0, t, real)
        put(0, 1, t, imag)
        low = jnp.dot(
            halves(first_down, step * (TRANS + t)), cols[TRANS + t], preferred_element_type=F32
        )
        nr, ni = plain[2 * step : 2 * step + BAND], plain[2 * step + BAND : 3 * step]
        put(1, 0, t, nr * low[:BAND] - ni * low[BAND:])
        put(1, 1, t, nr * low[BAND:] + ni * low[:BAND])


WORK = [
    pltpu.VMEM((2 * BAND * (TRANS + 1), ORDER), BF),
    pltpu.VMEM((2 * BAND * 2 * TRANS, ORDER), BF),
    pltpu.VMEM((6 * BAND, ORDER), F32),
]
SUMS = (2, TRANS, BAND, ORDER)
IN_VMEM = pl.BlockSpec(memory_space=pltpu.VMEM)
IN_SMEM = pl.BlockSpec(memory_space=pltpu.SMEM)
ANYWHERE = pl.BlockSpec(memory_space=pl.ANY)
IN_HBM = pl.BlockSpec(memory_space=pltpu.HBM)
BIG = pltpu.CompilerParams(vmem_limit_bytes=16 * MIB)


def open_kernel(
    piece, cols, rows, ph_in, pp_in, ph, pp, token, first_up, first_down, plain, sems
):
    loads = [
        pltpu.make_async_copy(source.at[part], target.at[part], sems.at[i, part])
        for i, (source, target) in enumerate(((ph_in, ph), (pp_in, pp)))
        for part in range(2)
    ]
    for load in loads:
        load.start()

    def ready():
        for load in loads:
            load.wait()

    def put(which, part, t, term):
        (ph, pp)[which][part, t] += term

    one_walker(piece[0], piece[1], cols, rows, first_up, first_down, plain, ready, put)
    token[...] = jnp.zeros_like(token)


def open_sums(piece, cols, rows, ph, pp):
    return pl.pallas_call(
        open_kernel,
        out_shape=(jax.ShapeDtypeStruct(SUMS, F32),) * 2
        + (jax.ShapeDtypeStruct((8, 128), F32),),
        in_specs=[IN_VMEM] * 3 + [IN_HBM] * 2,
        out_specs=(IN_VMEM,) * 3,
        scratch_shapes=WORK + [pltpu.SemaphoreType.DMA((2, 2))],
        cost_estimate=TINY,
        compiler_params=BIG,
        name="open_sums",
    )(piece, cols, rows, ph, pp)


def add_kernel(names, held, place, *refs):
    count = len(names["in"])
    pieces, (cols, rows, ph_in, pp_in, ph, pp) = refs[:count], refs[count : count + 6]
    kept, (first_up, first_down, plain) = refs[count + 6 : -3], refs[-3:]
    other = 1 - (place[0] & 1)
    for i, sheet in enumerate(held):
        piece, spin = sheet
        kept[i // 3][i % 3] = pieces[piece][spin]
    first = True
    for walker in names["walkers"]:
        if names["gathered"]:
            up, down = [pieces[w // 3][other, w % 3] for w in (2 * walker, 2 * walker + 1)]
        else:
            up, down = pieces[walker][0], pieces[walker][1]

        def put(which, part, t, term, first=first):
            source = (ph_in, pp_in) if first else (ph, pp)
            (ph, pp)[which][part, t] = source[which][part, t] + term

        one_walker(up, down, cols, rows, first_up, first_down, plain, lambda: None, put)
        first = False


def add(place, pieces, cols, rows, ph, pp, walkers, held=(), gathered=False):
    count = len(pieces)
    out_shape = [jax.ShapeDtypeStruct(SUMS, F32)] * 2
    out_shape += [jax.ShapeDtypeStruct((3, ORDER, ORDER), BF)] * (len(held) // 3)
    names = {"in": range(count), "walkers": walkers, "gathered": gathered}
    return pl.pallas_call(
        functools.partial(add_kernel, names, held),
        out_shape=tuple(out_shape),
        in_specs=[IN_SMEM] + [IN_VMEM] * (count + 4),
        out_specs=(IN_VMEM,) * len(out_shape),
        scratch_shapes=WORK,
        cost_estimate=TINY,
        compiler_params=BIG,
        name="add",
    )(place, *pieces, cols, rows, ph, pp)


def close_kernel(
    piece, cols, rows, ph_in, pp_in, ph, pp, first_up, first_down, plain, ph_sum, pp_sum, sems
):
    stores = []

    def put(which, part, t, term):
        source, total, target = ((ph_in, ph_sum, ph), (pp_in, pp_sum, pp))[which]
        total[part, t] = source[part, t] + term
        store = pltpu.make_async_copy(
            total.at[part, t], target.at[part, t], sems.at[which, part, t]
        )
        store.start()
        stores.append(store)

    one_walker(piece[0], piece[1], cols, rows, first_up, first_down, plain, lambda: None, put)
    for store in stores:
        store.wait()


def close_sums(piece, cols, rows, ph, pp):
    return pl.pallas_call(
        close_kernel,
        out_shape=(jax.ShapeDtypeStruct(SUMS, F32),) * 2,
        in_specs=[IN_VMEM] * 5,
        out_specs=(ANYWHERE,) * 2,
        scratch_shapes=WORK
        + [pltpu.VMEM(SUMS, F32)] * 2
        + [pltpu.SemaphoreType.DMA((2, 2, TRANS))],
        cost_estimate=TINY,
        compiler_params=BIG,
        name="close_sums",
    )(piece, cols, rows, ph, pp)


def scale_kernel(masses, spins, out):
    signed = (2 * spins[...] - 1).astype(F32)
    sign = jnp.where(pl.program_id(0) < 2, COUPLING, -COUPLING)
    out[0] = (masses[0, 0].astype(F32) * jnp.exp(sign * signed)).astype(BF)


def scale(masses, spins):
    half = ORDER // 2
    return pl.pallas_call(
        scale_kernel,
        grid=(4,),
        out_shape=jax.ShapeDtypeStruct((2, ORDER, ORDER), BF),
        in_specs=[
            pl.BlockSpec((1, 1, half, ORDER), lambda i: (0, i // 2, i % 2, 0)),
            pl.BlockSpec((1, ORDER), lambda i: (0, 0)),
        ],
        out_specs=pl.BlockSpec((1, half, ORDER), lambda i: (i // 2, i % 2, 0)),
        cost_estimate=TINY,
        compiler_params=pltpu.CompilerParams(vmem_limit_bytes=56 * MIB),
        name="scale",
    )(masses, spins)


def route_kernel(place, y_ref, own, got, token, *refs):
    outs, sems = refs[:3], refs[3]
    core = place[0] & 1
    for i, step in enumerate(Y_STEPS):
        keep = (core == 0) | (y_ref[0] + step >= PLANE)

        @pl.when(keep)
        def _(i=i):
            pltpu.make_async_copy(got, outs[i], sems.at[i]).start()

        @pl.when(jnp.logical_not(keep))
        def _(i=i):
            pltpu.make_async_copy(own, outs[i], sems.at[i]).start()

    for i in range(3):
        pltpu.make_async_copy(own, outs[i], sems.at[i]).wait()


def route(place, y, own, got, token):
    return pl.pallas_call(
        route_kernel,
        out_shape=(jax.ShapeDtypeStruct(own.shape, BF),) * 3,
        in_specs=[IN_SMEM] * 2 + [ANYWHERE] * 3,
        out_specs=(ANYWHERE,) * 3,
        scratch_shapes=[pltpu.SemaphoreType.DMA((3,))],
        cost_estimate=TINY,
        compiler_params=pltpu.CompilerParams(vmem_limit_bytes=MIB),
        name="route",
    )(place, y, own, got, token)


Y_STEPS = (1, 3, 2)
PLANE = 4
BLOCKS = 64


def planes_back(value):
    pairs = [
        (g * BLOCKS + b, g * BLOCKS + (b + PLANE * (1 + g % 2)) % BLOCKS)
        for g in range(4)
        for b in range(BLOCKS)
    ]
    return lax.ppermute(value, ("grp", "blk"), pairs)


def along_y(value, steps):
    return lax.ppermute(value, "blk", [(s, s // 4 * 4 + (s + steps) % 4) for s in range(BLOCKS)])


def both_cores(value):
    return lax.all_gather(value, "grp", axis=0, axis_index_groups=[[0, 1], [2, 3]])


def other_core(value):
    return lax.ppermute(value, "grp", [(s, s ^ 1) for s in range(4)])


def on_device(masses, spins, shift_table, flip_table, ph_in, pp_in):
    place = lax.axis_index("grp").reshape(1).astype(jnp.int32)
    y = (lax.axis_index("blk") % PLANE).reshape(1).astype(jnp.int32)
    own = scale(masses, spins)
    got = planes_back(own)
    cols, rows = tables(place, shift_table, flip_table)
    ph, pp, token = open_sums(own, cols, rows, ph_in, pp_in)
    got, token = lax.optimization_barrier((got, token))
    sent = route(place, y, own, got, token)
    right, left, middle = [along_y(v, d) for v, d in zip(sent, Y_STEPS)]
    ph, pp = add(place, [got], cols, rows, ph, pp, (0,))
    right, left, ph, pp = lax.optimization_barrier((right, left, ph, pp))
    sheets = tuple((piece, spin) for piece in range(3) for spin in range(2))
    ph, pp, *held = add(place, [got, right, left], cols, rows, ph, pp, (1, 2), sheets)
    held = [both_cores(v) for v in held]
    ph, pp = add(place, held, cols, rows, ph, pp, (0, 1, 2), gathered=True)
    middle, ph, pp = lax.optimization_barrier((middle, ph, pp))
    swapped = other_core(middle)
    ph, pp = add(place, [middle], cols, rows, ph, pp, (0,))
    return close_sums(swapped, cols, rows, ph, pp)


def solution(mesh):
    placed = (
        P("blk", None, None, None),
        P("blk", None),
        P("blk", None),
        P("blk", None),
        P(None, "blk", "grp", None),
        P(None, "blk", "grp", None),
    )
    return jax.shard_map(
        on_device,
        mesh=mesh,
        in_specs=placed,
        out_specs=(P(None, "blk", "grp", None), P(None, "blk", "grp", None)),
        check_vma=False,
    )
```

time: 55 us -> 48.1 us (0.87)
  Pallas kernels: 25.8 us -> 17.2 us
  waiting for transfers between devices: 1.72 us -> 3.97 us
  blocking collectives: 13 us -> 11.8 us
    pallas_call x6 -> x7, Pallas kernels: 20.1 us -> 13.5 us  [the longest x4 7.08 us: add(): pl.pallas_call(functools.partial(add_kernel, names, held), out_shape=tupl...]
    ppermute x1, waiting for transfers between devices: 1.71 us -> 3.71 us  [planes_back(): return lax.ppermute(value, ('grp', 'blk'), pairs)]
    pallas_call x1, Pallas kernels: 2 us -> 0.1 us  [route(): pl.pallas_call(route_kernel, out_shape=(jax.ShapeDtypeStruct(own.shape, B...]
    all_gather x4 -> x2, blocking collectives: 13 us -> 11.8 us  [both_cores(): lax.all_gather(value, 'grp', axis=0, axis_index_groups=[[0, 1], [2, 3]])]
    unnamed x12 -> x18, local copies, waits for them, and re-layouts: 5.1 us -> 5.05 us
  transfers between devices with their start and end apart: 4 -> 5, of which waited for: 1 -> 3; matrix products, arithmetic and copies ran while one was open for 0% -> 0% of each run, Pallas kernels for 33% -> 26%
where the time goes in v3:
time: 48.1 us; the launch traced here: 47.7 us
  Pallas kernels  17.2 us (36%)
  blocking collectives  11.8 us (25%)
  starting transfers between devices  8.74 us (18%)
  local copies, waits for them, and re-layouts  5.05 us (10%)
  waiting for transfers between devices  3.97 us (8%)
  between operations  0.9 us (2%)
    all_gather x2, blocking collectives, both_cores(): lax.all_gather(value, 'grp', axis=0, axis_index_groups=[[0, 1], [2, 3]])  11.8 us
    pallas_call x4, Pallas kernels, add(): pl.pallas_call(functools.partial(add_kernel, names, held), out_shape=tupl...  7.08 us
    unnamed x18, local copies, waits for them, and re-layouts  5.05 us
    ppermute x3, starting transfers between devices, along_y(): lax.ppermute(value, 'blk', [(s, s // 4 * 4 + (s + steps) % 4) for s in ra...  4.46 us
    ppermute x1, starting transfers between devices, planes_back(): return lax.ppermute(value, ('grp', 'blk'), pairs)  3.82 us
    ppermute x1, waiting for transfers between devices, planes_back(): return lax.ppermute(value, ('grp', 'blk'), pairs)  3.71 us
    pallas_call x1, Pallas kernels, tables(): pl.pallas_call(table_kernel, out_shape=(jax.ShapeDtypeStruct((2 * TRANS +...  3.67 us
    pallas_call x1, Pallas kernels, scale(): pl.pallas_call(scale_kernel, grid=(4,), out_shape=jax.ShapeDtypeStruct((2...  3 us
  transfers between devices with their start and end apart: 5, of which 3 were waited for; matrix products, arithmetic and copies ran while one was open for 0% of the time, Pallas kernels for 26%

profile of v3, /device:TPU:1, one launch (start us, length us, event | category | flops | bytes accessed | tf_op | source)
XLA Modules:
  0.0 47.7 jit_solution(14759951361898072656)
XLA Ops:
  0.6 3.0 %scale.1.piece.own = bf16[2,256,256]{2,1,0:T(8,128)(2,1)} custom-call(bf16[1,2,256,256]{3,2,1,0:T(8,128)(2,1)} %masses.1, s32[1,256]{1,0:T(1,128)} %spins.1), custom_call_target="tpu_custom_call" | custom-call | flops 1 | bytes 1 | tf_op jit(solution)/shard_map/scale/pallas_call | solution.py:272
  3.6 3.8 %collective-permute-start = (bf16[2,256,256]{2,1,0:T(8,128)(2,1)}, bf16[2,256,256]{2,1,0:T(8,128)(2,1)S(1)}, u32[]{:S(2)}, u32[]{:S(2)}) collective-permute-start(bf16[2,256,256]{2,1,0:T(8,128)(2,1)} %scale.1.piece.own), channel_id=1, source_target_pairs={{0,4},{1,5},{2,6},{3,7},{4,8},{5,9},{6,10},{7,11},{8,12},{9,13},{1... | collective-permute-start | bytes 786440 | tf_op jit(solution)/shard_map/ppermute | solution.py:329
  7.5 0.0 copy-start.7
  7.5 0.7 %copy-done.7 = s32[4,256]{1,0:T(4,128)S(1)} copy-done((s32[4,256]{1,0:T(4,128)S(1)}, s32[4,256]{1,0:T(4,128)}, u32[]{:S(2)}) %copy-start.7) | copy-done | bytes 4120
  8.1 0.0 copy-start.8
  8.1 0.7 %copy-done.8 = s32[4,256]{1,0:T(4,128)S(1)} copy-done((s32[4,256]{1,0:T(4,128)S(1)}, s32[4,256]{1,0:T(4,128)}, u32[]{:S(2)}) %copy-start.8) | copy-done | bytes 4120
  8.8 0.0 copy-start
  8.8 0.0 copy-start.5
  8.8 0.0 copy-start.6
  8.8 3.7 %tables.1 = (bf16[9,512,256]{2,1,0:T(8,128)(2,1)S(1)}, bf16[1152,256]{1,0:T(8,128)(2,1)S(1)}) custom-call(s32[1]{0:T(128)} %bitcast.place_ref.place, s32[4,256]{1,0:T(4,128)S(1)} %copy-done.7, s32[4,256]{1,0:T(4,128)S(1)} %copy-done.8), custom_call_target="tpu_custom_call" | custom-call | flops 4000000000 | bytes 1 | tf_op jit(solution)/shard_map/tables/pallas_call | solution.py:77
  12.5 0.0 copy-done
  12.5 0.0 copy-done.5
  12.5 0.0 copy-done.6
  12.5 1.5 %open_sums.1 = (f32[2,4,64,256]{3,2,1,0:T(8,128)S(1)}, f32[2,4,64,256]{3,2,1,0:T(8,128)S(1)}, f32[8,128]{1,0:T(8,128)S(1)}) custom-call(bf16[2,256,256]{2,1,0:T(8,128)(2,1)S(1)} %copy-done, bf16[9,512,256]{2,1,0:T(8,128)(2,1)S(1)} %get-tuple-element.29.cols.refs_1_.refs_3_.refs_2_, bf16[1152,256]{1,0:T(8,128)(2,1)S(1)} %get-tuple-element.30.rows.refs_2_.refs_4_.refs_3_, ...), custom_call_target="tpu_custom_call" | custom-call | flops 1 | bytes 1 | tf_op jit(solution)/shard_map/open_sums/pallas_call | solution.py:177
  14.0 0.0 copy-start.1
  14.0 0.8 %copy-done.1 = f32[2,4,64,256]{3,2,1,0:T(8,128)} copy-done((f32[2,4,64,256]{3,2,1,0:T(8,128)}, f32[2,4,64,256]{3,2,1,0:T(8,128)S(1)}, u32[]{:S(2)}) %copy-start.1) | copy-done | bytes 524312
  14.8 0.0 copy-start.3
  14.8 0.8 %copy-done.3 = f32[2,4,64,256]{3,2,1,0:T(8,128)} copy-done((f32[2,4,64,256]{3,2,1,0:T(8,128)}, f32[2,4,64,256]{3,2,1,0:T(8,128)S(1)}, u32[]{:S(2)}) %copy-start.3) | copy-done | bytes 524312
  15.6 3.7 %collective-permute-done.got.refs_0_ = bf16[2,256,256]{2,1,0:T(8,128)(2,1)S(1)} collective-permute-done((bf16[2,256,256]{2,1,0:T(8,128)(2,1)}, bf16[2,256,256]{2,1,0:T(8,128)(2,1)S(1)}, u32[]{:S(2)}, u32[]{:S(2)}) %collective-permute-start) | collective-permute-done | bytes 262176 | tf_op jit(solution)/shard_map/ppermute | solution.py:329
  19.3 0.1 route.1
  19.4 1.4 %collective-permute-start.2 = (bf16[2,256,256]{2,1,0:T(8,128)(2,1)S(1)}, bf16[2,256,256]{2,1,0:T(8,128)(2,1)S(1)}, u32[]{:S(2)}, u32[]{:S(2)}) collective-permute-start(bf16[2,256,256]{2,1,0:T(8,128)(2,1)S(1)} %get-tuple-element.35), channel_id=1, source_target_pairs={{0,1},{1,2},{2,3},{3,0},{4,5},{5,6},{6,7},{7,4},{8,9},{9,10},{10,1... | collective-permute-start | bytes 786440 | tf_op jit(solution)/shard_map/ppermute | solution.py:333
  20.8 1.5 %collective-permute-start.3 = (bf16[2,256,256]{2,1,0:T(8,128)(2,1)S(1)}, bf16[2,256,256]{2,1,0:T(8,128)(2,1)S(1)}, u32[]{:S(2)}, u32[]{:S(2)}) collective-permute-start(bf16[2,256,256]{2,1,0:T(8,128)(2,1)S(1)} %get-tuple-element.36), channel_id=1, source_target_pairs={{0,3},{1,0},{2,1},{3,2},{4,7},{5,4},{6,5},{7,6},{8,11},{9,8},{10,9... | collective-permute-start | bytes 786440 | tf_op jit(solution)/shard_map/ppermute | solution.py:333
  22.3 1.6 %collective-permute-start.1 = (bf16[2,256,256]{2,1,0:T(8,128)(2,1)S(1)}, bf16[2,256,256]{2,1,0:T(8,128)(2,1)S(1)}, u32[]{:S(2)}, u32[]{:S(2)}) collective-permute-start(bf16[2,256,256]{2,1,0:T(8,128)(2,1)S(1)} %get-tuple-element.34), channel_id=1, source_target_pairs={{0,2},{1,3},{2,0},{3,1},{4,6},{5,7},{6,4},{7,5},{8,10},{9,11},{10,... | collective-permute-start | bytes 786440 | tf_op jit(solution)/shard_map/ppermute | solution.py:333
  23.9 0.0 copy-start.2
  23.9 1.0 %copy-done.2 = f32[2,4,64,256]{3,2,1,0:T(8,128)S(1)} copy-done((f32[2,4,64,256]{3,2,1,0:T(8,128)S(1)}, f32[2,4,64,256]{3,2,1,0:T(8,128)}, u32[]{:S(2)}) %copy-start.2) | copy-done | bytes 524312
  24.9 0.0 copy-start.4
  24.9 1.0 %copy-done.4 = f32[2,4,64,256]{3,2,1,0:T(8,128)S(1)} copy-done((f32[2,4,64,256]{3,2,1,0:T(8,128)S(1)}, f32[2,4,64,256]{3,2,1,0:T(8,128)}, u32[]{:S(2)}) %copy-start.4) | copy-done | bytes 524312
  26.0 1.1 %add.9 = (f32[2,4,64,256]{3,2,1,0:T(8,128)S(1)}, f32[2,4,64,256]{3,2,1,0:T(8,128)S(1)}) custom-call(s32[1]{0:T(128)} %bitcast.place_ref.place, bf16[2,256,256]{2,1,0:T(8,128)(2,1)S(1)} %collective-permute-done.got.refs_0_, bf16[9,512,256]{2,1,0:T(8,128)(2,1)S(1)} %get-tuple-element.29.cols.refs_1_.refs_3_.refs_2_, ...), custom_call_target="tpu_custom_call" | custom-call | flops 1 | bytes 1 | tf_op jit(solution)/shard_map/add/pallas_call | solution.py:218
  27.0 0.0 collective-permute-done.2.refs_1_
  27.1 0.2 collective-permute-done.3.refs_2_
  27.2 2.1 %add.10 = (f32[2,4,64,256]{3,2,1,0:T(8,128)S(1)}, f32[2,4,64,256]{3,2,1,0:T(8,128)S(1)}, bf16[3,256,256]{2,1,0:T(8,128)(2,1)S(1)}, bf16[3,256,256]{2,1,0:T(8,128)(2,1)S(1)}) custom-call(s32[1]{0:T(128)} %bitcast.place_ref.place, bf16[2,256,256]{2,1,0:T(8,128)(2,1)S(1)} %collective-permute-done.got.refs_0_, ...), custom_call_target="tpu_custom_call" | custom-call | flops 1 | bytes 1 | tf_op jit(solution)/shard_map/add/pallas_call | solution.py:218
  29.3 9.3 %all-gather = bf16[6,256,256]{2,1,0:T(8,128)(2,1)S(1)} all-gather(bf16[3,256,256]{2,1,0:T(8,128)(2,1)S(1)} %get-tuple-element.45), channel_id=2, replica_groups={{0,64},{128,192},{1,65},{129,193},{2,66},{130,194},{3,67},{131,195},{4,..., dimensions={0}, use_global_device_ids=true | all-gather | bytes 1179648 | tf_op jit(solution)/shard_map/all_gather | solution.py:337
  38.6 2.5 %all-gather.1 = bf16[6,256,256]{2,1,0:T(8,128)(2,1)S(1)} all-gather(bf16[3,256,256]{2,1,0:T(8,128)(2,1)S(1)} %get-tuple-element.46), channel_id=3, replica_groups={{0,64},{128,192},{1,65},{129,193},{2,66},{130,194},{3,67},{131,195},{4,..., dimensions={0}, use_global_device_ids=true | all-gather | bytes 1179648 | tf_op jit(solution)/shard_map/all_gather | solution.py:337
  41.1 2.9 %add.11 = (f32[2,4,64,256]{3,2,1,0:T(8,128)S(1)}, f32[2,4,64,256]{3,2,1,0:T(8,128)S(1)}) custom-call(s32[1]{0:T(128)} %bitcast.place_ref.place, bf16[2,3,256,256]{3,2,1,0:T(8,128)(2,1)S(1)} %bitcast.4, bf16[2,3,256,256]{3,2,1,0:T(8,128)(2,1)S(1)} %bitcast.5, bf16[9,512,256]{2,1,0:T(8,128)(2,1)S(1)} %get-tuple-element.29.cols.refs_1_.refs_3_.refs_2_, ...), custom_call_target="tpu_custom_call" | custom-call | flops 1 | bytes 1 | tf_op jit(solution)/shard_map/add/pallas_call | solution.py:218
  44.0 0.0 collective-permute-done.1.refs_0_
  44.0 0.5 collective-permute-start.4
  44.5 1.1 %add.12 = (f32[2,4,64,256]{3,2,1,0:T(8,128)S(1)}, f32[2,4,64,256]{3,2,1,0:T(8,128)S(1)}) custom-call(s32[1]{0:T(128)} %bitcast.place_ref.place, bf16[2,256,256]{2,1,0:T(8,128)(2,1)S(1)} %collective-permute-done.1.refs_0_, bf16[9,512,256]{2,1,0:T(8,128)(2,1)S(1)} %get-tuple-element.29.cols.refs_1_.refs_3_.refs_2_, ...), custom_call_target="tpu_custom_call" | custom-call | flops 1 | bytes 1 | tf_op jit(solution)/shard_map/add/pallas_call | solution.py:218
  45.6 0.1 collective-permute-done.4.piece
  45.6 1.9 %close_sums.1 = (f32[2,4,64,256]{3,2,1,0:T(8,128)}, f32[2,4,64,256]{3,2,1,0:T(8,128)}) custom-call(bf16[2,256,256]{2,1,0:T(8,128)(2,1)S(1)} %collective-permute-done.4.piece, bf16[9,512,256]{2,1,0:T(8,128)(2,1)S(1)} %get-tuple-element.29.cols.refs_1_.refs_3_.refs_2_, bf16[1152,256]{1,0:T(8,128)(2,1)S(1)} %get-tuple-element.30.rows.refs_2_.refs_4_.refs_3_, ...), custom_call_target="tpu_custom_call" | custom-call | flops 1 | bytes 1 | tf_op jit(solution)/shard_map/close_sums/pallas_call | solution.py:250
Async XLA Ops:
  3.6 15.7 %collective-permute-start = (bf16[2,256,256]{2,1,0:T(8,128)(2,1)}, bf16[2,256,256]{2,1,0:T(8,128)(2,1)S(1)}, u32[]{:S(2)}, u32[]{:S(2)}) collective-permute-start(bf16[2,256,256]{2,1,0:T(8,128)(2,1)} %scale.1.piece.own), channel_id=1, source_target_pairs={{0,4},{1,5},{2,6},{3,7},{4,8},{5,9},{6,10},{7,11},{8,12},{9,13},{1... | collective-permute-start | bytes 786440 | tf_op jit(solution)/shard_map/ppermute | solution.py:329
  7.5 0.7 %copy-start.7 = (s32[4,256]{1,0:T(4,128)S(1)}, s32[4,256]{1,0:T(4,128)}, u32[]{:S(2)}) copy-start(s32[4,256]{1,0:T(4,128)} %shift_in.1) | copy-start | bytes 12292
  8.1 0.7 %copy-start.8 = (s32[4,256]{1,0:T(4,128)S(1)}, s32[4,256]{1,0:T(4,128)}, u32[]{:S(2)}) copy-start(s32[4,256]{1,0:T(4,128)} %flip_in.1) | copy-start | bytes 12292
  8.8 3.7 %copy-start = (bf16[2,256,256]{2,1,0:T(8,128)(2,1)S(1)}, bf16[2,256,256]{2,1,0:T(8,128)(2,1)}, u32[]{:S(2)}) copy-start(bf16[2,256,256]{2,1,0:T(8,128)(2,1)} %scale.1.piece.own) | copy-start | bytes 786436
  8.8 3.7 %copy-start.5 = (f32[2,4,64,256]{3,2,1,0:T(8,128)S(1)}, f32[2,4,64,256]{3,2,1,0:T(8,128)}, u32[]{:S(2)}) copy-start(f32[2,4,64,256]{3,2,1,0:T(8,128)} %ph_in.1) | copy-start | bytes 1572868
  8.8 3.7 %copy-start.6 = (f32[2,4,64,256]{3,2,1,0:T(8,128)S(1)}, f32[2,4,64,256]{3,2,1,0:T(8,128)}, u32[]{:S(2)}) copy-start(f32[2,4,64,256]{3,2,1,0:T(8,128)} %pp_in.1) | copy-start | bytes 1572868
  14.0 0.8 %copy-start.1 = (f32[2,4,64,256]{3,2,1,0:T(8,128)}, f32[2,4,64,256]{3,2,1,0:T(8,128)S(1)}, u32[]{:S(2)}) copy-start(f32[2,4,64,256]{3,2,1,0:T(8,128)S(1)} %get-tuple-element.37.refs_3_) | copy-start | bytes 1572868
  14.8 0.8 %copy-start.3 = (f32[2,4,64,256]{3,2,1,0:T(8,128)}, f32[2,4,64,256]{3,2,1,0:T(8,128)S(1)}, u32[]{:S(2)}) copy-start(f32[2,4,64,256]{3,2,1,0:T(8,128)S(1)} %get-tuple-element.38.refs_4_) | copy-start | bytes 1572868
  19.4 7.6 %collective-permute-start.2 = (bf16[2,256,256]{2,1,0:T(8,128)(2,1)S(1)}, bf16[2,256,256]{2,1,0:T(8,128)(2,1)S(1)}, u32[]{:S(2)}, u32[]{:S(2)}) collective-permute-start(bf16[2,256,256]{2,1,0:T(8,128)(2,1)S(1)} %get-tuple-element.35), channel_id=1, source_target_pairs={{0,1},{1,2},{2,3},{3,0},{4,5},{5,6},{6,7},{7,4},{8,9},{9,10},{10,1... | collective-permute-start | bytes 786440 | tf_op jit(solution)/shard_map/ppermute | solution.py:333
  20.8 6.4 %collective-permute-start.3 = (bf16[2,256,256]{2,1,0:T(8,128)(2,1)S(1)}, bf16[2,256,256]{2,1,0:T(8,128)(2,1)S(1)}, u32[]{:S(2)}, u32[]{:S(2)}) collective-permute-start(bf16[2,256,256]{2,1,0:T(8,128)(2,1)S(1)} %get-tuple-element.36), channel_id=1, source_target_pairs={{0,3},{1,0},{2,1},{3,2},{4,7},{5,4},{6,5},{7,6},{8,11},{9,8},{10,9... | collective-permute-start | bytes 786440 | tf_op jit(solution)/shard_map/ppermute | solution.py:333
  22.3 21.7 %collective-permute-start.1 = (bf16[2,256,256]{2,1,0:T(8,128)(2,1)S(1)}, bf16[2,256,256]{2,1,0:T(8,128)(2,1)S(1)}, u32[]{:S(2)}, u32[]{:S(2)}) collective-permute-start(bf16[2,256,256]{2,1,0:T(8,128)(2,1)S(1)} %get-tuple-element.34), channel_id=1, source_target_pairs={{0,2},{1,3},{2,0},{3,1},{4,6},{5,7},{6,4},{7,5},{8,10},{9,11},{10,... | collective-permute-start | bytes 786440 | tf_op jit(solution)/shard_map/ppermute | solution.py:333
  23.9 1.0 %copy-start.2 = (f32[2,4,64,256]{3,2,1,0:T(8,128)S(1)}, f32[2,4,64,256]{3,2,1,0:T(8,128)}, u32[]{:S(2)}) copy-start(f32[2,4,64,256]{3,2,1,0:T(8,128)} %copy-done.1) | copy-start | bytes 1572868
  24.9 1.0 %copy-start.4 = (f32[2,4,64,256]{3,2,1,0:T(8,128)S(1)}, f32[2,4,64,256]{3,2,1,0:T(8,128)}, u32[]{:S(2)}) copy-start(f32[2,4,64,256]{3,2,1,0:T(8,128)} %copy-done.3) | copy-start | bytes 1572868
  44.0 1.6 %collective-permute-start.4 = (bf16[2,256,256]{2,1,0:T(8,128)(2,1)S(1)}, bf16[2,256,256]{2,1,0:T(8,128)(2,1)S(1)}, u32[]{:S(2)}, u32[]{:S(2)}) collective-permute-start(bf16[2,256,256]{2,1,0:T(8,128)(2,1)S(1)} %collective-permute-done.1.refs_0_), channel_id=1, source_target_pairs={{0,64},{64,0},{128,192},{192,128},{1,65},{65,1},{129,193},{193,129... | collective-permute-start | bytes 786440 | tf_op jit(solution)/shard_map/ppermute | solution.py:341

commit v4 on v3

v4 whole, which is shorter than its diff:
```python
import functools
import math

import jax
import jax.numpy as jnp
from jax import lax
from jax.experimental import pallas as pl
from jax.experimental.pallas import tpu as pltpu
from jax.sharding import PartitionSpec as P

NK = 16
ORDER = 256
BAND = 64
TRANS = 4
COUPLING = 0.5
BF = jnp.bfloat16
F32 = jnp.float32
MIB = 1 << 20
TINY = pl.CostEstimate(flops=1, bytes_accessed=1, transcendentals=0)


def wave(freq, mom, tau, site):
    turns = ((2 * freq + 1) * tau - 2 * mom * site) & 31
    phase = turns.astype(F32) * (math.pi / 16.0)
    return (jnp.cos(phase) * 0.0625).astype(BF), (jnp.sin(phase) * 0.0625).astype(BF)


def table_kernel(
    place_ref, shift_in, flip_in, cols_ref, rows_ref, shift_ref, flip_ref, sems
):
    fetch = [
        pltpu.make_async_copy(shift_in, shift_ref, sems.at[0]),
        pltpu.make_async_copy(flip_in, flip_ref, sems.at[1]),
    ]
    for copy in fetch:
        copy.start()
    square = (ORDER, ORDER)
    sub = lax.broadcasted_iota(jnp.int32, square, 0)
    lane = lax.broadcasted_iota(jnp.int32, square, 1)
    re, im = wave(lane >> 4, lane & 15, sub >> 4, sub & 15)
    cols_ref[2 * TRANS, :ORDER] = re
    cols_ref[2 * TRANS, ORDER:] = im
    re, im = wave(sub >> 4, sub & 15, lane >> 4, lane & 15)
    base = jnp.concatenate([re, im], 1)
    both = lax.broadcasted_iota(jnp.int32, (2 * BAND, ORDER), 0)
    grp = jnp.where(both < BAND, place_ref[0], place_ref[0] ^ 1)
    band_row = (both & (BAND - 1)) + grp * BAND
    band_lane = lax.broadcasted_iota(jnp.int32, (2 * BAND, ORDER), 1)

    def put_rows(slot, target):
        pick = jnp.where(band_lane == target, 1.0, 0.0).astype(BF)
        out = jnp.dot(pick, base, preferred_element_type=F32).astype(BF)
        for b in range(2):
            part = out[BAND * b : BAND * (b + 1)]
            rows_ref[b, 2 * BAND * slot : 2 * BAND * slot + BAND] = part[:, :ORDER]
            rows_ref[b, 2 * BAND * slot + BAND : 2 * BAND * (slot + 1)] = part[:, ORDER:]

    def put_cols(slot, target):
        pick = jnp.where(sub == target, 1.0, 0.0).astype(BF)
        cols_ref[slot] = jnp.dot(cols_ref[2 * TRANS], pick, preferred_element_type=F32).astype(BF)

    put_rows(0, band_row)
    for copy in fetch:
        copy.wait()
    for t in range(TRANS):
        freq, mom = shift_ref[t, 0] >> 4, shift_ref[t, 0] & 15

        def moved(i, freq=freq, mom=mom):
            return ((((i >> 4) + freq) & 15) << 4) + (((i & 15) + mom) & 15)

        put_rows(1 + t, moved(band_row))
        put_cols(t, moved(lane))
        freq, mom = flip_ref[t, 0] >> 4, flip_ref[t, 0] & 15

        def turned(i, freq=freq, mom=mom):
            return (((freq - (i >> 4)) & 15) << 4) + ((mom - (i & 15)) & 15)

        put_rows(1 + TRANS + t, turned(band_row))
        put_cols(TRANS + t, turned(lane))


def tables(place, shift, flip):
    return pl.pallas_call(
        table_kernel,
        out_shape=(
            jax.ShapeDtypeStruct((2 * TRANS + 1, 2 * ORDER, ORDER), BF),
            jax.ShapeDtypeStruct((2, (2 * TRANS + 1) * 2 * BAND, ORDER), BF),
        ),
        in_specs=[
            pl.BlockSpec(memory_space=pltpu.SMEM),
            pl.BlockSpec(memory_space=pltpu.HBM),
            pl.BlockSpec(memory_space=pltpu.HBM),
        ],
        out_specs=(pl.BlockSpec(memory_space=pltpu.VMEM),) * 2,
        scratch_shapes=[
            pltpu.SMEM((TRANS, ORDER), jnp.int32),
            pltpu.SMEM((TRANS, ORDER), jnp.int32),
            pltpu.SemaphoreType.DMA((2,)),
        ],
        cost_estimate=pl.CostEstimate(flops=4 * 10**9, bytes_accessed=1, transcendentals=0),
        compiler_params=pltpu.CompilerParams(vmem_limit_bytes=12 * MIB),
        name="tables",
    )(place, shift, flip)


def paired(re, im):
    return jnp.concatenate(
        [jnp.concatenate([re, im], 1), jnp.concatenate([im, -re], 1)], 0
    )


def halves(ref, begin):
    return paired(ref[begin : begin + BAND], ref[begin + BAND : begin + 2 * BAND])


def one_walker(up, down, cols, rows, first_up, first_down, plain, ready, put):
    step = 2 * BAND
    first_up[...] = jnp.dot(rows[: step * (TRANS + 1)], up, preferred_element_type=F32).astype(BF)
    first_down[...] = jnp.dot(rows[step:], down, preferred_element_type=F32).astype(BF)
    across = (((1,), (1,)), ((), ()))
    turned_up = lax.dot_general(rows[:step], up, across, preferred_element_type=F32).astype(BF)
    turned_down = lax.dot_general(rows[:step], down, across, preferred_element_type=F32).astype(BF)
    left = jnp.concatenate(
        [halves(turned_up, 0), halves(turned_down, 0), halves(first_up, 0)], 0
    )
    plain[...] = jnp.dot(left, cols[2 * TRANS], preferred_element_type=F32)
    ready()
    for t in range(TRANS):
        left = jnp.concatenate([halves(first_up, step * (1 + t)), halves(first_down, step * t)], 0)
        moved = jnp.dot(left, cols[t], preferred_element_type=F32)
        real, imag = 0.0, 0.0
        for s in range(2):
            nr, ni = plain[step * s : step * s + BAND], plain[step * s + BAND : step * (s + 1)]
            mr, mi = moved[step * s : step * s + BAND], moved[step * s + BAND : step * (s + 1)]
            real = real + (nr * mr + ni * mi)
            imag = imag + (nr * mi - ni * mr)
        put(0, 0, t, real)
        put(0, 1, t, imag)
        low = jnp.dot(
            halves(first_down, step * (TRANS + t)), cols[TRANS + t], preferred_element_type=F32
        )
        nr, ni = plain[2 * step : 2 * step + BAND], plain[2 * step + BAND : 3 * step]
        put(1, 0, t, nr * low[:BAND] - ni * low[BAND:])
        put(1, 1, t, nr * low[BAND:] + ni * low[:BAND])


WORK = [
    pltpu.VMEM((2 * BAND * (TRANS + 1), ORDER), BF),
    pltpu.VMEM((2 * BAND * 2 * TRANS, ORDER), BF),
    pltpu.VMEM((6 * BAND, ORDER), F32),
]
SUMS = (2, TRANS, BAND, ORDER)
PIECE = (2, ORDER, ORDER)
IN_VMEM = pl.BlockSpec(memory_space=pltpu.VMEM)
IN_SMEM = pl.BlockSpec(memory_space=pltpu.SMEM)
ANYWHERE = pl.BlockSpec(memory_space=pl.ANY)
IN_HBM = pl.BlockSpec(memory_space=pltpu.HBM)
BIG = pltpu.CompilerParams(vmem_limit_bytes=16 * MIB)


def open_kernel(piece, cols, rows, ph_in, pp_in, sums, first_up, first_down, plain, sems):
    loads = [
        pltpu.make_async_copy(source.at[part], sums.at[i, part], sems.at[i, part])
        for i, source in enumerate((ph_in, pp_in))
        for part in range(2)
    ]
    for load in loads:
        load.start()

    def ready():
        for load in loads:
            load.wait()

    def put(which, part, t, term):
        sums[which, part, t] += term

    one_walker(piece[0], piece[1], cols, rows.at[0], first_up, first_down, plain, ready, put)


def open_sums(piece, cols, rows, ph, pp):
    return pl.pallas_call(
        open_kernel,
        out_shape=jax.ShapeDtypeStruct((2, *SUMS), F32),
        in_specs=[IN_VMEM] * 3 + [IN_HBM] * 2,
        out_specs=IN_VMEM,
        scratch_shapes=WORK + [pltpu.SemaphoreType.DMA((2, 2))],
        cost_estimate=TINY,
        compiler_params=BIG,
        name="open_sums",
    )(piece, cols, rows, ph, pp)


def fetch_lane(core, pair, hold, sem):
    for c in range(2):

        @pl.when(core == c)
        def _(c=c):
            pltpu.make_async_copy(pair[c], hold, sem).start()


def spread_kernel(count, fresh, send, place, *refs):
    pairs = [refs[2 * i : 2 * i + 2] for i in range(count)]
    cols, rows, before = refs[2 * count : 2 * count + 3]
    after = refs[2 * count + 3 : 2 * count + 4 + send]
    first_up, first_down, plain, hold, sems, *held = refs[2 * count + 4 + send :]
    core = place[0] & 1
    for n, pair in enumerate(pairs):
        fetch_lane(core, pair, hold.at[n], sems.at[n])
    for n, pair in enumerate(pairs):
        pltpu.make_async_copy(pair[0], hold.at[n], sems.at[n]).wait()
        for b in range(2):

            def put(which, part, t, term, n=n, b=b):
                if n == 0:
                    if not (fresh and b):
                        term = term + before[2 * b + which, part, t]
                elif send and b:
                    term = term + held[0][which, part, t]
                else:
                    term = term + after[0][2 * b + which, part, t]
                if not (send and b):
                    after[0][2 * b + which, part, t] = term
                elif n < count - 1:
                    held[0][which, part, t] = term
                else:
                    after[1][which, part, t] = term.astype(BF)

            one_walker(
                hold[n, 0], hold[n, 1], cols, rows.at[b], first_up, first_down, plain,
                lambda: None, put,
            )


def spread(place, pairs, cols, rows, sums, send=False):
    count, fresh = len(pairs), sums.shape[0] == 2
    out_shape = [jax.ShapeDtypeStruct((2 if send else 4, *SUMS), F32)]
    if send:
        out_shape.append(jax.ShapeDtypeStruct((2, *SUMS), BF))
    return pl.pallas_call(
        functools.partial(spread_kernel, count, fresh, send),
        out_shape=tuple(out_shape),
        in_specs=[IN_SMEM] + [ANYWHERE] * (2 * count) + [IN_VMEM] * 3,
        out_specs=(IN_VMEM,) * len(out_shape),
        scratch_shapes=WORK
        + [pltpu.VMEM((count, *PIECE), BF), pltpu.SemaphoreType.DMA((count,))]
        + [pltpu.VMEM((2, *SUMS), F32)] * send,
        cost_estimate=TINY,
        compiler_params=BIG,
        name="spread",
    )(place, *[piece for pair in pairs for piece in pair], cols, rows, sums)


def add_kernel(place, lane0, lane1, cols, rows, before, after, first_up, first_down, plain, hold, sem):
    fetch_lane(place[0] & 1, (lane0, lane1), hold, sem.at[0])
    pltpu.make_async_copy(lane0, hold, sem.at[0]).wait()

    def put(which, part, t, term):
        after[which, part, t] = before[which, part, t] + term

    one_walker(
        hold[0], hold[1], cols, rows.at[0], first_up, first_down, plain, lambda: None, put
    )


def add(place, pair, cols, rows, sums):
    return pl.pallas_call(
        add_kernel,
        out_shape=jax.ShapeDtypeStruct((2, *SUMS), F32),
        in_specs=[IN_SMEM] + [ANYWHERE] * 2 + [IN_VMEM] * 3,
        out_specs=IN_VMEM,
        scratch_shapes=WORK + [pltpu.VMEM(PIECE, BF), pltpu.SemaphoreType.DMA((1,))],
        cost_estimate=TINY,
        compiler_params=BIG,
        name="add",
    )(place, *pair, cols, rows, sums)


def close_kernel(
    place, lane0, lane1, cols, rows, sums, others, ph, pp,
    first_up, first_down, plain, hold, sem, total, sems,
):
    fetch_lane(place[0] & 1, (lane0, lane1), hold, sem.at[0])
    pltpu.make_async_copy(lane0, hold, sem.at[0]).wait()
    stores = []

    def put(which, part, t, term):
        other = others[which, part, t].astype(F32)
        total[which, part, t] = sums[which, part, t] + other + term
        store = pltpu.make_async_copy(
            total.at[which, part, t], (ph, pp)[which].at[part, t], sems.at[which, part, t]
        )
        store.start()
        stores.append(store)

    one_walker(
        hold[0], hold[1], cols, rows.at[0], first_up, first_down, plain, lambda: None, put
    )
    for store in stores:
        store.wait()


def close_sums(place, pair, cols, rows, sums, others):
    return pl.pallas_call(
        close_kernel,
        out_shape=(jax.ShapeDtypeStruct(SUMS, F32),) * 2,
        in_specs=[IN_SMEM] + [ANYWHERE] * 2 + [IN_VMEM] * 4,
        out_specs=(ANYWHERE,) * 2,
        scratch_shapes=WORK
        + [pltpu.VMEM(PIECE, BF), pltpu.SemaphoreType.DMA((1,))]
        + [pltpu.VMEM((2, *SUMS), F32), pltpu.SemaphoreType.DMA((2, 2, TRANS))],
        cost_estimate=TINY,
        compiler_params=BIG,
        name="close_sums",
    )(place, *pair, cols, rows, sums, others)


def scale_kernel(masses, spins, out, raw, done, in_sems, out_sems):
    half = ORDER // 2
    parts = [(spin, pl.ds(begin, half)) for spin in range(2) for begin in (0, half)]
    loads = [
        pltpu.make_async_copy(masses.at[0, spin, rows], raw.at[spin, rows], in_sems.at[i])
        for i, (spin, rows) in enumerate(parts)
    ]
    stores = [
        pltpu.make_async_copy(done.at[spin, rows], out.at[spin, rows], out_sems.at[i])
        for i, (spin, rows) in enumerate(parts)
    ]
    for load in loads:
        load.start()
    signed = (2 * spins[...] - 1).astype(F32)
    factors = jnp.exp(COUPLING * signed), jnp.exp(-COUPLING * signed)
    for (spin, rows), load, store in zip(parts, loads, stores):
        load.wait()
        done[spin, rows] = (raw[spin, rows].astype(F32) * factors[spin]).astype(BF)
        store.start()
    for store in stores:
        store.wait()


def scale(masses, spins):
    return pl.pallas_call(
        scale_kernel,
        out_shape=jax.ShapeDtypeStruct((2, ORDER, ORDER), BF),
        in_specs=[ANYWHERE, IN_VMEM],
        out_specs=ANYWHERE,
        scratch_shapes=[pltpu.VMEM((2, ORDER, ORDER), BF)] * 2
        + [pltpu.SemaphoreType.DMA((4,))] * 2,
        cost_estimate=TINY,
        compiler_params=pltpu.CompilerParams(vmem_limit_bytes=56 * MIB),
        name="scale",
    )(masses, spins)


def route_kernel(steps, y_ref, own, got, after, *refs):
    outs, sems = refs[: len(steps)], refs[len(steps)]
    for i, step in enumerate(steps):
        wraps = y_ref[0] + step >= PLANE

        @pl.when(wraps)
        def _(i=i):
            pltpu.make_async_copy(got, outs[i], sems.at[i]).start()

        @pl.when(jnp.logical_not(wraps))
        def _(i=i):
            pltpu.make_async_copy(own, outs[i], sems.at[i]).start()

    for i in range(len(steps)):
        pltpu.make_async_copy(own, outs[i], sems.at[i]).wait()


def route(y, own, got, after, steps):
    return pl.pallas_call(
        functools.partial(route_kernel, steps),
        out_shape=(jax.ShapeDtypeStruct(own.shape, BF),) * len(steps),
        in_specs=[IN_SMEM] + [ANYWHERE] * 2 + [IN_VMEM],
        out_specs=(ANYWHERE,) * len(steps),
        scratch_shapes=[pltpu.SemaphoreType.DMA((len(steps),))],
        cost_estimate=TINY,
        compiler_params=pltpu.CompilerParams(vmem_limit_bytes=MIB),
        name="route",
    )(y, own, got, after)


PLANE = 4
BLOCKS = 64


def move(value, pairs):
    flat = [(a * BLOCKS + b, c * BLOCKS + d) for (a, b), (c, d) in pairs]
    return lax.ppermute(value, ("grp", "blk"), flat)


def next_plane(value, core):
    return move(
        value,
        [((g, b), (g + core, (b + PLANE) % BLOCKS)) for g in (0, 2) for b in range(BLOCKS)],
    )


def along_y(value, steps, core):
    return move(
        value,
        [
            ((g + core, b), (g + core, b // PLANE * PLANE + (b + steps) % PLANE))
            for g in (0, 2)
            for b in range(BLOCKS)
        ],
    )


def other_core(value, cores=(0, 1)):
    return lax.ppermute(value, "grp", [(s, s ^ 1) for s in range(4) if s % 2 in cores])


def on_device(masses, spins, shift_table, flip_table, ph_in, pp_in):
    place = lax.axis_index("grp").reshape(1).astype(jnp.int32)
    y = (lax.axis_index("blk") % PLANE).reshape(1).astype(jnp.int32)
    own = scale(masses, spins)
    near = next_plane(own, 0)
    cols, rows = tables(place, shift_table, flip_table)
    near, cols = lax.optimization_barrier((near, cols))
    far = next_plane(near, 1)
    right0, left0 = along_y(near, 1, 0), along_y(near, 3, 0)
    sums = open_sums(own, cols, rows, ph_in, pp_in)
    far, sums = lax.optimization_barrier((far, sums))
    right, left, middle = route(y, own, far, sums, (1, 3, 2))
    middle0 = along_y(near, 2, 0)
    right1, left1 = along_y(right, 1, 1), along_y(left, 3, 1)
    (sums,) = spread(place, [(near, far)], cols, rows, sums)
    middle, sums = lax.optimization_barrier((middle, sums))
    middle1 = along_y(middle, 2, 1)
    right0, left0, right1, left1, sums = lax.optimization_barrier(
        (right0, left0, right1, left1, sums)
    )
    sums, sent = spread(place, [(right0, right1), (left0, left1)], cols, rows, sums, True)
    others = other_core(sent)
    middle0, middle1, sums = lax.optimization_barrier((middle0, middle1, sums))
    swapped = other_core(middle1, (1,)), other_core(middle0, (0,))
    sums = add(place, (middle0, middle1), cols, rows, sums)
    return close_sums(place, swapped, cols, rows, sums, others)


def solution(mesh):
    placed = (
        P("blk", None, None, None),
        P("blk", None),
        P("blk", None),
        P("blk", None),
        P(None, "blk", "grp", None),
        P(None, "blk", "grp", None),
    )
    return jax.shard_map(
        on_device,
        mesh=mesh,
        in_specs=placed,
        out_specs=(P(None, "blk", "grp", None), P(None, "blk", "grp", None)),
        check_vma=False,
    )
```

time: 48.1 us -> 55 us (1.14)
  starting transfers between devices: 8.74 us -> 20.6 us
  blocking collectives: 11.8 us -> 0 us
  waiting for transfers between devices: 3.97 us -> 11 us
  local copies, waits for them, and re-layouts: 5.05 us -> 4.4 us
    ppermute x5 -> x11, starting transfers between devices: 8.74 us -> 20.6 us  [the longest x8 15.8 us: move(): return lax.ppermute(value, ('grp', 'blk'), flat)]
    all_gather x2 -> x0, blocking collectives: 11.8 us -> none  [both_cores(): lax.all_gather(value, 'grp', axis=0, axis_index_groups=[[0, 1], [2, 3]])]
    ppermute x5 -> x11, waiting for transfers between devices: 3.97 us -> 11 us  [the longest x8 10.1 us: move(): return lax.ppermute(value, ('grp', 'blk'), flat)]
    unnamed x18 -> x10, local copies, waits for them, and re-layouts: 5.05 us -> 4.4 us
    pallas_call x7 -> x6, Pallas kernels: 11.7 us -> 11.9 us  [the longest x2 6.87 us: spread(): pl.pallas_call(functools.partial(spread_kernel, count, fresh, send), out_...]
  transfers between devices with their start and end apart: 5 -> 11, of which waited for: 3 -> 2; matrix products, arithmetic and copies ran while one was open for 0% -> 0% of each run, Pallas kernels for 26% -> 24%
where the time goes in v4:
time: 55 us; the launch traced here: 54.4 us
  starting transfers between devices  20.6 us (37%)
  Pallas kernels  17.5 us (32%)
  waiting for transfers between devices  11 us (20%)
  local copies, waits for them, and re-layouts  4.4 us (8%)
  between operations  0.83 us (2%)
    ppermute x8, starting transfers between devices, move(): return lax.ppermute(value, ('grp', 'blk'), flat)  15.8 us
    ppermute x8, waiting for transfers between devices, move(): return lax.ppermute(value, ('grp', 'blk'), flat)  10.1 us
    pallas_call x2, Pallas kernels, spread(): pl.pallas_call(functools.partial(spread_kernel, count, fresh, send), out_...  6.87 us
    ppermute x3, starting transfers between devices, other_core(): lax.ppermute(value, 'grp', [(s, s ^ 1) for s in range(4) if s % 2 in cores])  4.78 us
    unnamed x10, local copies, waits for them, and re-layouts  4.4 us
    pallas_call x1, Pallas kernels, tables(): pl.pallas_call(table_kernel, out_shape=(jax.ShapeDtypeStruct((2 * TRANS +...  3.61 us
    pallas_call x1, Pallas kernels, scale(): pl.pallas_call(scale_kernel, out_shape=jax.ShapeDtypeStruct((2, ORDER, OR...  2.32 us
    pallas_call x1, Pallas kernels, close_sums(): pl.pallas_call(close_kernel, out_shape=(jax.ShapeDtypeStruct(SUMS, F32),)...  2.01 us
  transfers between devices with their start and end apart: 11, of which 2 were waited for; matrix products, arithmetic and copies ran while one was open for 0% of the time, Pallas kernels for 24%

profile of v4, /device:TPU:1, one launch (start us, length us, event | category | flops | bytes accessed | tf_op | source)
XLA Modules:
  0.0 54.4 jit_solution(11269593125498625136)
XLA Ops:
  0.6 2.3 %scale.1.piece.own = bf16[2,256,256]{2,1,0:T(8,128)(2,1)} custom-call(bf16[1,2,256,256]{3,2,1,0:T(8,128)(2,1)} %masses.1, s32[1,256]{1,0:T(1,128)} %spins.1), custom_call_target="tpu_custom_call" | custom-call | flops 1 | bytes 1 | tf_op jit(solution)/shard_map/scale/pallas_call | solution.py:341
  3.0 1.4 %collective-permute-start = (bf16[2,256,256]{2,1,0:T(8,128)(2,1)}, bf16[2,256,256]{2,1,0:T(8,128)(2,1)}, u32[]{:S(2)}, u32[]{:S(2)}) collective-permute-start(bf16[2,256,256]{2,1,0:T(8,128)(2,1)} %scale.1.piece.own), channel_id=1, source_target_pairs={{0,4},{1,5},{2,6},{3,7},{4,8},{5,9},{6,10},{7,11},{8,12},{9,13},{1... | collective-permute-start | bytes 786440 | tf_op jit(solution)/shard_map/ppermute | solution.py:390
  4.3 0.0 copy-start.3
  4.3 0.7 %copy-done.3 = s32[4,256]{1,0:T(4,128)S(1)} copy-done((s32[4,256]{1,0:T(4,128)S(1)}, s32[4,256]{1,0:T(4,128)}, u32[]{:S(2)}) %copy-start.3) | copy-done | bytes 4120
  5.0 0.0 copy-start.4
  5.0 0.7 %copy-done.4 = s32[4,256]{1,0:T(4,128)S(1)} copy-done((s32[4,256]{1,0:T(4,128)S(1)}, s32[4,256]{1,0:T(4,128)}, u32[]{:S(2)}) %copy-start.4) | copy-done | bytes 4120
  5.7 3.6 %tables.1 = (bf16[9,512,256]{2,1,0:T(8,128)(2,1)S(1)}, bf16[2,1152,256]{2,1,0:T(8,128)(2,1)S(1)}) custom-call(s32[1]{0:T(128)} %bitcast.place_ref.place, s32[4,256]{1,0:T(4,128)S(1)} %copy-done.3, s32[4,256]{1,0:T(4,128)S(1)} %copy-done.4), custom_call_target="tpu_custom_call" | custom-call | flops 4000000000 | bytes 1 | tf_op jit(solution)/shard_map/tables/pallas_call | solution.py:83
  9.3 0.0 collective-permute-done.refs_0_
  9.3 1.3 %collective-permute-start.2 = (bf16[2,256,256]{2,1,0:T(8,128)(2,1)}, bf16[2,256,256]{2,1,0:T(8,128)(2,1)}, u32[]{:S(2)}, u32[]{:S(2)}) collective-permute-start(bf16[2,256,256]{2,1,0:T(8,128)(2,1)} %collective-permute-done.refs_0_), channel_id=1, source_target_pairs={{0,68},{1,69},{2,70},{3,71},{4,72},{5,73},{6,74},{7,75},{8,76},{9,... | collective-permute-start | bytes 786440 | tf_op jit(solution)/shard_map/ppermute | solution.py:390
  10.7 0.7 %collective-permute-start.5 = (bf16[2,256,256]{2,1,0:T(8,128)(2,1)}, bf16[2,256,256]{2,1,0:T(8,128)(2,1)S(1)}, u32[]{:S(2)}, u32[]{:S(2)}) collective-permute-start(bf16[2,256,256]{2,1,0:T(8,128)(2,1)} %collective-permute-done.refs_0_), channel_id=1, source_target_pairs={{0,3},{1,0},{2,1},{3,2},{4,7},{5,4},{6,5},{7,6},{8,11},{9,8},{10,9... | collective-permute-start | bytes 786440 | tf_op jit(solution)/shard_map/ppermute | solution.py:390
  11.3 0.7 %collective-permute-start.4 = (bf16[2,256,256]{2,1,0:T(8,128)(2,1)}, bf16[2,256,256]{2,1,0:T(8,128)(2,1)S(1)}, u32[]{:S(2)}, u32[]{:S(2)}) collective-permute-start(bf16[2,256,256]{2,1,0:T(8,128)(2,1)} %collective-permute-done.refs_0_), channel_id=1, source_target_pairs={{0,1},{1,2},{2,3},{3,0},{4,5},{5,6},{6,7},{7,4},{8,9},{9,10},{10,1... | collective-permute-start | bytes 786440 | tf_op jit(solution)/shard_map/ppermute | solution.py:390
  12.0 0.0 copy-start
  12.0 0.9 %copy-done = bf16[2,256,256]{2,1,0:T(8,128)(2,1)S(1)} copy-done((bf16[2,256,256]{2,1,0:T(8,128)(2,1)S(1)}, bf16[2,256,256]{2,1,0:T(8,128)(2,1)}, u32[]{:S(2)}) %copy-start) | copy-done | bytes 262168
  13.0 0.0 copy-start.1
  13.0 1.0 %copy-done.1 = f32[2,4,64,256]{3,2,1,0:T(8,128)S(1)} copy-done((f32[2,4,64,256]{3,2,1,0:T(8,128)S(1)}, f32[2,4,64,256]{3,2,1,0:T(8,128)}, u32[]{:S(2)}) %copy-start.1) | copy-done | bytes 524312
  14.0 0.0 copy-start.2
  14.0 1.0 %copy-done.2 = f32[2,4,64,256]{3,2,1,0:T(8,128)S(1)} copy-done((f32[2,4,64,256]{3,2,1,0:T(8,128)S(1)}, f32[2,4,64,256]{3,2,1,0:T(8,128)}, u32[]{:S(2)}) %copy-start.2) | copy-done | bytes 524312
  15.1 1.5 %open_sums.1.after.refs_4_ = f32[2,2,4,64,256]{4,3,2,1,0:T(8,128)S(1)} custom-call(bf16[2,256,256]{2,1,0:T(8,128)(2,1)S(1)} %copy-done, bf16[9,512,256]{2,1,0:T(8,128)(2,1)S(1)} %get-tuple-element.25.cols.refs_2_.refs_4_, bf16[2,1152,256]{2,1,0:T(8,128)(2,1)S(1)} %get-tuple-element.26.rows.refs_3_.refs_5_, f32[2,4,64,256]{3,2,1,0:T(8,128)S(1)} %copy-done.1, ...), custom_call_target="tpu_custom_call" | custom-call | flops 1 | bytes 1 | tf_op jit(solution)/shard_map/open_sums/pallas_call | solution.py:181
  16.5 10.1 %collective-permute-done.2.got.refs_1_ = bf16[2,256,256]{2,1,0:T(8,128)(2,1)} collective-permute-done((bf16[2,256,256]{2,1,0:T(8,128)(2,1)}, bf16[2,256,256]{2,1,0:T(8,128)(2,1)}, u32[]{:S(2)}, u32[]{:S(2)}) %collective-permute-start.2) | collective-permute-done | bytes 262176 | tf_op jit(solution)/shard_map/ppermute | solution.py:390
  26.6 0.1 route.1
  26.7 4.1 %collective-permute-start.6 = (bf16[2,256,256]{2,1,0:T(8,128)(2,1)S(1)}, bf16[2,256,256]{2,1,0:T(8,128)(2,1)S(1)}, u32[]{:S(2)}, u32[]{:S(2)}) collective-permute-start(bf16[2,256,256]{2,1,0:T(8,128)(2,1)S(1)} %get-tuple-element.31), channel_id=1, source_target_pairs={{64,65},{65,66},{66,67},{67,64},{68,69},{69,70},{70,71},{71,68},{7... | collective-permute-start | bytes 786440 | tf_op jit(solution)/shard_map/ppermute | solution.py:390
  30.8 3.6 %collective-permute-start.7 = (bf16[2,256,256]{2,1,0:T(8,128)(2,1)S(1)}, bf16[2,256,256]{2,1,0:T(8,128)(2,1)S(1)}, u32[]{:S(2)}, u32[]{:S(2)}) collective-permute-start(bf16[2,256,256]{2,1,0:T(8,128)(2,1)S(1)} %get-tuple-element.32), channel_id=1, source_target_pairs={{64,67},{65,64},{66,65},{67,66},{68,71},{69,68},{70,69},{71,70},{7... | collective-permute-start | bytes 786440 | tf_op jit(solution)/shard_map/ppermute | solution.py:390
  34.4 0.7 %collective-permute-start.1 = (bf16[2,256,256]{2,1,0:T(8,128)(2,1)}, bf16[2,256,256]{2,1,0:T(8,128)(2,1)S(1)}, u32[]{:S(2)}, u32[]{:S(2)}) collective-permute-start(bf16[2,256,256]{2,1,0:T(8,128)(2,1)} %collective-permute-done.refs_0_), channel_id=1, source_target_pairs={{0,2},{1,3},{2,0},{3,1},{4,6},{5,7},{6,4},{7,5},{8,10},{9,11},{10,... | collective-permute-start | bytes 786440 | tf_op jit(solution)/shard_map/ppermute | solution.py:390
  35.1 2.9 %spread.2.refs_6_ = f32[4,2,4,64,256]{4,3,2,1,0:T(8,128)S(1)} custom-call(s32[1]{0:T(128)} %bitcast.place_ref.place, bf16[2,256,256]{2,1,0:T(8,128)(2,1)} %collective-permute-done.refs_0_, bf16[2,256,256]{2,1,0:T(8,128)(2,1)} %collective-permute-done.2.got.refs_1_, bf16[9,512,256]{2,1,0:T(8,128)(2,1)S(1)} %get-tuple-element.25.cols.refs_2_.refs_4_, ...), custom_call_target="tpu_custom_call" | custom-call | flops 1 | bytes 1 | tf_op jit(solution)/shard_map/spread/pallas_call | solution.py:239
  38.0 0.0 collective-permute-done.5.refs_2_
  38.0 3.4 %collective-permute-start.3 = (bf16[2,256,256]{2,1,0:T(8,128)(2,1)S(1)}, bf16[2,256,256]{2,1,0:T(8,128)(2,1)S(1)}, u32[]{:S(2)}, u32[]{:S(2)}) collective-permute-start(bf16[2,256,256]{2,1,0:T(8,128)(2,1)S(1)} %get-tuple-element.30), channel_id=1, source_target_pairs={{64,66},{65,67},{66,64},{67,65},{68,70},{69,71},{70,68},{71,69},{7... | collective-permute-start | bytes 786440 | tf_op jit(solution)/shard_map/ppermute | solution.py:390
  41.4 0.0 collective-permute-done.4.refs_0_
  41.4 0.0 collective-permute-done.6.refs_1_
  41.4 0.0 collective-permute-done.7.refs_3_
  41.4 4.0 %spread.3 = (f32[2,2,4,64,256]{4,3,2,1,0:T(8,128)S(1)}, bf16[2,2,4,64,256]{4,3,2,1,0:T(8,128)(2,1)S(1)}) custom-call(s32[1]{0:T(128)} %bitcast.place_ref.place, bf16[2,256,256]{2,1,0:T(8,128)(2,1)S(1)} %collective-permute-done.4.refs_0_, bf16[2,256,256]{2,1,0:T(8,128)(2,1)S(1)} %collective-permute-done.6.refs_1_, ...), custom_call_target="tpu_custom_call" | custom-call | flops 1 | bytes 1 | tf_op jit(solution)/shard_map/spread/pallas_call | solution.py:239
  45.4 1.5 %collective-permute-start.10 = (bf16[2,2,4,64,256]{4,3,2,1,0:T(8,128)(2,1)S(1)}, bf16[2,2,4,64,256]{4,3,2,1,0:T(8,128)(2,1)S(1)}, u32[]{:S(2)}, u32[]{:S(2)}) collective-permute-start(bf16[2,2,4,64,256]{4,3,2,1,0:T(8,128)(2,1)S(1)} %get-tuple-element.43), channel_id=1, source_target_pairs={{0,64},{64,0},{128,192},{192,128},{1,65},{65,1},{129,193},{193,129... | collective-permute-start | bytes 1572872 | tf_op jit(solution)/shard_map/ppermute | solution.py:412
  47.0 0.0 collective-permute-done.1.lane0
  47.0 0.0 collective-permute-done.3.lane1
  47.0 1.9 %collective-permute-start.8 = (bf16[2,256,256]{2,1,0:T(8,128)(2,1)S(1)}, bf16[2,256,256]{2,1,0:T(8,128)(2,1)S(1)}, u32[]{:S(2)}, u32[]{:S(2)}) collective-permute-start(bf16[2,256,256]{2,1,0:T(8,128)(2,1)S(1)} %collective-permute-done.3.lane1), channel_id=1, source_target_pairs={{64,0},{192,128},{65,1},{193,129},{66,2},{194,130},{67,3},{195,131... | collective-permute-start | bytes 786440 | tf_op jit(solution)/shard_map/ppermute | solution.py:412
  48.9 1.3 %collective-permute-start.9 = (bf16[2,256,256]{2,1,0:T(8,128)(2,1)S(1)}, bf16[2,256,256]{2,1,0:T(8,128)(2,1)S(1)}, u32[]{:S(2)}, u32[]{:S(2)}) collective-permute-start(bf16[2,256,256]{2,1,0:T(8,128)(2,1)S(1)} %collective-permute-done.1.lane0), channel_id=1, source_target_pairs={{0,64},{128,192},{1,65},{129,193},{2,66},{130,194},{3,67},{131,195... | collective-permute-start | bytes 786440 | tf_op jit(solution)/shard_map/ppermute | solution.py:412
  50.2 1.2 %add.6.sums = f32[2,2,4,64,256]{4,3,2,1,0:T(8,128)S(1)} custom-call(s32[1]{0:T(128)} %bitcast.place_ref.place, bf16[2,256,256]{2,1,0:T(8,128)(2,1)S(1)} %collective-permute-done.1.lane0, bf16[2,256,256]{2,1,0:T(8,128)(2,1)S(1)} %collective-permute-done.3.lane1, bf16[9,512,256]{2,1,0:T(8,128)(2,1)S(1)} %get-tuple-element.25.cols.refs_2_.refs_4_, ...), custom_call_target="tpu_custom_call" | custom-call | flops 1 | bytes 1 | tf_op jit(solution)/shard_map/add/pallas_call | solution.py:266
  51.4 0.0 collective-permute-done.8.lane0
  51.4 0.9 %collective-permute-done.9.lane1 = bf16[2,256,256]{2,1,0:T(8,128)(2,1)S(1)} collective-permute-done((bf16[2,256,256]{2,1,0:T(8,128)(2,1)S(1)}, bf16[2,256,256]{2,1,0:T(8,128)(2,1)S(1)}, u32[]{:S(2)}, u32[]{:S(2)}) %collective-permute-start.9) | collective-permute-done | bytes 262176 | tf_op jit(solution)/shard_map/ppermute | solution.py:412
  52.4 0.0 collective-permute-done.10.others
  52.4 2.0 %close_sums.1 = (f32[2,4,64,256]{3,2,1,0:T(8,128)}, f32[2,4,64,256]{3,2,1,0:T(8,128)}) custom-call(s32[1]{0:T(128)} %bitcast.place_ref.place, bf16[2,256,256]{2,1,0:T(8,128)(2,1)S(1)} %collective-permute-done.8.lane0, bf16[2,256,256]{2,1,0:T(8,128)(2,1)S(1)} %collective-permute-done.9.lane1, bf16[9,512,256]{2,1,0:T(8,128)(2,1)S(1)} %get-tuple-element.25.cols.refs_2_.refs_4_, ...), custom_call_target="tpu_custom_call" | custom-call | flops 1 | bytes 1 | tf_op jit(solution)/shard_map/close_sums/pallas_call | solution.py:303
Async XLA Ops:
  3.0 6.4 %collective-permute-start = (bf16[2,256,256]{2,1,0:T(8,128)(2,1)}, bf16[2,256,256]{2,1,0:T(8,128)(2,1)}, u32[]{:S(2)}, u32[]{:S(2)}) collective-permute-start(bf16[2,256,256]{2,1,0:T(8,128)(2,1)} %scale.1.piece.own), channel_id=1, source_target_pairs={{0,4},{1,5},{2,6},{3,7},{4,8},{5,9},{6,10},{7,11},{8,12},{9,13},{1... | collective-permute-start | bytes 786440 | tf_op jit(solution)/shard_map/ppermute | solution.py:390
  4.3 0.7 %copy-start.3 = (s32[4,256]{1,0:T(4,128)S(1)}, s32[4,256]{1,0:T(4,128)}, u32[]{:S(2)}) copy-start(s32[4,256]{1,0:T(4,128)} %shift_in.1) | copy-start | bytes 12292
  5.0 0.7 %copy-start.4 = (s32[4,256]{1,0:T(4,128)S(1)}, s32[4,256]{1,0:T(4,128)}, u32[]{:S(2)}) copy-start(s32[4,256]{1,0:T(4,128)} %flip_in.1) | copy-start | bytes 12292
  9.3 17.3 %collective-permute-start.2 = (bf16[2,256,256]{2,1,0:T(8,128)(2,1)}, bf16[2,256,256]{2,1,0:T(8,128)(2,1)}, u32[]{:S(2)}, u32[]{:S(2)}) collective-permute-start(bf16[2,256,256]{2,1,0:T(8,128)(2,1)} %collective-permute-done.refs_0_), channel_id=1, source_target_pairs={{0,68},{1,69},{2,70},{3,71},{4,72},{5,73},{6,74},{7,75},{8,76},{9,... | collective-permute-start | bytes 786440 | tf_op jit(solution)/shard_map/ppermute | solution.py:390
  10.7 27.3 %collective-permute-start.5 = (bf16[2,256,256]{2,1,0:T(8,128)(2,1)}, bf16[2,256,256]{2,1,0:T(8,128)(2,1)S(1)}, u32[]{:S(2)}, u32[]{:S(2)}) collective-permute-start(bf16[2,256,256]{2,1,0:T(8,128)(2,1)} %collective-permute-done.refs_0_), channel_id=1, source_target_pairs={{0,3},{1,0},{2,1},{3,2},{4,7},{5,4},{6,5},{7,6},{8,11},{9,8},{10,9... | collective-permute-start | bytes 786440 | tf_op jit(solution)/shard_map/ppermute | solution.py:390
  11.3 30.1 %collective-permute-start.4 = (bf16[2,256,256]{2,1,0:T(8,128)(2,1)}, bf16[2,256,256]{2,1,0:T(8,128)(2,1)S(1)}, u32[]{:S(2)}, u32[]{:S(2)}) collective-permute-start(bf16[2,256,256]{2,1,0:T(8,128)(2,1)} %collective-permute-done.refs_0_), channel_id=1, source_target_pairs={{0,1},{1,2},{2,3},{3,0},{4,5},{5,6},{6,7},{7,4},{8,9},{9,10},{10,1... | collective-permute-start | bytes 786440 | tf_op jit(solution)/shard_map/ppermute | solution.py:390
  12.0 1.0 %copy-start = (bf16[2,256,256]{2,1,0:T(8,128)(2,1)S(1)}, bf16[2,256,256]{2,1,0:T(8,128)(2,1)}, u32[]{:S(2)}) copy-start(bf16[2,256,256]{2,1,0:T(8,128)(2,1)} %scale.1.piece.own) | copy-start | bytes 786436
  13.0 1.0 %copy-start.1 = (f32[2,4,64,256]{3,2,1,0:T(8,128)S(1)}, f32[2,4,64,256]{3,2,1,0:T(8,128)}, u32[]{:S(2)}) copy-start(f32[2,4,64,256]{3,2,1,0:T(8,128)} %ph_in.1) | copy-start | bytes 1572868
  14.0 1.0 %copy-start.2 = (f32[2,4,64,256]{3,2,1,0:T(8,128)S(1)}, f32[2,4,64,256]{3,2,1,0:T(8,128)}, u32[]{:S(2)}) copy-start(f32[2,4,64,256]{3,2,1,0:T(8,128)} %pp_in.1) | copy-start | bytes 1572868
  26.7 14.7 %collective-permute-start.6 = (bf16[2,256,256]{2,1,0:T(8,128)(2,1)S(1)}, bf16[2,256,256]{2,1,0:T(8,128)(2,1)S(1)}, u32[]{:S(2)}, u32[]{:S(2)}) collective-permute-start(bf16[2,256,256]{2,1,0:T(8,128)(2,1)S(1)} %get-tuple-element.31), channel_id=1, source_target_pairs={{64,65},{65,66},{66,67},{67,64},{68,69},{69,70},{70,71},{71,68},{7... | collective-permute-start | bytes 786440 | tf_op jit(solution)/shard_map/ppermute | solution.py:390
  30.8 10.6 %collective-permute-start.7 = (bf16[2,256,256]{2,1,0:T(8,128)(2,1)S(1)}, bf16[2,256,256]{2,1,0:T(8,128)(2,1)S(1)}, u32[]{:S(2)}, u32[]{:S(2)}) collective-permute-start(bf16[2,256,256]{2,1,0:T(8,128)(2,1)S(1)} %get-tuple-element.32), channel_id=1, source_target_pairs={{64,67},{65,64},{66,65},{67,66},{68,71},{69,68},{70,69},{71,70},{7... | collective-permute-start | bytes 786440 | tf_op jit(solution)/shard_map/ppermute | solution.py:390
  34.4 12.6 %collective-permute-start.1 = (bf16[2,256,256]{2,1,0:T(8,128)(2,1)}, bf16[2,256,256]{2,1,0:T(8,128)(2,1)S(1)}, u32[]{:S(2)}, u32[]{:S(2)}) collective-permute-start(bf16[2,256,256]{2,1,0:T(8,128)(2,1)} %collective-permute-done.refs_0_), channel_id=1, source_target_pairs={{0,2},{1,3},{2,0},{3,1},{4,6},{5,7},{6,4},{7,5},{8,10},{9,11},{10,... | collective-permute-start | bytes 786440 | tf_op jit(solution)/shard_map/ppermute | solution.py:390
  38.0 9.0 %collective-permute-start.3 = (bf16[2,256,256]{2,1,0:T(8,128)(2,1)S(1)}, bf16[2,256,256]{2,1,0:T(8,128)(2,1)S(1)}, u32[]{:S(2)}, u32[]{:S(2)}) collective-permute-start(bf16[2,256,256]{2,1,0:T(8,128)(2,1)S(1)} %get-tuple-element.30), channel_id=1, source_target_pairs={{64,66},{65,67},{66,64},{67,65},{68,70},{69,71},{70,68},{71,69},{7... | collective-permute-start | bytes 786440 | tf_op jit(solution)/shard_map/ppermute | solution.py:390
  45.4 6.9 %collective-permute-start.10 = (bf16[2,2,4,64,256]{4,3,2,1,0:T(8,128)(2,1)S(1)}, bf16[2,2,4,64,256]{4,3,2,1,0:T(8,128)(2,1)S(1)}, u32[]{:S(2)}, u32[]{:S(2)}) collective-permute-start(bf16[2,2,4,64,256]{4,3,2,1,0:T(8,128)(2,1)S(1)} %get-tuple-element.43), channel_id=1, source_target_pairs={{0,64},{64,0},{128,192},{192,128},{1,65},{65,1},{129,193},{193,129... | collective-permute-start | bytes 1572872 | tf_op jit(solution)/shard_map/ppermute | solution.py:412
  47.0 4.4 %collective-permute-start.8 = (bf16[2,256,256]{2,1,0:T(8,128)(2,1)S(1)}, bf16[2,256,256]{2,1,0:T(8,128)(2,1)S(1)}, u32[]{:S(2)}, u32[]{:S(2)}) collective-permute-start(bf16[2,256,256]{2,1,0:T(8,128)(2,1)S(1)} %collective-permute-done.3.lane1), channel_id=1, source_target_pairs={{64,0},{192,128},{65,1},{193,129},{66,2},{194,130},{67,3},{195,131... | collective-permute-start | bytes 786440 | tf_op jit(solution)/shard_map/ppermute | solution.py:412
  48.9 3.4 %collective-permute-start.9 = (bf16[2,256,256]{2,1,0:T(8,128)(2,1)S(1)}, bf16[2,256,256]{2,1,0:T(8,128)(2,1)S(1)}, u32[]{:S(2)}, u32[]{:S(2)}) collective-permute-start(bf16[2,256,256]{2,1,0:T(8,128)(2,1)S(1)} %collective-permute-done.1.lane0), channel_id=1, source_target_pairs={{0,64},{128,192},{1,65},{129,193},{2,66},{130,194},{3,67},{131,195... | collective-permute-start | bytes 786440 | tf_op jit(solution)/shard_map/ppermute | solution.py:412

commit v5 on v4

--- a/solution.py
+++ b/solution.py
@@ -158,7 +158,9 @@
 BIG = pltpu.CompilerParams(vmem_limit_bytes=16 * MIB)
 
 
-def open_kernel(piece, cols, rows, ph_in, pp_in, sums, first_up, first_down, plain, sems):
+def open_kernel(
+    piece, cols, rows, ph_in, pp_in, sums, kept, first_up, first_down, plain, sems
+):
     loads = [
         pltpu.make_async_copy(source.at[part], sums.at[i, part], sems.at[i, part])
         for i, source in enumerate((ph_in, pp_in))
@@ -175,39 +177,28 @@
         sums[which, part, t] += term
 
     one_walker(piece[0], piece[1], cols, rows.at[0], first_up, first_down, plain, ready, put)
+    kept[...] = piece[...]
 
 
 def open_sums(piece, cols, rows, ph, pp):
     return pl.pallas_call(
         open_kernel,
-        out_shape=jax.ShapeDtypeStruct((2, *SUMS), F32),
+        out_shape=(jax.ShapeDtypeStruct((2, *SUMS), F32), jax.ShapeDtypeStruct(PIECE, BF)),
         in_specs=[IN_VMEM] * 3 + [IN_HBM] * 2,
-        out_specs=IN_VMEM,
+        out_specs=(IN_VMEM,) * 2,
         scratch_shapes=WORK + [pltpu.SemaphoreType.DMA((2, 2))],
-        cost_estimate=TINY,
+        cost_estimate=pl.CostEstimate(flops=4 * 10**9, bytes_accessed=1, transcendentals=0),
         compiler_params=BIG,
         name="open_sums",
     )(piece, cols, rows, ph, pp)
 
 
-def fetch_lane(core, pair, hold, sem):
-    for c in range(2):
-
-        @pl.when(core == c)
-        def _(c=c):
-            pltpu.make_async_copy(pair[c], hold, sem).start()
-
-
-def spread_kernel(count, fresh, send, place, *refs):
-    pairs = [refs[2 * i : 2 * i + 2] for i in range(count)]
-    cols, rows, before = refs[2 * count : 2 * count + 3]
-    after = refs[2 * count + 3 : 2 * count + 4 + send]
-    first_up, first_down, plain, hold, sems, *held = refs[2 * count + 4 + send :]
-    core = place[0] & 1
-    for n, pair in enumerate(pairs):
-        fetch_lane(core, pair, hold.at[n], sems.at[n])
-    for n, pair in enumerate(pairs):
-        pltpu.make_async_copy(pair[0], hold.at[n], sems.at[n]).wait()
+def spread_kernel(count, fresh, send, *refs):
+    pieces = refs[:count]
+    cols, rows, before = refs[count : count + 3]
+    after = refs[count + 3 : count + 4 + send]
+    first_up, first_down, plain, *held = refs[count + 4 + send :]
+    for n, piece in enumerate(pieces):
         for b in range(2):
 
             def put(which, part, t, term, n=n, b=b):
@@ -226,61 +217,53 @@
                     after[1][which, part, t] = term.astype(BF)
 
             one_walker(
-                hold[n, 0], hold[n, 1], cols, rows.at[b], first_up, first_down, plain,
+                piece[0], piece[1], cols, rows.at[b], first_up, first_down, plain,
                 lambda: None, put,
             )
 
 
-def spread(place, pairs, cols, rows, sums, send=False):
-    count, fresh = len(pairs), sums.shape[0] == 2
+def spread(pieces, cols, rows, sums, send=False):
+    count, fresh = len(pieces), sums.shape[0] == 2
     out_shape = [jax.ShapeDtypeStruct((2 if send else 4, *SUMS), F32)]
     if send:
         out_shape.append(jax.ShapeDtypeStruct((2, *SUMS), BF))
     return pl.pallas_call(
         functools.partial(spread_kernel, count, fresh, send),
         out_shape=tuple(out_shape),
-        in_specs=[IN_SMEM] + [ANYWHERE] * (2 * count) + [IN_VMEM] * 3,
+        in_specs=[IN_VMEM] * (count + 3),
         out_specs=(IN_VMEM,) * len(out_shape),
-        scratch_shapes=WORK
-        + [pltpu.VMEM((count, *PIECE), BF), pltpu.SemaphoreType.DMA((count,))]
-        + [pltpu.VMEM((2, *SUMS), F32)] * send,
+        scratch_shapes=WORK + [pltpu.VMEM((2, *SUMS), F32)] * send,
         cost_estimate=TINY,
         compiler_params=BIG,
         name="spread",
-    )(place, *[piece for pair in pairs for piece in pair], cols, rows, sums)
-
-
-def add_kernel(place, lane0, lane1, cols, rows, before, after, first_up, first_down, plain, hold, sem):
-    fetch_lane(place[0] & 1, (lane0, lane1), hold, sem.at[0])
-    pltpu.make_async_copy(lane0, hold, sem.at[0]).wait()
-
+    )(*pieces, cols, rows, sums)
+
+
+def add_kernel(piece, cols, rows, before, after, first_up, first_down, plain):
     def put(which, part, t, term):
         after[which, part, t] = before[which, part, t] + term
 
     one_walker(
-        hold[0], hold[1], cols, rows.at[0], first_up, first_down, plain, lambda: None, put
-    )
-
-
-def add(place, pair, cols, rows, sums):
+        piece[0], piece[1], cols, rows.at[0], first_up, first_down, plain, lambda: None, put
+    )
+
+
+def add(piece, cols, rows, sums):
     return pl.pallas_call(
         add_kernel,
         out_shape=jax.ShapeDtypeStruct((2, *SUMS), F32),
-        in_specs=[IN_SMEM] + [ANYWHERE] * 2 + [IN_VMEM] * 3,
+        in_specs=[IN_VMEM] * 4,
         out_specs=IN_VMEM,
-        scratch_shapes=WORK + [pltpu.VMEM(PIECE, BF), pltpu.SemaphoreType.DMA((1,))],
+        scratch_shapes=WORK,
         cost_estimate=TINY,
         compiler_params=BIG,
         name="add",
-    )(place, *pair, cols, rows, sums)
+    )(piece, cols, rows, sums)
 
 
 def close_kernel(
-    place, lane0, lane1, cols, rows, sums, others, ph, pp,
-    first_up, first_down, plain, hold, sem, total, sems,
+    piece, cols, rows, sums, others, ph, pp, first_up, first_down, plain, total, sems
 ):
-    fetch_lane(place[0] & 1, (lane0, lane1), hold, sem.at[0])
-    pltpu.make_async_copy(lane0, hold, sem.at[0]).wait()
     stores = []
 
     def put(which, part, t, term):
@@ -293,68 +276,48 @@
         stores.append(store)
 
     one_walker(
-        hold[0], hold[1], cols, rows.at[0], first_up, first_down, plain, lambda: None, put
+        piece[0], piece[1], cols, rows.at[0], first_up, first_down, plain, lambda: None, put
     )
     for store in stores:
         store.wait()
 
 
-def close_sums(place, pair, cols, rows, sums, others):
+def close_sums(piece, cols, rows, sums, others):
     return pl.pallas_call(
         close_kernel,
         out_shape=(jax.ShapeDtypeStruct(SUMS, F32),) * 2,
-        in_specs=[IN_SMEM] + [ANYWHERE] * 2 + [IN_VMEM] * 4,
+        in_specs=[IN_VMEM] * 5,
         out_specs=(ANYWHERE,) * 2,
         scratch_shapes=WORK
-        + [pltpu.VMEM(PIECE, BF), pltpu.SemaphoreType.DMA((1,))]
         + [pltpu.VMEM((2, *SUMS), F32), pltpu.SemaphoreType.DMA((2, 2, TRANS))],
         cost_estimate=TINY,
         compiler_params=BIG,
         name="close_sums",
-    )(place, *pair, cols, rows, sums, others)
-
-
-def scale_kernel(masses, spins, out, raw, done, in_sems, out_sems):
-    half = ORDER // 2
-    parts = [(spin, pl.ds(begin, half)) for spin in range(2) for begin in (0, half)]
-    loads = [
-        pltpu.make_async_copy(masses.at[0, spin, rows], raw.at[spin, rows], in_sems.at[i])
-        for i, (spin, rows) in enumerate(parts)
-    ]
-    stores = [
-        pltpu.make_async_copy(done.at[spin, rows], out.at[spin, rows], out_sems.at[i])
-        for i, (spin, rows) in enumerate(parts)
-    ]
-    for load in loads:
-        load.start()
+    )(piece, cols, rows, sums, others)
+
+
+def scale_kernel(masses, spins, out):
     signed = (2 * spins[...] - 1).astype(F32)
-    factors = jnp.exp(COUPLING * signed), jnp.exp(-COUPLING * signed)
-    for (spin, rows), load, store in zip(parts, loads, stores):
-        load.wait()
-        done[spin, rows] = (raw[spin, rows].astype(F32) * factors[spin]).astype(BF)
-        store.start()
-    for store in stores:
-        store.wait()
+    for spin, sign in enumerate((COUPLING, -COUPLING)):
+        out[spin] = (masses[0, spin].astype(F32) * jnp.exp(sign * signed)).astype(BF)
 
 
 def scale(masses, spins):
     return pl.pallas_call(
         scale_kernel,
-        out_shape=jax.ShapeDtypeStruct((2, ORDER, ORDER), BF),
-        in_specs=[ANYWHERE, IN_VMEM],
-        out_specs=ANYWHERE,
-        scratch_shapes=[pltpu.VMEM((2, ORDER, ORDER), BF)] * 2
-        + [pltpu.SemaphoreType.DMA((4,))] * 2,
+        out_shape=jax.ShapeDtypeStruct(PIECE, BF),
+        in_specs=[IN_VMEM] * 2,
+        out_specs=IN_VMEM,
         cost_estimate=TINY,
         compiler_params=pltpu.CompilerParams(vmem_limit_bytes=56 * MIB),
         name="scale",
     )(masses, spins)
 
 
-def route_kernel(steps, y_ref, own, got, after, *refs):
+def route_kernel(steps, place, y_ref, own, got, *refs):
     outs, sems = refs[: len(steps)], refs[len(steps)]
     for i, step in enumerate(steps):
-        wraps = y_ref[0] + step >= PLANE
+        wraps = (place[0] & 1 == 0) | (y_ref[0] + step >= PLANE)
 
         @pl.when(wraps)
         def _(i=i):
@@ -368,76 +331,60 @@
         pltpu.make_async_copy(own, outs[i], sems.at[i]).wait()
 
 
-def route(y, own, got, after, steps):
+def route(place, y, own, got, steps):
     return pl.pallas_call(
         functools.partial(route_kernel, steps),
         out_shape=(jax.ShapeDtypeStruct(own.shape, BF),) * len(steps),
-        in_specs=[IN_SMEM] + [ANYWHERE] * 2 + [IN_VMEM],
+        in_specs=[IN_SMEM] * 2 + [ANYWHERE] * 2,
         out_specs=(ANYWHERE,) * len(steps),
         scratch_shapes=[pltpu.SemaphoreType.DMA((len(steps),))],
         cost_estimate=TINY,
         compiler_params=pltpu.CompilerParams(vmem_limit_bytes=MIB),
         name="route",
-    )(y, own, got, after)
+    )(place, y, own, got)
 
 
 PLANE = 4
 BLOCKS = 64
 
 
-def move(value, pairs):
-    flat = [(a * BLOCKS + b, c * BLOCKS + d) for (a, b), (c, d) in pairs]
-    return lax.ppermute(value, ("grp", "blk"), flat)
-
-
-def next_plane(value, core):
-    return move(
-        value,
-        [((g, b), (g + core, (b + PLANE) % BLOCKS)) for g in (0, 2) for b in range(BLOCKS)],
-    )
-
-
-def along_y(value, steps, core):
-    return move(
-        value,
-        [
-            ((g + core, b), (g + core, b // PLANE * PLANE + (b + steps) % PLANE))
-            for g in (0, 2)
-            for b in range(BLOCKS)
-        ],
-    )
-
-
-def other_core(value, cores=(0, 1)):
-    return lax.ppermute(value, "grp", [(s, s ^ 1) for s in range(4) if s % 2 in cores])
+def planes_back(value):
+    pairs = [
+        (g * BLOCKS + b, g * BLOCKS + (b + PLANE * (1 + g % 2)) % BLOCKS)
+        for g in range(4)
+        for b in range(BLOCKS)
+    ]
+    return lax.ppermute(value, ("grp", "blk"), pairs)
+
+
+def along_y(value, steps):
+    pairs = [(b, b // PLANE * PLANE + (b + steps) % PLANE) for b in range(BLOCKS)]
+    return lax.ppermute(value, "blk", pairs)
+
+
+def other_core(value):
+    return lax.ppermute(value, "grp", [(s, s ^ 1) for s in range(4)])
 
 
 def on_device(masses, spins, shift_table, flip_table, ph_in, pp_in):
     place = lax.axis_index("grp").reshape(1).astype(jnp.int32)
     y = (lax.axis_index("blk") % PLANE).reshape(1).astype(jnp.int32)
     own = scale(masses, spins)
-    near = next_plane(own, 0)
+    got = planes_back(own)
     cols, rows = tables(place, shift_table, flip_table)
-    near, cols = lax.optimization_barrier((near, cols))
-    far = next_plane(near, 1)
-    right0, left0 = along_y(near, 1, 0), along_y(near, 3, 0)
-    sums = open_sums(own, cols, rows, ph_in, pp_in)
-    far, sums = lax.optimization_barrier((far, sums))
-    right, left, middle = route(y, own, far, sums, (1, 3, 2))
-    middle0 = along_y(near, 2, 0)
-    right1, left1 = along_y(right, 1, 1), along_y(left, 3, 1)
-    (sums,) = spread(place, [(near, far)], cols, rows, sums)
+    sums, kept = open_sums(own, cols, rows, ph_in, pp_in)
+    right, left, middle = route(place, y, kept, got, (1, 3, 2))
+    right, left = along_y(right, 1), along_y(left, 3)
+    (sums,) = spread([got], cols, rows, sums)
     middle, sums = lax.optimization_barrier((middle, sums))
-    middle1 = along_y(middle, 2, 1)
-    right0, left0, right1, left1, sums = lax.optimization_barrier(
-        (right0, left0, right1, left1, sums)
-    )
-    sums, sent = spread(place, [(right0, right1), (left0, left1)], cols, rows, sums, True)
+    middle = along_y(middle, 2)
+    right, left, sums = lax.optimization_barrier((right, left, sums))
+    sums, sent = spread([right, left], cols, rows, sums, True)
     others = other_core(sent)
-    middle0, middle1, sums = lax.optimization_barrier((middle0, middle1, sums))
-    swapped = other_core(middle1, (1,)), other_core(middle0, (0,))
-    sums = add(place, (middle0, middle1), cols, rows, sums)
-    return close_sums(place, swapped, cols, rows, sums, others)
+    middle, sums = lax.optimization_barrier((middle, sums))
+    swapped = other_core(middle)
+    sums = add(middle, cols, rows, sums)
+    return close_sums(swapped, cols, rows, sums, others)
 
 
 def solution(mesh):

time: 55 us -> 40.4 us (0.73)
  waiting for transfers between devices: 11 us -> 6.08 us
  starting transfers between devices: 20.6 us -> 16.4 us
  local copies, waits for them, and re-layouts: 4.4 us -> 1.38 us
  Pallas kernels: 17.5 us -> 15.6 us
    ppermute x11 -> x6, waiting for transfers between devices: 11 us -> 6.08 us  [the longest x1 5.34 us: planes_back(): return lax.ppermute(value, ('grp', 'blk'), pairs)]
    ppermute x11 -> x6, starting transfers between devices: 20.6 us -> 16.4 us  [the longest x2 7.84 us: other_core(): return lax.ppermute(value, 'grp', [(s, s ^ 1) for s in range(4)])]
    unnamed x10, local copies, waits for them, and re-layouts: 4.4 us -> 1.38 us
    pallas_call x2, Pallas kernels: 6.87 us -> 5.63 us  [spread(): pl.pallas_call(functools.partial(spread_kernel, count, fresh, send), out_...]
    pallas_call x2, Pallas kernels: 3.79 us -> 3.2 us  [the longest x1 1.71 us: scale(): pl.pallas_call(scale_kernel, out_shape=jax.ShapeDtypeStruct(PIECE, BF), i...]
  transfers between devices with their start and end apart: 11 -> 6, of which waited for: 2 -> 2; matrix products, arithmetic and copies ran while one was open for 0% -> 0% of each run, Pallas kernels for 24% -> 29%
where the time goes in v5:
time: 40.4 us; the launch traced here: 40.3 us
  starting transfers between devices  16.4 us (41%)
  Pallas kernels  15.6 us (39%)
  waiting for transfers between devices  6.08 us (15%)
  local copies, waits for them, and re-layouts  1.38 us (3%)
  between operations  0.87 us (2%)
    ppermute x2, starting transfers between devices, other_core(): return lax.ppermute(value, 'grp', [(s, s ^ 1) for s in range(4)])  7.84 us
    pallas_call x2, Pallas kernels, spread(): pl.pallas_call(functools.partial(spread_kernel, count, fresh, send), out_...  5.63 us
    ppermute x1, waiting for transfers between devices, planes_back(): return lax.ppermute(value, ('grp', 'blk'), pairs)  5.34 us
    ppermute x3, starting transfers between devices, along_y(): return lax.ppermute(value, 'blk', pairs)  4.72 us
    ppermute x1, starting transfers between devices, planes_back(): return lax.ppermute(value, ('grp', 'blk'), pairs)  3.82 us
    pallas_call x1, Pallas kernels, tables(): pl.pallas_call(table_kernel, out_shape=(jax.ShapeDtypeStruct((2 * TRANS +...  3.61 us
    pallas_call x1, Pallas kernels, close_sums(): pl.pallas_call(close_kernel, out_shape=(jax.ShapeDtypeStruct(SUMS, F32),)...  1.95 us
    pallas_call x1, Pallas kernels, scale(): pl.pallas_call(scale_kernel, out_shape=jax.ShapeDtypeStruct(PIECE, BF), i...  1.71 us
  transfers between devices with their start and end apart: 6, of which 2 were waited for; matrix products, arithmetic and copies ran while one was open for 0% of the time, Pallas kernels for 29%

profile of v5, /device:TPU:1, one launch (start us, length us, event | category | flops | bytes accessed | tf_op | source)
XLA Modules:
  0.0 40.3 jit_solution(7856488619803492839)
XLA Ops:
  0.6 1.7 %scale.1.piece = bf16[2,256,256]{2,1,0:T(8,128)(2,1)} custom-call(bf16[1,2,256,256]{3,2,1,0:T(8,128)(2,1)} %masses.1, s32[1,256]{1,0:T(1,128)} %spins.1), custom_call_target="tpu_custom_call" | custom-call | flops 1 | bytes 1 | tf_op jit(solution)/shard_map/scale/pallas_call | solution.py:306
  2.3 3.8 %collective-permute-start = (bf16[2,256,256]{2,1,0:T(8,128)(2,1)}, bf16[2,256,256]{2,1,0:T(8,128)(2,1)S(1)}, u32[]{:S(2)}, u32[]{:S(2)}) collective-permute-start(bf16[2,256,256]{2,1,0:T(8,128)(2,1)} %scale.1.piece), channel_id=1, source_target_pairs={{0,4},{1,5},{2,6},{3,7},{4,8},{5,9},{6,10},{7,11},{8,12},{9,13},{1... | collective-permute-start | bytes 786440 | tf_op jit(solution)/shard_map/ppermute | solution.py:357
  6.2 0.0 copy-start.3
  6.2 0.7 %copy-done.3 = s32[4,256]{1,0:T(4,128)S(1)} copy-done((s32[4,256]{1,0:T(4,128)S(1)}, s32[4,256]{1,0:T(4,128)}, u32[]{:S(2)}) %copy-start.3) | copy-done | bytes 4120
  6.8 0.0 copy-start.4
  6.8 0.7 %copy-done.4 = s32[4,256]{1,0:T(4,128)S(1)} copy-done((s32[4,256]{1,0:T(4,128)S(1)}, s32[4,256]{1,0:T(4,128)}, u32[]{:S(2)}) %copy-start.4) | copy-done | bytes 4120
  7.5 0.0 copy-start
  7.5 0.0 copy-start.1
  7.5 0.0 copy-start.2
  7.5 3.6 %tables.1 = (bf16[9,512,256]{2,1,0:T(8,128)(2,1)S(1)}, bf16[2,1152,256]{2,1,0:T(8,128)(2,1)S(1)}) custom-call(s32[1]{0:T(128)} %bitcast.place_ref.place, s32[4,256]{1,0:T(4,128)S(1)} %copy-done.3, s32[4,256]{1,0:T(4,128)S(1)} %copy-done.4), custom_call_target="tpu_custom_call" | custom-call | flops 4000000000 | bytes 1 | tf_op jit(solution)/shard_map/tables/pallas_call | solution.py:83
  11.2 0.0 copy-done
  11.2 0.0 copy-done.1
  11.2 0.0 copy-done.2
  11.2 1.5 %open_sums.1 = (f32[2,2,4,64,256]{4,3,2,1,0:T(8,128)S(1)}, bf16[2,256,256]{2,1,0:T(8,128)(2,1)S(1)}) custom-call(bf16[2,256,256]{2,1,0:T(8,128)(2,1)S(1)} %copy-done, bf16[9,512,256]{2,1,0:T(8,128)(2,1)S(1)} %get-tuple-element.18.cols.refs_1_.refs_2_, bf16[2,1152,256]{2,1,0:T(8,128)(2,1)S(1)} %get-tuple-element.19.rows.refs_2_.refs_3_, ...), custom_call_target="tpu_custom_call" | custom-call | flops 4000000000 | bytes 1 | tf_op jit(solution)/shard_map/open_sums/pallas_call | solution.py:184
  12.7 5.3 %collective-permute-done.got.refs_0_ = bf16[2,256,256]{2,1,0:T(8,128)(2,1)S(1)} collective-permute-done((bf16[2,256,256]{2,1,0:T(8,128)(2,1)}, bf16[2,256,256]{2,1,0:T(8,128)(2,1)S(1)}, u32[]{:S(2)}, u32[]{:S(2)}) %collective-permute-start) | collective-permute-done | bytes 262176 | tf_op jit(solution)/shard_map/ppermute | solution.py:357
  18.0 0.1 route.1
  18.1 1.4 %collective-permute-start.2 = (bf16[2,256,256]{2,1,0:T(8,128)(2,1)S(1)}, bf16[2,256,256]{2,1,0:T(8,128)(2,1)S(1)}, u32[]{:S(2)}, u32[]{:S(2)}) collective-permute-start(bf16[2,256,256]{2,1,0:T(8,128)(2,1)S(1)} %get-tuple-element.24), channel_id=1, source_target_pairs={{0,1},{1,2},{2,3},{3,0},{4,5},{5,6},{6,7},{7,4},{8,9},{9,10},{10,1... | collective-permute-start | bytes 786440 | tf_op jit(solution)/shard_map/ppermute | solution.py:362
  19.5 1.5 %collective-permute-start.3 = (bf16[2,256,256]{2,1,0:T(8,128)(2,1)S(1)}, bf16[2,256,256]{2,1,0:T(8,128)(2,1)S(1)}, u32[]{:S(2)}, u32[]{:S(2)}) collective-permute-start(bf16[2,256,256]{2,1,0:T(8,128)(2,1)S(1)} %get-tuple-element.25), channel_id=1, source_target_pairs={{0,3},{1,0},{2,1},{3,2},{4,7},{5,4},{6,5},{7,6},{8,11},{9,8},{10,9... | collective-permute-start | bytes 786440 | tf_op jit(solution)/shard_map/ppermute | solution.py:362
  21.0 1.9 %spread.2.refs_4_ = f32[4,2,4,64,256]{4,3,2,1,0:T(8,128)S(1)} custom-call(bf16[2,256,256]{2,1,0:T(8,128)(2,1)S(1)} %collective-permute-done.got.refs_0_, bf16[9,512,256]{2,1,0:T(8,128)(2,1)S(1)} %get-tuple-element.18.cols.refs_1_.refs_2_, bf16[2,1152,256]{2,1,0:T(8,128)(2,1)S(1)} %get-tuple-element.19.rows.refs_2_.refs_3_, ...), custom_call_target="tpu_custom_call" | custom-call | flops 1 | bytes 1 | tf_op jit(solution)/shard_map/spread/pallas_call | solution.py:230
  23.0 1.8 %collective-permute-start.1 = (bf16[2,256,256]{2,1,0:T(8,128)(2,1)S(1)}, bf16[2,256,256]{2,1,0:T(8,128)(2,1)S(1)}, u32[]{:S(2)}, u32[]{:S(2)}) collective-permute-start(bf16[2,256,256]{2,1,0:T(8,128)(2,1)S(1)} %get-tuple-element.23), channel_id=1, source_target_pairs={{0,2},{1,3},{2,0},{3,1},{4,6},{5,7},{6,4},{7,5},{8,10},{9,11},{10,... | collective-permute-start | bytes 786440 | tf_op jit(solution)/shard_map/ppermute | solution.py:362
  24.8 0.0 collective-permute-done.2.refs_0_
  24.8 0.0 collective-permute-done.3.refs_1_
  24.8 3.7 %spread.3 = (f32[2,2,4,64,256]{4,3,2,1,0:T(8,128)S(1)}, bf16[2,2,4,64,256]{4,3,2,1,0:T(8,128)(2,1)S(1)}) custom-call(bf16[2,256,256]{2,1,0:T(8,128)(2,1)S(1)} %collective-permute-done.2.refs_0_, bf16[2,256,256]{2,1,0:T(8,128)(2,1)S(1)} %collective-permute-done.3.refs_1_, bf16[9,512,256]{2,1,0:T(8,128)(2,1)S(1)} %get-tuple-element.18.cols.refs_1_.refs_2_, ...), custom_call_target="tpu_custom_call" | custom-call | flops 1 | bytes 1 | tf_op jit(solution)/shard_map/spread/pallas_call | solution.py:230
  28.5 7.7 %collective-permute-start.5 = (bf16[2,2,4,64,256]{4,3,2,1,0:T(8,128)(2,1)S(1)}, bf16[2,2,4,64,256]{4,3,2,1,0:T(8,128)(2,1)S(1)}, u32[]{:S(2)}, u32[]{:S(2)}) collective-permute-start(bf16[2,2,4,64,256]{4,3,2,1,0:T(8,128)(2,1)S(1)} %get-tuple-element.33), channel_id=1, source_target_pairs={{0,64},{64,0},{128,192},{192,128},{1,65},{65,1},{129,193},{193,129... | collective-permute-start | bytes 1572872 | tf_op jit(solution)/shard_map/ppermute | solution.py:366
  36.2 0.0 collective-permute-done.1.piece
  36.3 0.1 collective-permute-start.4
  36.4 1.1 %add.6.sums = f32[2,2,4,64,256]{4,3,2,1,0:T(8,128)S(1)} custom-call(bf16[2,256,256]{2,1,0:T(8,128)(2,1)S(1)} %collective-permute-done.1.piece, bf16[9,512,256]{2,1,0:T(8,128)(2,1)S(1)} %get-tuple-element.18.cols.refs_1_.refs_2_, bf16[2,1152,256]{2,1,0:T(8,128)(2,1)S(1)} %get-tuple-element.19.rows.refs_2_.refs_3_, ...), custom_call_target="tpu_custom_call" | custom-call | flops 1 | bytes 1 | tf_op jit(solution)/shard_map/add/pallas_call | solution.py:252
  37.4 0.7 %collective-permute-done.4.piece = bf16[2,256,256]{2,1,0:T(8,128)(2,1)S(1)} collective-permute-done((bf16[2,256,256]{2,1,0:T(8,128)(2,1)S(1)}, bf16[2,256,256]{2,1,0:T(8,128)(2,1)S(1)}, u32[]{:S(2)}, u32[]{:S(2)}) %collective-permute-start.4) | collective-permute-done | bytes 262176 | tf_op jit(solution)/shard_map/ppermute | solution.py:366
  38.2 0.0 collective-permute-done.5.others
  38.2 2.0 %close_sums.1 = (f32[2,4,64,256]{3,2,1,0:T(8,128)}, f32[2,4,64,256]{3,2,1,0:T(8,128)}) custom-call(bf16[2,256,256]{2,1,0:T(8,128)(2,1)S(1)} %collective-permute-done.4.piece, bf16[9,512,256]{2,1,0:T(8,128)(2,1)S(1)} %get-tuple-element.18.cols.refs_1_.refs_2_, bf16[2,1152,256]{2,1,0:T(8,128)(2,1)S(1)} %get-tuple-element.19.rows.refs_2_.refs_3_, ...), custom_call_target="tpu_custom_call" | custom-call | flops 1 | bytes 1 | tf_op jit(solution)/shard_map/close_sums/pallas_call | solution.py:286
Async XLA Ops:
  2.3 15.7 %collective-permute-start = (bf16[2,256,256]{2,1,0:T(8,128)(2,1)}, bf16[2,256,256]{2,1,0:T(8,128)(2,1)S(1)}, u32[]{:S(2)}, u32[]{:S(2)}) collective-permute-start(bf16[2,256,256]{2,1,0:T(8,128)(2,1)} %scale.1.piece), channel_id=1, source_target_pairs={{0,4},{1,5},{2,6},{3,7},{4,8},{5,9},{6,10},{7,11},{8,12},{9,13},{1... | collective-permute-start | bytes 786440 | tf_op jit(solution)/shard_map/ppermute | solution.py:357
  6.2 0.7 %copy-start.3 = (s32[4,256]{1,0:T(4,128)S(1)}, s32[4,256]{1,0:T(4,128)}, u32[]{:S(2)}) copy-start(s32[4,256]{1,0:T(4,128)} %shift_in.1) | copy-start | bytes 12292
  6.8 0.7 %copy-start.4 = (s32[4,256]{1,0:T(4,128)S(1)}, s32[4,256]{1,0:T(4,128)}, u32[]{:S(2)}) copy-start(s32[4,256]{1,0:T(4,128)} %flip_in.1) | copy-start | bytes 12292
  7.5 3.6 %copy-start = (bf16[2,256,256]{2,1,0:T(8,128)(2,1)S(1)}, bf16[2,256,256]{2,1,0:T(8,128)(2,1)}, u32[]{:S(2)}) copy-start(bf16[2,256,256]{2,1,0:T(8,128)(2,1)} %scale.1.piece) | copy-start | bytes 786436
  7.5 3.6 %copy-start.1 = (f32[2,4,64,256]{3,2,1,0:T(8,128)S(1)}, f32[2,4,64,256]{3,2,1,0:T(8,128)}, u32[]{:S(2)}) copy-start(f32[2,4,64,256]{3,2,1,0:T(8,128)} %ph_in.1) | copy-start | bytes 1572868
  7.5 3.6 %copy-start.2 = (f32[2,4,64,256]{3,2,1,0:T(8,128)S(1)}, f32[2,4,64,256]{3,2,1,0:T(8,128)}, u32[]{:S(2)}) copy-start(f32[2,4,64,256]{3,2,1,0:T(8,128)} %pp_in.1) | copy-start | bytes 1572868
  18.1 6.6 %collective-permute-start.2 = (bf16[2,256,256]{2,1,0:T(8,128)(2,1)S(1)}, bf16[2,256,256]{2,1,0:T(8,128)(2,1)S(1)}, u32[]{:S(2)}, u32[]{:S(2)}) collective-permute-start(bf16[2,256,256]{2,1,0:T(8,128)(2,1)S(1)} %get-tuple-element.24), channel_id=1, source_target_pairs={{0,1},{1,2},{2,3},{3,0},{4,5},{5,6},{6,7},{7,4},{8,9},{9,10},{10,1... | collective-permute-start | bytes 786440 | tf_op jit(solution)/shard_map/ppermute | solution.py:362
  19.5 5.3 %collective-permute-start.3 = (bf16[2,256,256]{2,1,0:T(8,128)(2,1)S(1)}, bf16[2,256,256]{2,1,0:T(8,128)(2,1)S(1)}, u32[]{:S(2)}, u32[]{:S(2)}) collective-permute-start(bf16[2,256,256]{2,1,0:T(8,128)(2,1)S(1)} %get-tuple-element.25), channel_id=1, source_target_pairs={{0,3},{1,0},{2,1},{3,2},{4,7},{5,4},{6,5},{7,6},{8,11},{9,8},{10,9... | collective-permute-start | bytes 786440 | tf_op jit(solution)/shard_map/ppermute | solution.py:362
  23.0 13.3 %collective-permute-start.1 = (bf16[2,256,256]{2,1,0:T(8,128)(2,1)S(1)}, bf16[2,256,256]{2,1,0:T(8,128)(2,1)S(1)}, u32[]{:S(2)}, u32[]{:S(2)}) collective-permute-start(bf16[2,256,256]{2,1,0:T(8,128)(2,1)S(1)} %get-tuple-element.23), channel_id=1, source_target_pairs={{0,2},{1,3},{2,0},{3,1},{4,6},{5,7},{6,4},{7,5},{8,10},{9,11},{10,... | collective-permute-start | bytes 786440 | tf_op jit(solution)/shard_map/ppermute | solution.py:362
  28.5 9.7 %collective-permute-start.5 = (bf16[2,2,4,64,256]{4,3,2,1,0:T(8,128)(2,1)S(1)}, bf16[2,2,4,64,256]{4,3,2,1,0:T(8,128)(2,1)S(1)}, u32[]{:S(2)}, u32[]{:S(2)}) collective-permute-start(bf16[2,2,4,64,256]{4,3,2,1,0:T(8,128)(2,1)S(1)} %get-tuple-element.33), channel_id=1, source_target_pairs={{0,64},{64,0},{128,192},{192,128},{1,65},{65,1},{129,193},{193,129... | collective-permute-start | bytes 1572872 | tf_op jit(solution)/shard_map/ppermute | solution.py:366
  36.3 1.9 %collective-permute-start.4 = (bf16[2,256,256]{2,1,0:T(8,128)(2,1)S(1)}, bf16[2,256,256]{2,1,0:T(8,128)(2,1)S(1)}, u32[]{:S(2)}, u32[]{:S(2)}) collective-permute-start(bf16[2,256,256]{2,1,0:T(8,128)(2,1)S(1)} %collective-permute-done.1.piece), channel_id=1, source_target_pairs={{0,64},{64,0},{128,192},{192,128},{1,65},{65,1},{129,193},{193,129... | collective-permute-start | bytes 786440 | tf_op jit(solution)/shard_map/ppermute | solution.py:366

commit v6 on v5

--- a/solution.py
+++ b/solution.py
@@ -378,8 +378,10 @@
     (sums,) = spread([got], cols, rows, sums)
     middle, sums = lax.optimization_barrier((middle, sums))
     middle = along_y(middle, 2)
-    right, left, sums = lax.optimization_barrier((right, left, sums))
-    sums, sent = spread([right, left], cols, rows, sums, True)
+    right, sums = lax.optimization_barrier((right, sums))
+    (sums,) = spread([right], cols, rows, sums)
+    left, sums = lax.optimization_barrier((left, sums))
+    sums, sent = spread([left], cols, rows, sums, True)
     others = other_core(sent)
     middle, sums = lax.optimization_barrier((middle, sums))
     swapped = other_core(middle)

time: 40.4 us -> 39.6 us (0.980)
  waiting for transfers between devices: 6.08 us -> 5.44 us
    ppermute x2, waiting for transfers between devices: 0.73 us -> 0.09 us  [other_core(): return lax.ppermute(value, 'grp', [(s, s ^ 1) for s in range(4)])]
    ppermute x2, starting transfers between devices: 7.84 us -> 7.44 us  [other_core(): return lax.ppermute(value, 'grp', [(s, s ^ 1) for s in range(4)])]
    pallas_call x2 -> x3, Pallas kernels: 5.63 us -> 5.78 us  [spread(): pl.pallas_call(functools.partial(spread_kernel, count, fresh, send), out_...]
  transfers between devices with their start and end apart: 6 -> 6, of which waited for: 2 -> 2; matrix products, arithmetic and copies ran while one was open for 0% -> 0% of each run, Pallas kernels for 29% -> 30%
where the time goes in v6:
time: 39.6 us; the launch traced here: 39.4 us
  starting transfers between devices  16 us (40%)
  Pallas kernels  15.7 us (40%)
  waiting for transfers between devices  5.44 us (14%)
  local copies, waits for them, and re-layouts  1.38 us (3%)
  between operations  0.89 us (2%)
    ppermute x2, starting transfers between devices, other_core(): return lax.ppermute(value, 'grp', [(s, s ^ 1) for s in range(4)])  7.44 us
    pallas_call x3, Pallas kernels, spread(): pl.pallas_call(functools.partial(spread_kernel, count, fresh, send), out_...  5.78 us
    ppermute x1, waiting for transfers between devices, planes_back(): return lax.ppermute(value, ('grp', 'blk'), pairs)  5.34 us
    ppermute x3, starting transfers between devices, along_y(): return lax.ppermute(value, 'blk', pairs)  4.72 us
    ppermute x1, starting transfers between devices, planes_back(): return lax.ppermute(value, ('grp', 'blk'), pairs)  3.82 us
    pallas_call x1, Pallas kernels, tables(): pl.pallas_call(table_kernel, out_shape=(jax.ShapeDtypeStruct((2 * TRANS +...  3.61 us
    pallas_call x1, Pallas kernels, close_sums(): pl.pallas_call(close_kernel, out_shape=(jax.ShapeDtypeStruct(SUMS, F32),)...  1.95 us
    pallas_call x1, Pallas kernels, scale(): pl.pallas_call(scale_kernel, out_shape=jax.ShapeDtypeStruct(PIECE, BF), i...  1.71 us
  transfers between devices with their start and end apart: 6, of which 2 were waited for; matrix products, arithmetic and copies ran while one was open for 0% of the time, Pallas kernels for 30%

profile of v6, /device:TPU:1, one launch (start us, length us, event | category | flops | bytes accessed | tf_op | source)
XLA Modules:
  0.0 39.4 jit_solution(10369313339935032287)
XLA Ops:
  0.6 1.7 %scale.1.piece = bf16[2,256,256]{2,1,0:T(8,128)(2,1)} custom-call(bf16[1,2,256,256]{3,2,1,0:T(8,128)(2,1)} %masses.1, s32[1,256]{1,0:T(1,128)} %spins.1), custom_call_target="tpu_custom_call" | custom-call | flops 1 | bytes 1 | tf_op jit(solution)/shard_map/scale/pallas_call | solution.py:306
  2.3 3.8 %collective-permute-start = (bf16[2,256,256]{2,1,0:T(8,128)(2,1)}, bf16[2,256,256]{2,1,0:T(8,128)(2,1)S(1)}, u32[]{:S(2)}, u32[]{:S(2)}) collective-permute-start(bf16[2,256,256]{2,1,0:T(8,128)(2,1)} %scale.1.piece), channel_id=1, source_target_pairs={{0,4},{1,5},{2,6},{3,7},{4,8},{5,9},{6,10},{7,11},{8,12},{9,13},{1... | collective-permute-start | bytes 786440 | tf_op jit(solution)/shard_map/ppermute | solution.py:357
  6.2 0.0 copy-start.3
  6.2 0.7 %copy-done.3 = s32[4,256]{1,0:T(4,128)S(1)} copy-done((s32[4,256]{1,0:T(4,128)S(1)}, s32[4,256]{1,0:T(4,128)}, u32[]{:S(2)}) %copy-start.3) | copy-done | bytes 4120
  6.8 0.0 copy-start.4
  6.8 0.7 %copy-done.4 = s32[4,256]{1,0:T(4,128)S(1)} copy-done((s32[4,256]{1,0:T(4,128)S(1)}, s32[4,256]{1,0:T(4,128)}, u32[]{:S(2)}) %copy-start.4) | copy-done | bytes 4120
  7.5 0.0 copy-start
  7.5 0.0 copy-start.1
  7.5 0.0 copy-start.2
  7.5 3.6 %tables.1 = (bf16[9,512,256]{2,1,0:T(8,128)(2,1)S(1)}, bf16[2,1152,256]{2,1,0:T(8,128)(2,1)S(1)}) custom-call(s32[1]{0:T(128)} %bitcast.place_ref.place, s32[4,256]{1,0:T(4,128)S(1)} %copy-done.3, s32[4,256]{1,0:T(4,128)S(1)} %copy-done.4), custom_call_target="tpu_custom_call" | custom-call | flops 4000000000 | bytes 1 | tf_op jit(solution)/shard_map/tables/pallas_call | solution.py:83
  11.2 0.0 copy-done
  11.2 0.0 copy-done.1
  11.2 0.0 copy-done.2
  11.2 1.5 %open_sums.1 = (f32[2,2,4,64,256]{4,3,2,1,0:T(8,128)S(1)}, bf16[2,256,256]{2,1,0:T(8,128)(2,1)S(1)}) custom-call(bf16[2,256,256]{2,1,0:T(8,128)(2,1)S(1)} %copy-done, bf16[9,512,256]{2,1,0:T(8,128)(2,1)S(1)} %get-tuple-element.19.cols.refs_1_, bf16[2,1152,256]{2,1,0:T(8,128)(2,1)S(1)} %get-tuple-element.20.rows.refs_2_, f32[2,4,64,256]{3,2,1,0:T(8,128)S(1)} %copy-done.1, ...), custom_call_target="tpu_custom_call" | custom-call | flops 4000000000 | bytes 1 | tf_op jit(solution)/shard_map/open_sums/pallas_call | solution.py:184
  12.7 5.3 %collective-permute-done.got.refs_0_ = bf16[2,256,256]{2,1,0:T(8,128)(2,1)S(1)} collective-permute-done((bf16[2,256,256]{2,1,0:T(8,128)(2,1)}, bf16[2,256,256]{2,1,0:T(8,128)(2,1)S(1)}, u32[]{:S(2)}, u32[]{:S(2)}) %collective-permute-start) | collective-permute-done | bytes 262176 | tf_op jit(solution)/shard_map/ppermute | solution.py:357
  18.0 0.1 route.1
  18.1 1.4 %collective-permute-start.3 = (bf16[2,256,256]{2,1,0:T(8,128)(2,1)S(1)}, bf16[2,256,256]{2,1,0:T(8,128)(2,1)S(1)}, u32[]{:S(2)}, u32[]{:S(2)}) collective-permute-start(bf16[2,256,256]{2,1,0:T(8,128)(2,1)S(1)} %get-tuple-element.26), channel_id=1, source_target_pairs={{0,1},{1,2},{2,3},{3,0},{4,5},{5,6},{6,7},{7,4},{8,9},{9,10},{10,1... | collective-permute-start | bytes 786440 | tf_op jit(solution)/shard_map/ppermute | solution.py:362
  19.5 1.5 %collective-permute-start.2 = (bf16[2,256,256]{2,1,0:T(8,128)(2,1)S(1)}, bf16[2,256,256]{2,1,0:T(8,128)(2,1)S(1)}, u32[]{:S(2)}, u32[]{:S(2)}) collective-permute-start(bf16[2,256,256]{2,1,0:T(8,128)(2,1)S(1)} %get-tuple-element.25), channel_id=1, source_target_pairs={{0,3},{1,0},{2,1},{3,2},{4,7},{5,4},{6,5},{7,6},{8,11},{9,8},{10,9... | collective-permute-start | bytes 786440 | tf_op jit(solution)/shard_map/ppermute | solution.py:362
  21.0 1.9 %spread.3.refs_3_ = f32[4,2,4,64,256]{4,3,2,1,0:T(8,128)S(1)} custom-call(bf16[2,256,256]{2,1,0:T(8,128)(2,1)S(1)} %collective-permute-done.got.refs_0_, bf16[9,512,256]{2,1,0:T(8,128)(2,1)S(1)} %get-tuple-element.19.cols.refs_1_, bf16[2,1152,256]{2,1,0:T(8,128)(2,1)S(1)} %get-tuple-element.20.rows.refs_2_, f32[2,2,4,64,256]{4,3,2,1,0:T(8,128)S(1)} %get-tuple-element.23.refs_3_), custom_call_target="tpu_custom_call" | custom-call | flops 1 | bytes 1 | tf_op jit(solution)/shard_map/spread/pallas_call | solution.py:230
  23.0 1.8 %collective-permute-start.1 = (bf16[2,256,256]{2,1,0:T(8,128)(2,1)S(1)}, bf16[2,256,256]{2,1,0:T(8,128)(2,1)S(1)}, u32[]{:S(2)}, u32[]{:S(2)}) collective-permute-start(bf16[2,256,256]{2,1,0:T(8,128)(2,1)S(1)} %get-tuple-element.24), channel_id=1, source_target_pairs={{0,2},{1,3},{2,0},{3,1},{4,6},{5,7},{6,4},{7,5},{8,10},{9,11},{10,... | collective-permute-start | bytes 786440 | tf_op jit(solution)/shard_map/ppermute | solution.py:362
  24.8 0.0 collective-permute-done.3.refs_0_
  24.8 1.9 %spread.4.refs_3_ = f32[4,2,4,64,256]{4,3,2,1,0:T(8,128)S(1)} custom-call(bf16[2,256,256]{2,1,0:T(8,128)(2,1)S(1)} %collective-permute-done.3.refs_0_, bf16[9,512,256]{2,1,0:T(8,128)(2,1)S(1)} %get-tuple-element.19.cols.refs_1_, bf16[2,1152,256]{2,1,0:T(8,128)(2,1)S(1)} %get-tuple-element.20.rows.refs_2_, f32[4,2,4,64,256]{4,3,2,1,0:T(8,128)S(1)} %spread.3.refs_3_), custom_call_target="tpu_custom_call" | custom-call | flops 1 | bytes 1 | tf_op jit(solution)/shard_map/spread/pallas_call | solution.py:230
  26.7 0.0 collective-permute-done.2.refs_0_
  26.7 1.9 %spread.5 = (f32[2,2,4,64,256]{4,3,2,1,0:T(8,128)S(1)}, bf16[2,2,4,64,256]{4,3,2,1,0:T(8,128)(2,1)S(1)}) custom-call(bf16[2,256,256]{2,1,0:T(8,128)(2,1)S(1)} %collective-permute-done.2.refs_0_, bf16[9,512,256]{2,1,0:T(8,128)(2,1)S(1)} %get-tuple-element.19.cols.refs_1_, bf16[2,1152,256]{2,1,0:T(8,128)(2,1)S(1)} %get-tuple-element.20.rows.refs_2_, ...), custom_call_target="tpu_custom_call" | custom-call | flops 1 | bytes 1 | tf_op jit(solution)/shard_map/spread/pallas_call | solution.py:230
  28.7 6.0 %collective-permute-start.5 = (bf16[2,2,4,64,256]{4,3,2,1,0:T(8,128)(2,1)S(1)}, bf16[2,2,4,64,256]{4,3,2,1,0:T(8,128)(2,1)S(1)}, u32[]{:S(2)}, u32[]{:S(2)}) collective-permute-start(bf16[2,2,4,64,256]{4,3,2,1,0:T(8,128)(2,1)S(1)} %get-tuple-element.35), channel_id=1, source_target_pairs={{0,64},{64,0},{128,192},{192,128},{1,65},{65,1},{129,193},{193,129... | collective-permute-start | bytes 1572872 | tf_op jit(solution)/shard_map/ppermute | solution.py:366
  34.7 0.0 collective-permute-done.1.piece
  34.7 1.4 %collective-permute-start.4 = (bf16[2,256,256]{2,1,0:T(8,128)(2,1)S(1)}, bf16[2,256,256]{2,1,0:T(8,128)(2,1)S(1)}, u32[]{:S(2)}, u32[]{:S(2)}) collective-permute-start(bf16[2,256,256]{2,1,0:T(8,128)(2,1)S(1)} %collective-permute-done.1.piece), channel_id=1, source_target_pairs={{0,64},{64,0},{128,192},{192,128},{1,65},{65,1},{129,193},{193,129... | collective-permute-start | bytes 786440 | tf_op jit(solution)/shard_map/ppermute | solution.py:366
  36.1 1.1 %add.6.sums = f32[2,2,4,64,256]{4,3,2,1,0:T(8,128)S(1)} custom-call(bf16[2,256,256]{2,1,0:T(8,128)(2,1)S(1)} %collective-permute-done.1.piece, bf16[9,512,256]{2,1,0:T(8,128)(2,1)S(1)} %get-tuple-element.19.cols.refs_1_, bf16[2,1152,256]{2,1,0:T(8,128)(2,1)S(1)} %get-tuple-element.20.rows.refs_2_, f32[2,2,4,64,256]{4,3,2,1,0:T(8,128)S(1)} %get-tuple-element.34.before), custom_call_target="tpu_custom_call" | custom-call | flops 1 | bytes 1 | tf_op jit(solution)/shard_map/add/pallas_call | solution.py:252
  37.2 0.1 collective-permute-done.4.piece
  37.3 0.0 collective-permute-done.5.others
  37.3 1.9 %close_sums.1 = (f32[2,4,64,256]{3,2,1,0:T(8,128)}, f32[2,4,64,256]{3,2,1,0:T(8,128)}) custom-call(bf16[2,256,256]{2,1,0:T(8,128)(2,1)S(1)} %collective-permute-done.4.piece, bf16[9,512,256]{2,1,0:T(8,128)(2,1)S(1)} %get-tuple-element.19.cols.refs_1_, bf16[2,1152,256]{2,1,0:T(8,128)(2,1)S(1)} %get-tuple-element.20.rows.refs_2_, ...), custom_call_target="tpu_custom_call" | custom-call | flops 1 | bytes 1 | tf_op jit(solution)/shard_map/close_sums/pallas_call | solution.py:286
Async XLA Ops:
  2.3 15.7 %collective-permute-start = (bf16[2,256,256]{2,1,0:T(8,128)(2,1)}, bf16[2,256,256]{2,1,0:T(8,128)(2,1)S(1)}, u32[]{:S(2)}, u32[]{:S(2)}) collective-permute-start(bf16[2,256,256]{2,1,0:T(8,128)(2,1)} %scale.1.piece), channel_id=1, source_target_pairs={{0,4},{1,5},{2,6},{3,7},{4,8},{5,9},{6,10},{7,11},{8,12},{9,13},{1... | collective-permute-start | bytes 786440 | tf_op jit(solution)/shard_map/ppermute | solution.py:357
  6.2 0.7 %copy-start.3 = (s32[4,256]{1,0:T(4,128)S(1)}, s32[4,256]{1,0:T(4,128)}, u32[]{:S(2)}) copy-start(s32[4,256]{1,0:T(4,128)} %shift_in.1) | copy-start | bytes 12292
  6.8 0.7 %copy-start.4 = (s32[4,256]{1,0:T(4,128)S(1)}, s32[4,256]{1,0:T(4,128)}, u32[]{:S(2)}) copy-start(s32[4,256]{1,0:T(4,128)} %flip_in.1) | copy-start | bytes 12292
  7.5 3.6 %copy-start = (bf16[2,256,256]{2,1,0:T(8,128)(2,1)S(1)}, bf16[2,256,256]{2,1,0:T(8,128)(2,1)}, u32[]{:S(2)}) copy-start(bf16[2,256,256]{2,1,0:T(8,128)(2,1)} %scale.1.piece) | copy-start | bytes 786436
  7.5 3.6 %copy-start.1 = (f32[2,4,64,256]{3,2,1,0:T(8,128)S(1)}, f32[2,4,64,256]{3,2,1,0:T(8,128)}, u32[]{:S(2)}) copy-start(f32[2,4,64,256]{3,2,1,0:T(8,128)} %ph_in.1) | copy-start | bytes 1572868
  7.5 3.6 %copy-start.2 = (f32[2,4,64,256]{3,2,1,0:T(8,128)S(1)}, f32[2,4,64,256]{3,2,1,0:T(8,128)}, u32[]{:S(2)}) copy-start(f32[2,4,64,256]{3,2,1,0:T(8,128)} %pp_in.1) | copy-start | bytes 1572868
  18.1 6.6 %collective-permute-start.3 = (bf16[2,256,256]{2,1,0:T(8,128)(2,1)S(1)}, bf16[2,256,256]{2,1,0:T(8,128)(2,1)S(1)}, u32[]{:S(2)}, u32[]{:S(2)}) collective-permute-start(bf16[2,256,256]{2,1,0:T(8,128)(2,1)S(1)} %get-tuple-element.26), channel_id=1, source_target_pairs={{0,1},{1,2},{2,3},{3,0},{4,5},{5,6},{6,7},{7,4},{8,9},{9,10},{10,1... | collective-permute-start | bytes 786440 | tf_op jit(solution)/shard_map/ppermute | solution.py:362
  19.5 7.2 %collective-permute-start.2 = (bf16[2,256,256]{2,1,0:T(8,128)(2,1)S(1)}, bf16[2,256,256]{2,1,0:T(8,128)(2,1)S(1)}, u32[]{:S(2)}, u32[]{:S(2)}) collective-permute-start(bf16[2,256,256]{2,1,0:T(8,128)(2,1)S(1)} %get-tuple-element.25), channel_id=1, source_target_pairs={{0,3},{1,0},{2,1},{3,2},{4,7},{5,4},{6,5},{7,6},{8,11},{9,8},{10,9... | collective-permute-start | bytes 786440 | tf_op jit(solution)/shard_map/ppermute | solution.py:362
  23.0 11.7 %collective-permute-start.1 = (bf16[2,256,256]{2,1,0:T(8,128)(2,1)S(1)}, bf16[2,256,256]{2,1,0:T(8,128)(2,1)S(1)}, u32[]{:S(2)}, u32[]{:S(2)}) collective-permute-start(bf16[2,256,256]{2,1,0:T(8,128)(2,1)S(1)} %get-tuple-element.24), channel_id=1, source_target_pairs={{0,2},{1,3},{2,0},{3,1},{4,6},{5,7},{6,4},{7,5},{8,10},{9,11},{10,... | collective-permute-start | bytes 786440 | tf_op jit(solution)/shard_map/ppermute | solution.py:362
  28.7 8.6 %collective-permute-start.5 = (bf16[2,2,4,64,256]{4,3,2,1,0:T(8,128)(2,1)S(1)}, bf16[2,2,4,64,256]{4,3,2,1,0:T(8,128)(2,1)S(1)}, u32[]{:S(2)}, u32[]{:S(2)}) collective-permute-start(bf16[2,2,4,64,256]{4,3,2,1,0:T(8,128)(2,1)S(1)} %get-tuple-element.35), channel_id=1, source_target_pairs={{0,64},{64,0},{128,192},{192,128},{1,65},{65,1},{129,193},{193,129... | collective-permute-start | bytes 1572872 | tf_op jit(solution)/shard_map/ppermute | solution.py:366
  34.7 2.6 %collective-permute-start.4 = (bf16[2,256,256]{2,1,0:T(8,128)(2,1)S(1)}, bf16[2,256,256]{2,1,0:T(8,128)(2,1)S(1)}, u32[]{:S(2)}, u32[]{:S(2)}) collective-permute-start(bf16[2,256,256]{2,1,0:T(8,128)(2,1)S(1)} %collective-permute-done.1.piece), channel_id=1, source_target_pairs={{0,64},{64,0},{128,192},{192,128},{1,65},{65,1},{129,193},{193,129... | collective-permute-start | bytes 786440 | tf_op jit(solution)/shard_map/ppermute | solution.py:366

commit v7 on v6

--- a/solution.py
+++ b/solution.py
@@ -349,11 +349,13 @@
 
 
 def planes_back(value):
-    pairs = [
-        (g * BLOCKS + b, g * BLOCKS + (b + PLANE * (1 + g % 2)) % BLOCKS)
-        for g in range(4)
-        for b in range(BLOCKS)
-    ]
+    pairs = []
+    for g in range(4):
+        for b in range(BLOCKS):
+            target = (b + PLANE * (1 + g % 2)) % BLOCKS
+            crosses = target // (BLOCKS // 2) != b // (BLOCKS // 2)
+            chip = g ^ 2 if crosses else g
+            pairs.append((g * BLOCKS + b, chip * BLOCKS + target))
     return lax.ppermute(value, ("grp", "blk"), pairs)
 
 

time: 39.6 us -> 39.3 us (level)
  transfers between devices with their start and end apart: 6 -> 6, of which waited for: 2 -> 2; matrix products, arithmetic and copies ran while one was open for 0% -> 0% of each run, Pallas kernels for 30% -> 31%
where the time goes in v7:
time: 39.3 us; the launch traced here: 39.1 us
  starting transfers between devices  16 us (41%)
  Pallas kernels  15.7 us (40%)
  waiting for transfers between devices  5.17 us (13%)
  local copies, waits for them, and re-layouts  1.38 us (4%)
  between operations  0.89 us (2%)
    ppermute x2, starting transfers between devices, other_core(): return lax.ppermute(value, 'grp', [(s, s ^ 1) for s in range(4)])  7.44 us
    pallas_call x3, Pallas kernels, spread(): pl.pallas_call(functools.partial(spread_kernel, count, fresh, send), out_...  5.78 us
    ppermute x1, waiting for transfers between devices, planes_back(): return lax.ppermute(value, ('grp', 'blk'), pairs)  5.07 us
    ppermute x3, starting transfers between devices, along_y(): return lax.ppermute(value, 'blk', pairs)  4.72 us
    ppermute x1, starting transfers between devices, planes_back(): return lax.ppermute(value, ('grp', 'blk'), pairs)  3.82 us
    pallas_call x1, Pallas kernels, tables(): pl.pallas_call(table_kernel, out_shape=(jax.ShapeDtypeStruct((2 * TRANS +...  3.61 us
    pallas_call x1, Pallas kernels, close_sums(): pl.pallas_call(close_kernel, out_shape=(jax.ShapeDtypeStruct(SUMS, F32),)...  1.95 us
    pallas_call x1, Pallas kernels, scale(): pl.pallas_call(scale_kernel, out_shape=jax.ShapeDtypeStruct(PIECE, BF), i...  1.71 us
  transfers between devices with their start and end apart: 6, of which 2 were waited for; matrix products, arithmetic and copies ran while one was open for 0% of the time, Pallas kernels for 31%

profile of v7, /device:TPU:1, one launch (start us, length us, event | category | flops | bytes accessed | tf_op | source)
XLA Modules:
  0.0 39.1 jit_solution(16279735905884141284)
XLA Ops:
  0.6 1.7 %scale.1.piece = bf16[2,256,256]{2,1,0:T(8,128)(2,1)} custom-call(bf16[1,2,256,256]{3,2,1,0:T(8,128)(2,1)} %masses.1, s32[1,256]{1,0:T(1,128)} %spins.1), custom_call_target="tpu_custom_call" | custom-call | flops 1 | bytes 1 | tf_op jit(solution)/shard_map/scale/pallas_call | solution.py:306
  2.3 3.8 %collective-permute-start = (bf16[2,256,256]{2,1,0:T(8,128)(2,1)}, bf16[2,256,256]{2,1,0:T(8,128)(2,1)S(1)}, u32[]{:S(2)}, u32[]{:S(2)}) collective-permute-start(bf16[2,256,256]{2,1,0:T(8,128)(2,1)} %scale.1.piece), channel_id=1, source_target_pairs={{0,4},{1,5},{2,6},{3,7},{4,8},{5,9},{6,10},{7,11},{8,12},{9,13},{1... | collective-permute-start | bytes 786440 | tf_op jit(solution)/shard_map/ppermute | solution.py:359
  6.2 0.0 copy-start.3
  6.2 0.7 %copy-done.3 = s32[4,256]{1,0:T(4,128)S(1)} copy-done((s32[4,256]{1,0:T(4,128)S(1)}, s32[4,256]{1,0:T(4,128)}, u32[]{:S(2)}) %copy-start.3) | copy-done | bytes 4120
  6.8 0.0 copy-start.4
  6.8 0.7 %copy-done.4 = s32[4,256]{1,0:T(4,128)S(1)} copy-done((s32[4,256]{1,0:T(4,128)S(1)}, s32[4,256]{1,0:T(4,128)}, u32[]{:S(2)}) %copy-start.4) | copy-done | bytes 4120
  7.5 0.0 copy-start
  7.5 0.0 copy-start.1
  7.5 0.0 copy-start.2
  7.5 3.6 %tables.1 = (bf16[9,512,256]{2,1,0:T(8,128)(2,1)S(1)}, bf16[2,1152,256]{2,1,0:T(8,128)(2,1)S(1)}) custom-call(s32[1]{0:T(128)} %bitcast.place_ref.place, s32[4,256]{1,0:T(4,128)S(1)} %copy-done.3, s32[4,256]{1,0:T(4,128)S(1)} %copy-done.4), custom_call_target="tpu_custom_call" | custom-call | flops 4000000000 | bytes 1 | tf_op jit(solution)/shard_map/tables/pallas_call | solution.py:83
  11.2 0.0 copy-done
  11.2 0.0 copy-done.1
  11.2 0.0 copy-done.2
  11.2 1.5 %open_sums.1 = (f32[2,2,4,64,256]{4,3,2,1,0:T(8,128)S(1)}, bf16[2,256,256]{2,1,0:T(8,128)(2,1)S(1)}) custom-call(bf16[2,256,256]{2,1,0:T(8,128)(2,1)S(1)} %copy-done, bf16[9,512,256]{2,1,0:T(8,128)(2,1)S(1)} %get-tuple-element.19.cols.refs_1_, bf16[2,1152,256]{2,1,0:T(8,128)(2,1)S(1)} %get-tuple-element.20.rows.refs_2_, f32[2,4,64,256]{3,2,1,0:T(8,128)S(1)} %copy-done.1, ...), custom_call_target="tpu_custom_call" | custom-call | flops 4000000000 | bytes 1 | tf_op jit(solution)/shard_map/open_sums/pallas_call | solution.py:184
  12.7 5.1 %collective-permute-done.got.refs_0_ = bf16[2,256,256]{2,1,0:T(8,128)(2,1)S(1)} collective-permute-done((bf16[2,256,256]{2,1,0:T(8,128)(2,1)}, bf16[2,256,256]{2,1,0:T(8,128)(2,1)S(1)}, u32[]{:S(2)}, u32[]{:S(2)}) %collective-permute-start) | collective-permute-done | bytes 262176 | tf_op jit(solution)/shard_map/ppermute | solution.py:359
  17.8 0.1 route.1
  17.9 1.4 %collective-permute-start.3 = (bf16[2,256,256]{2,1,0:T(8,128)(2,1)S(1)}, bf16[2,256,256]{2,1,0:T(8,128)(2,1)S(1)}, u32[]{:S(2)}, u32[]{:S(2)}) collective-permute-start(bf16[2,256,256]{2,1,0:T(8,128)(2,1)S(1)} %get-tuple-element.26), channel_id=1, source_target_pairs={{0,1},{1,2},{2,3},{3,0},{4,5},{5,6},{6,7},{7,4},{8,9},{9,10},{10,1... | collective-permute-start | bytes 786440 | tf_op jit(solution)/shard_map/ppermute | solution.py:364
  19.2 1.5 %collective-permute-start.2 = (bf16[2,256,256]{2,1,0:T(8,128)(2,1)S(1)}, bf16[2,256,256]{2,1,0:T(8,128)(2,1)S(1)}, u32[]{:S(2)}, u32[]{:S(2)}) collective-permute-start(bf16[2,256,256]{2,1,0:T(8,128)(2,1)S(1)} %get-tuple-element.25), channel_id=1, source_target_pairs={{0,3},{1,0},{2,1},{3,2},{4,7},{5,4},{6,5},{7,6},{8,11},{9,8},{10,9... | collective-permute-start | bytes 786440 | tf_op jit(solution)/shard_map/ppermute | solution.py:364
  20.8 1.9 %spread.3.refs_3_ = f32[4,2,4,64,256]{4,3,2,1,0:T(8,128)S(1)} custom-call(bf16[2,256,256]{2,1,0:T(8,128)(2,1)S(1)} %collective-permute-done.got.refs_0_, bf16[9,512,256]{2,1,0:T(8,128)(2,1)S(1)} %get-tuple-element.19.cols.refs_1_, bf16[2,1152,256]{2,1,0:T(8,128)(2,1)S(1)} %get-tuple-element.20.rows.refs_2_, f32[2,2,4,64,256]{4,3,2,1,0:T(8,128)S(1)} %get-tuple-element.23.refs_3_), custom_call_target="tpu_custom_call" | custom-call | flops 1 | bytes 1 | tf_op jit(solution)/shard_map/spread/pallas_call | solution.py:230
  22.7 1.8 %collective-permute-start.1 = (bf16[2,256,256]{2,1,0:T(8,128)(2,1)S(1)}, bf16[2,256,256]{2,1,0:T(8,128)(2,1)S(1)}, u32[]{:S(2)}, u32[]{:S(2)}) collective-permute-start(bf16[2,256,256]{2,1,0:T(8,128)(2,1)S(1)} %get-tuple-element.24), channel_id=1, source_target_pairs={{0,2},{1,3},{2,0},{3,1},{4,6},{5,7},{6,4},{7,5},{8,10},{9,11},{10,... | collective-permute-start | bytes 786440 | tf_op jit(solution)/shard_map/ppermute | solution.py:364
  24.5 0.0 collective-permute-done.3.refs_0_
  24.5 1.9 %spread.4.refs_3_ = f32[4,2,4,64,256]{4,3,2,1,0:T(8,128)S(1)} custom-call(bf16[2,256,256]{2,1,0:T(8,128)(2,1)S(1)} %collective-permute-done.3.refs_0_, bf16[9,512,256]{2,1,0:T(8,128)(2,1)S(1)} %get-tuple-element.19.cols.refs_1_, bf16[2,1152,256]{2,1,0:T(8,128)(2,1)S(1)} %get-tuple-element.20.rows.refs_2_, f32[4,2,4,64,256]{4,3,2,1,0:T(8,128)S(1)} %spread.3.refs_3_), custom_call_target="tpu_custom_call" | custom-call | flops 1 | bytes 1 | tf_op jit(solution)/shard_map/spread/pallas_call | solution.py:230
  26.5 0.0 collective-permute-done.2.refs_0_
  26.5 1.9 %spread.5 = (f32[2,2,4,64,256]{4,3,2,1,0:T(8,128)S(1)}, bf16[2,2,4,64,256]{4,3,2,1,0:T(8,128)(2,1)S(1)}) custom-call(bf16[2,256,256]{2,1,0:T(8,128)(2,1)S(1)} %collective-permute-done.2.refs_0_, bf16[9,512,256]{2,1,0:T(8,128)(2,1)S(1)} %get-tuple-element.19.cols.refs_1_, bf16[2,1152,256]{2,1,0:T(8,128)(2,1)S(1)} %get-tuple-element.20.rows.refs_2_, ...), custom_call_target="tpu_custom_call" | custom-call | flops 1 | bytes 1 | tf_op jit(solution)/shard_map/spread/pallas_call | solution.py:230
  28.4 6.0 %collective-permute-start.5 = (bf16[2,2,4,64,256]{4,3,2,1,0:T(8,128)(2,1)S(1)}, bf16[2,2,4,64,256]{4,3,2,1,0:T(8,128)(2,1)S(1)}, u32[]{:S(2)}, u32[]{:S(2)}) collective-permute-start(bf16[2,2,4,64,256]{4,3,2,1,0:T(8,128)(2,1)S(1)} %get-tuple-element.35), channel_id=1, source_target_pairs={{0,64},{64,0},{128,192},{192,128},{1,65},{65,1},{129,193},{193,129... | collective-permute-start | bytes 1572872 | tf_op jit(solution)/shard_map/ppermute | solution.py:368
  34.4 0.0 collective-permute-done.1.piece
  34.4 1.4 %collective-permute-start.4 = (bf16[2,256,256]{2,1,0:T(8,128)(2,1)S(1)}, bf16[2,256,256]{2,1,0:T(8,128)(2,1)S(1)}, u32[]{:S(2)}, u32[]{:S(2)}) collective-permute-start(bf16[2,256,256]{2,1,0:T(8,128)(2,1)S(1)} %collective-permute-done.1.piece), channel_id=1, source_target_pairs={{0,64},{64,0},{128,192},{192,128},{1,65},{65,1},{129,193},{193,129... | collective-permute-start | bytes 786440 | tf_op jit(solution)/shard_map/ppermute | solution.py:368
  35.9 1.1 %add.6.sums = f32[2,2,4,64,256]{4,3,2,1,0:T(8,128)S(1)} custom-call(bf16[2,256,256]{2,1,0:T(8,128)(2,1)S(1)} %collective-permute-done.1.piece, bf16[9,512,256]{2,1,0:T(8,128)(2,1)S(1)} %get-tuple-element.19.cols.refs_1_, bf16[2,1152,256]{2,1,0:T(8,128)(2,1)S(1)} %get-tuple-element.20.rows.refs_2_, f32[2,2,4,64,256]{4,3,2,1,0:T(8,128)S(1)} %get-tuple-element.34.before), custom_call_target="tpu_custom_call" | custom-call | flops 1 | bytes 1 | tf_op jit(solution)/shard_map/add/pallas_call | solution.py:252
  36.9 0.1 collective-permute-done.4.piece
  37.0 0.0 collective-permute-done.5.others
  37.0 1.9 %close_sums.1 = (f32[2,4,64,256]{3,2,1,0:T(8,128)}, f32[2,4,64,256]{3,2,1,0:T(8,128)}) custom-call(bf16[2,256,256]{2,1,0:T(8,128)(2,1)S(1)} %collective-permute-done.4.piece, bf16[9,512,256]{2,1,0:T(8,128)(2,1)S(1)} %get-tuple-element.19.cols.refs_1_, bf16[2,1152,256]{2,1,0:T(8,128)(2,1)S(1)} %get-tuple-element.20.rows.refs_2_, ...), custom_call_target="tpu_custom_call" | custom-call | flops 1 | bytes 1 | tf_op jit(solution)/shard_map/close_sums/pallas_call | solution.py:286
Async XLA Ops:
  2.3 15.4 %collective-permute-start = (bf16[2,256,256]{2,1,0:T(8,128)(2,1)}, bf16[2,256,256]{2,1,0:T(8,128)(2,1)S(1)}, u32[]{:S(2)}, u32[]{:S(2)}) collective-permute-start(bf16[2,256,256]{2,1,0:T(8,128)(2,1)} %scale.1.piece), channel_id=1, source_target_pairs={{0,4},{1,5},{2,6},{3,7},{4,8},{5,9},{6,10},{7,11},{8,12},{9,13},{1... | collective-permute-start | bytes 786440 | tf_op jit(solution)/shard_map/ppermute | solution.py:359
  6.2 0.7 %copy-start.3 = (s32[4,256]{1,0:T(4,128)S(1)}, s32[4,256]{1,0:T(4,128)}, u32[]{:S(2)}) copy-start(s32[4,256]{1,0:T(4,128)} %shift_in.1) | copy-start | bytes 12292
  6.8 0.7 %copy-start.4 = (s32[4,256]{1,0:T(4,128)S(1)}, s32[4,256]{1,0:T(4,128)}, u32[]{:S(2)}) copy-start(s32[4,256]{1,0:T(4,128)} %flip_in.1) | copy-start | bytes 12292
  7.5 3.6 %copy-start = (bf16[2,256,256]{2,1,0:T(8,128)(2,1)S(1)}, bf16[2,256,256]{2,1,0:T(8,128)(2,1)}, u32[]{:S(2)}) copy-start(bf16[2,256,256]{2,1,0:T(8,128)(2,1)} %scale.1.piece) | copy-start | bytes 786436
  7.5 3.6 %copy-start.1 = (f32[2,4,64,256]{3,2,1,0:T(8,128)S(1)}, f32[2,4,64,256]{3,2,1,0:T(8,128)}, u32[]{:S(2)}) copy-start(f32[2,4,64,256]{3,2,1,0:T(8,128)} %ph_in.1) | copy-start | bytes 1572868
  7.5 3.6 %copy-start.2 = (f32[2,4,64,256]{3,2,1,0:T(8,128)S(1)}, f32[2,4,64,256]{3,2,1,0:T(8,128)}, u32[]{:S(2)}) copy-start(f32[2,4,64,256]{3,2,1,0:T(8,128)} %pp_in.1) | copy-start | bytes 1572868
  17.9 6.6 %collective-permute-start.3 = (bf16[2,256,256]{2,1,0:T(8,128)(2,1)S(1)}, bf16[2,256,256]{2,1,0:T(8,128)(2,1)S(1)}, u32[]{:S(2)}, u32[]{:S(2)}) collective-permute-start(bf16[2,256,256]{2,1,0:T(8,128)(2,1)S(1)} %get-tuple-element.26), channel_id=1, source_target_pairs={{0,1},{1,2},{2,3},{3,0},{4,5},{5,6},{6,7},{7,4},{8,9},{9,10},{10,1... | collective-permute-start | bytes 786440 | tf_op jit(solution)/shard_map/ppermute | solution.py:364
  19.2 7.2 %collective-permute-start.2 = (bf16[2,256,256]{2,1,0:T(8,128)(2,1)S(1)}, bf16[2,256,256]{2,1,0:T(8,128)(2,1)S(1)}, u32[]{:S(2)}, u32[]{:S(2)}) collective-permute-start(bf16[2,256,256]{2,1,0:T(8,128)(2,1)S(1)} %get-tuple-element.25), channel_id=1, source_target_pairs={{0,3},{1,0},{2,1},{3,2},{4,7},{5,4},{6,5},{7,6},{8,11},{9,8},{10,9... | collective-permute-start | bytes 786440 | tf_op jit(solution)/shard_map/ppermute | solution.py:364
  22.7 11.7 %collective-permute-start.1 = (bf16[2,256,256]{2,1,0:T(8,128)(2,1)S(1)}, bf16[2,256,256]{2,1,0:T(8,128)(2,1)S(1)}, u32[]{:S(2)}, u32[]{:S(2)}) collective-permute-start(bf16[2,256,256]{2,1,0:T(8,128)(2,1)S(1)} %get-tuple-element.24), channel_id=1, source_target_pairs={{0,2},{1,3},{2,0},{3,1},{4,6},{5,7},{6,4},{7,5},{8,10},{9,11},{10,... | collective-permute-start | bytes 786440 | tf_op jit(solution)/shard_map/ppermute | solution.py:364
  28.4 8.6 %collective-permute-start.5 = (bf16[2,2,4,64,256]{4,3,2,1,0:T(8,128)(2,1)S(1)}, bf16[2,2,4,64,256]{4,3,2,1,0:T(8,128)(2,1)S(1)}, u32[]{:S(2)}, u32[]{:S(2)}) collective-permute-start(bf16[2,2,4,64,256]{4,3,2,1,0:T(8,128)(2,1)S(1)} %get-tuple-element.35), channel_id=1, source_target_pairs={{0,64},{64,0},{128,192},{192,128},{1,65},{65,1},{129,193},{193,129... | collective-permute-start | bytes 1572872 | tf_op jit(solution)/shard_map/ppermute | solution.py:368
  34.4 2.6 %collective-permute-start.4 = (bf16[2,256,256]{2,1,0:T(8,128)(2,1)S(1)}, bf16[2,256,256]{2,1,0:T(8,128)(2,1)S(1)}, u32[]{:S(2)}, u32[]{:S(2)}) collective-permute-start(bf16[2,256,256]{2,1,0:T(8,128)(2,1)S(1)} %collective-permute-done.1.piece), channel_id=1, source_target_pairs={{0,64},{64,0},{128,192},{192,128},{1,65},{65,1},{129,193},{193,129... | collective-permute-start | bytes 786440 | tf_op jit(solution)/shard_map/ppermute | solution.py:368

commit v8 on v7

--- a/solution.py
+++ b/solution.py
@@ -378,7 +378,6 @@
     right, left, middle = route(place, y, kept, got, (1, 3, 2))
     right, left = along_y(right, 1), along_y(left, 3)
     (sums,) = spread([got], cols, rows, sums)
-    middle, sums = lax.optimization_barrier((middle, sums))
     middle = along_y(middle, 2)
     right, sums = lax.optimization_barrier((right, sums))
     (sums,) = spread([right], cols, rows, sums)

time: 39.3 us -> 40 us (1.018)
  waiting for transfers between devices: 5.17 us -> 6.02 us
    ppermute x2, waiting for transfers between devices: 0.09 us -> 0.73 us  [other_core(): return lax.ppermute(value, 'grp', [(s, s ^ 1) for s in range(4)])]
  transfers between devices with their start and end apart: 6 -> 6, of which waited for: 2 -> 3; matrix products, arithmetic and copies ran while one was open for 0% -> 0% of each run, Pallas kernels for 31% -> 30%
where the time goes in v8:
time: 40 us; the launch traced here: 39.8 us
  starting transfers between devices  15.8 us (40%)
  Pallas kernels  15.7 us (39%)
  waiting for transfers between devices  6.02 us (15%)
  local copies, waits for them, and re-layouts  1.38 us (3%)
  between operations  0.89 us (2%)
    ppermute x2, starting transfers between devices, other_core(): return lax.ppermute(value, 'grp', [(s, s ^ 1) for s in range(4)])  7.55 us
    pallas_call x3, Pallas kernels, spread(): pl.pallas_call(functools.partial(spread_kernel, count, fresh, send), out_...  5.78 us
    ppermute x1, waiting for transfers between devices, planes_back(): return lax.ppermute(value, ('grp', 'blk'), pairs)  5.07 us
    ppermute x3, starting transfers between devices, along_y(): return lax.ppermute(value, 'blk', pairs)  4.46 us
    ppermute x1, starting transfers between devices, planes_back(): return lax.ppermute(value, ('grp', 'blk'), pairs)  3.82 us
    pallas_call x1, Pallas kernels, tables(): pl.pallas_call(table_kernel, out_shape=(jax.ShapeDtypeStruct((2 * TRANS +...  3.61 us
    pallas_call x1, Pallas kernels, close_sums(): pl.pallas_call(close_kernel, out_shape=(jax.ShapeDtypeStruct(SUMS, F32),)...  1.95 us
    pallas_call x1, Pallas kernels, scale(): pl.pallas_call(scale_kernel, out_shape=jax.ShapeDtypeStruct(PIECE, BF), i...  1.71 us
  transfers between devices with their start and end apart: 6, of which 3 were waited for; matrix products, arithmetic and copies ran while one was open for 0% of the time, Pallas kernels for 30%

profile of v8, /device:TPU:1, one launch (start us, length us, event | category | flops | bytes accessed | tf_op | source)
XLA Modules:
  0.0 39.8 jit_solution(5628468298098279489)
XLA Ops:
  0.6 1.7 %scale.1.piece = bf16[2,256,256]{2,1,0:T(8,128)(2,1)} custom-call(bf16[1,2,256,256]{3,2,1,0:T(8,128)(2,1)} %masses.1, s32[1,256]{1,0:T(1,128)} %spins.1), custom_call_target="tpu_custom_call" | custom-call | flops 1 | bytes 1 | tf_op jit(solution)/shard_map/scale/pallas_call | solution.py:306
  2.3 3.8 %collective-permute-start = (bf16[2,256,256]{2,1,0:T(8,128)(2,1)}, bf16[2,256,256]{2,1,0:T(8,128)(2,1)S(1)}, u32[]{:S(2)}, u32[]{:S(2)}) collective-permute-start(bf16[2,256,256]{2,1,0:T(8,128)(2,1)} %scale.1.piece), channel_id=1, source_target_pairs={{0,4},{1,5},{2,6},{3,7},{4,8},{5,9},{6,10},{7,11},{8,12},{9,13},{1... | collective-permute-start | bytes 786440 | tf_op jit(solution)/shard_map/ppermute | solution.py:359
  6.2 0.0 copy-start.3
  6.2 0.7 %copy-done.3 = s32[4,256]{1,0:T(4,128)S(1)} copy-done((s32[4,256]{1,0:T(4,128)S(1)}, s32[4,256]{1,0:T(4,128)}, u32[]{:S(2)}) %copy-start.3) | copy-done | bytes 4120
  6.8 0.0 copy-start.4
  6.8 0.7 %copy-done.4 = s32[4,256]{1,0:T(4,128)S(1)} copy-done((s32[4,256]{1,0:T(4,128)S(1)}, s32[4,256]{1,0:T(4,128)}, u32[]{:S(2)}) %copy-start.4) | copy-done | bytes 4120
  7.5 0.0 copy-start
  7.5 0.0 copy-start.1
  7.5 0.0 copy-start.2
  7.5 3.6 %tables.1 = (bf16[9,512,256]{2,1,0:T(8,128)(2,1)S(1)}, bf16[2,1152,256]{2,1,0:T(8,128)(2,1)S(1)}) custom-call(s32[1]{0:T(128)} %bitcast.place_ref.place, s32[4,256]{1,0:T(4,128)S(1)} %copy-done.3, s32[4,256]{1,0:T(4,128)S(1)} %copy-done.4), custom_call_target="tpu_custom_call" | custom-call | flops 4000000000 | bytes 1 | tf_op jit(solution)/shard_map/tables/pallas_call | solution.py:83
  11.2 0.0 copy-done
  11.2 0.0 copy-done.1
  11.2 0.0 copy-done.2
  11.2 1.5 %open_sums.1 = (f32[2,2,4,64,256]{4,3,2,1,0:T(8,128)S(1)}, bf16[2,256,256]{2,1,0:T(8,128)(2,1)S(1)}) custom-call(bf16[2,256,256]{2,1,0:T(8,128)(2,1)S(1)} %copy-done, bf16[9,512,256]{2,1,0:T(8,128)(2,1)S(1)} %get-tuple-element.17.cols.refs_1_, bf16[2,1152,256]{2,1,0:T(8,128)(2,1)S(1)} %get-tuple-element.18.rows.refs_2_, f32[2,4,64,256]{3,2,1,0:T(8,128)S(1)} %copy-done.1, ...), custom_call_target="tpu_custom_call" | custom-call | flops 4000000000 | bytes 1 | tf_op jit(solution)/shard_map/open_sums/pallas_call | solution.py:184
  12.7 5.1 %collective-permute-done.got.refs_0_ = bf16[2,256,256]{2,1,0:T(8,128)(2,1)S(1)} collective-permute-done((bf16[2,256,256]{2,1,0:T(8,128)(2,1)}, bf16[2,256,256]{2,1,0:T(8,128)(2,1)S(1)}, u32[]{:S(2)}, u32[]{:S(2)}) %collective-permute-start) | collective-permute-done | bytes 262176 | tf_op jit(solution)/shard_map/ppermute | solution.py:359
  17.8 0.1 route.1
  17.9 1.4 %collective-permute-start.3 = (bf16[2,256,256]{2,1,0:T(8,128)(2,1)S(1)}, bf16[2,256,256]{2,1,0:T(8,128)(2,1)S(1)}, u32[]{:S(2)}, u32[]{:S(2)}) collective-permute-start(bf16[2,256,256]{2,1,0:T(8,128)(2,1)S(1)} %get-tuple-element.22), channel_id=1, source_target_pairs={{0,1},{1,2},{2,3},{3,0},{4,5},{5,6},{6,7},{7,4},{8,9},{9,10},{10,1... | collective-permute-start | bytes 786440 | tf_op jit(solution)/shard_map/ppermute | solution.py:364
  19.2 1.5 %collective-permute-start.2 = (bf16[2,256,256]{2,1,0:T(8,128)(2,1)S(1)}, bf16[2,256,256]{2,1,0:T(8,128)(2,1)S(1)}, u32[]{:S(2)}, u32[]{:S(2)}) collective-permute-start(bf16[2,256,256]{2,1,0:T(8,128)(2,1)S(1)} %get-tuple-element.21), channel_id=1, source_target_pairs={{0,3},{1,0},{2,1},{3,2},{4,7},{5,4},{6,5},{7,6},{8,11},{9,8},{10,9... | collective-permute-start | bytes 786440 | tf_op jit(solution)/shard_map/ppermute | solution.py:364
  20.8 1.6 %collective-permute-start.1 = (bf16[2,256,256]{2,1,0:T(8,128)(2,1)S(1)}, bf16[2,256,256]{2,1,0:T(8,128)(2,1)S(1)}, u32[]{:S(2)}, u32[]{:S(2)}) collective-permute-start(bf16[2,256,256]{2,1,0:T(8,128)(2,1)S(1)} %get-tuple-element.20), channel_id=1, source_target_pairs={{0,2},{1,3},{2,0},{3,1},{4,6},{5,7},{6,4},{7,5},{8,10},{9,11},{10,... | collective-permute-start | bytes 786440 | tf_op jit(solution)/shard_map/ppermute | solution.py:364
  22.3 1.9 %spread.3.refs_3_ = f32[4,2,4,64,256]{4,3,2,1,0:T(8,128)S(1)} custom-call(bf16[2,256,256]{2,1,0:T(8,128)(2,1)S(1)} %collective-permute-done.got.refs_0_, bf16[9,512,256]{2,1,0:T(8,128)(2,1)S(1)} %get-tuple-element.17.cols.refs_1_, bf16[2,1152,256]{2,1,0:T(8,128)(2,1)S(1)} %get-tuple-element.18.rows.refs_2_, f32[2,2,4,64,256]{4,3,2,1,0:T(8,128)S(1)} %get-tuple-element.23.refs_3_), custom_call_target="tpu_custom_call" | custom-call | flops 1 | bytes 1 | tf_op jit(solution)/shard_map/spread/pallas_call | solution.py:230
  24.2 0.2 collective-permute-done.3.refs_0_
  24.4 1.9 %spread.4.refs_3_ = f32[4,2,4,64,256]{4,3,2,1,0:T(8,128)S(1)} custom-call(bf16[2,256,256]{2,1,0:T(8,128)(2,1)S(1)} %collective-permute-done.3.refs_0_, bf16[9,512,256]{2,1,0:T(8,128)(2,1)S(1)} %get-tuple-element.17.cols.refs_1_, bf16[2,1152,256]{2,1,0:T(8,128)(2,1)S(1)} %get-tuple-element.18.rows.refs_2_, f32[4,2,4,64,256]{4,3,2,1,0:T(8,128)S(1)} %spread.3.refs_3_), custom_call_target="tpu_custom_call" | custom-call | flops 1 | bytes 1 | tf_op jit(solution)/shard_map/spread/pallas_call | solution.py:230
  26.4 0.0 collective-permute-done.2.refs_0_
  26.4 1.9 %spread.5 = (f32[2,2,4,64,256]{4,3,2,1,0:T(8,128)S(1)}, bf16[2,2,4,64,256]{4,3,2,1,0:T(8,128)(2,1)S(1)}) custom-call(bf16[2,256,256]{2,1,0:T(8,128)(2,1)S(1)} %collective-permute-done.2.refs_0_, bf16[9,512,256]{2,1,0:T(8,128)(2,1)S(1)} %get-tuple-element.17.cols.refs_1_, bf16[2,1152,256]{2,1,0:T(8,128)(2,1)S(1)} %get-tuple-element.18.rows.refs_2_, ...), custom_call_target="tpu_custom_call" | custom-call | flops 1 | bytes 1 | tf_op jit(solution)/shard_map/spread/pallas_call | solution.py:230
  28.3 7.4 %collective-permute-start.5 = (bf16[2,2,4,64,256]{4,3,2,1,0:T(8,128)(2,1)S(1)}, bf16[2,2,4,64,256]{4,3,2,1,0:T(8,128)(2,1)S(1)}, u32[]{:S(2)}, u32[]{:S(2)}) collective-permute-start(bf16[2,2,4,64,256]{4,3,2,1,0:T(8,128)(2,1)S(1)} %get-tuple-element.31), channel_id=1, source_target_pairs={{0,64},{64,0},{128,192},{192,128},{1,65},{65,1},{129,193},{193,129... | collective-permute-start | bytes 1572872 | tf_op jit(solution)/shard_map/ppermute | solution.py:368
  35.8 0.0 collective-permute-done.1.piece
  35.8 0.1 collective-permute-start.4
  35.9 1.1 %add.6.sums = f32[2,2,4,64,256]{4,3,2,1,0:T(8,128)S(1)} custom-call(bf16[2,256,256]{2,1,0:T(8,128)(2,1)S(1)} %collective-permute-done.1.piece, bf16[9,512,256]{2,1,0:T(8,128)(2,1)S(1)} %get-tuple-element.17.cols.refs_1_, bf16[2,1152,256]{2,1,0:T(8,128)(2,1)S(1)} %get-tuple-element.18.rows.refs_2_, f32[2,2,4,64,256]{4,3,2,1,0:T(8,128)S(1)} %get-tuple-element.30.before), custom_call_target="tpu_custom_call" | custom-call | flops 1 | bytes 1 | tf_op jit(solution)/shard_map/add/pallas_call | solution.py:252
  37.0 0.7 %collective-permute-done.4.piece = bf16[2,256,256]{2,1,0:T(8,128)(2,1)S(1)} collective-permute-done((bf16[2,256,256]{2,1,0:T(8,128)(2,1)S(1)}, bf16[2,256,256]{2,1,0:T(8,128)(2,1)S(1)}, u32[]{:S(2)}, u32[]{:S(2)}) %collective-permute-start.4) | collective-permute-done | bytes 262176 | tf_op jit(solution)/shard_map/ppermute | solution.py:368
  37.7 0.0 collective-permute-done.5.others
  37.7 2.0 %close_sums.1 = (f32[2,4,64,256]{3,2,1,0:T(8,128)}, f32[2,4,64,256]{3,2,1,0:T(8,128)}) custom-call(bf16[2,256,256]{2,1,0:T(8,128)(2,1)S(1)} %collective-permute-done.4.piece, bf16[9,512,256]{2,1,0:T(8,128)(2,1)S(1)} %get-tuple-element.17.cols.refs_1_, bf16[2,1152,256]{2,1,0:T(8,128)(2,1)S(1)} %get-tuple-element.18.rows.refs_2_, ...), custom_call_target="tpu_custom_call" | custom-call | flops 1 | bytes 1 | tf_op jit(solution)/shard_map/close_sums/pallas_call | solution.py:286
Async XLA Ops:
  2.3 15.4 %collective-permute-start = (bf16[2,256,256]{2,1,0:T(8,128)(2,1)}, bf16[2,256,256]{2,1,0:T(8,128)(2,1)S(1)}, u32[]{:S(2)}, u32[]{:S(2)}) collective-permute-start(bf16[2,256,256]{2,1,0:T(8,128)(2,1)} %scale.1.piece), channel_id=1, source_target_pairs={{0,4},{1,5},{2,6},{3,7},{4,8},{5,9},{6,10},{7,11},{8,12},{9,13},{1... | collective-permute-start | bytes 786440 | tf_op jit(solution)/shard_map/ppermute | solution.py:359
  6.2 0.7 %copy-start.3 = (s32[4,256]{1,0:T(4,128)S(1)}, s32[4,256]{1,0:T(4,128)}, u32[]{:S(2)}) copy-start(s32[4,256]{1,0:T(4,128)} %shift_in.1) | copy-start | bytes 12292
  6.8 0.7 %copy-start.4 = (s32[4,256]{1,0:T(4,128)S(1)}, s32[4,256]{1,0:T(4,128)}, u32[]{:S(2)}) copy-start(s32[4,256]{1,0:T(4,128)} %flip_in.1) | copy-start | bytes 12292
  7.5 3.6 %copy-start = (bf16[2,256,256]{2,1,0:T(8,128)(2,1)S(1)}, bf16[2,256,256]{2,1,0:T(8,128)(2,1)}, u32[]{:S(2)}) copy-start(bf16[2,256,256]{2,1,0:T(8,128)(2,1)} %scale.1.piece) | copy-start | bytes 786436
  7.5 3.6 %copy-start.1 = (f32[2,4,64,256]{3,2,1,0:T(8,128)S(1)}, f32[2,4,64,256]{3,2,1,0:T(8,128)}, u32[]{:S(2)}) copy-start(f32[2,4,64,256]{3,2,1,0:T(8,128)} %ph_in.1) | copy-start | bytes 1572868
  7.5 3.6 %copy-start.2 = (f32[2,4,64,256]{3,2,1,0:T(8,128)S(1)}, f32[2,4,64,256]{3,2,1,0:T(8,128)}, u32[]{:S(2)}) copy-start(f32[2,4,64,256]{3,2,1,0:T(8,128)} %pp_in.1) | copy-start | bytes 1572868
  17.9 6.6 %collective-permute-start.3 = (bf16[2,256,256]{2,1,0:T(8,128)(2,1)S(1)}, bf16[2,256,256]{2,1,0:T(8,128)(2,1)S(1)}, u32[]{:S(2)}, u32[]{:S(2)}) collective-permute-start(bf16[2,256,256]{2,1,0:T(8,128)(2,1)S(1)} %get-tuple-element.22), channel_id=1, source_target_pairs={{0,1},{1,2},{2,3},{3,0},{4,5},{5,6},{6,7},{7,4},{8,9},{9,10},{10,1... | collective-permute-start | bytes 786440 | tf_op jit(solution)/shard_map/ppermute | solution.py:364
  19.2 7.2 %collective-permute-start.2 = (bf16[2,256,256]{2,1,0:T(8,128)(2,1)S(1)}, bf16[2,256,256]{2,1,0:T(8,128)(2,1)S(1)}, u32[]{:S(2)}, u32[]{:S(2)}) collective-permute-start(bf16[2,256,256]{2,1,0:T(8,128)(2,1)S(1)} %get-tuple-element.21), channel_id=1, source_target_pairs={{0,3},{1,0},{2,1},{3,2},{4,7},{5,4},{6,5},{7,6},{8,11},{9,8},{10,9... | collective-permute-start | bytes 786440 | tf_op jit(solution)/shard_map/ppermute | solution.py:364
  20.8 15.0 %collective-permute-start.1 = (bf16[2,256,256]{2,1,0:T(8,128)(2,1)S(1)}, bf16[2,256,256]{2,1,0:T(8,128)(2,1)S(1)}, u32[]{:S(2)}, u32[]{:S(2)}) collective-permute-start(bf16[2,256,256]{2,1,0:T(8,128)(2,1)S(1)} %get-tuple-element.20), channel_id=1, source_target_pairs={{0,2},{1,3},{2,0},{3,1},{4,6},{5,7},{6,4},{7,5},{8,10},{9,11},{10,... | collective-permute-start | bytes 786440 | tf_op jit(solution)/shard_map/ppermute | solution.py:364
  28.3 9.4 %collective-permute-start.5 = (bf16[2,2,4,64,256]{4,3,2,1,0:T(8,128)(2,1)S(1)}, bf16[2,2,4,64,256]{4,3,2,1,0:T(8,128)(2,1)S(1)}, u32[]{:S(2)}, u32[]{:S(2)}) collective-permute-start(bf16[2,2,4,64,256]{4,3,2,1,0:T(8,128)(2,1)S(1)} %get-tuple-element.31), channel_id=1, source_target_pairs={{0,64},{64,0},{128,192},{192,128},{1,65},{65,1},{129,193},{193,129... | collective-permute-start | bytes 1572872 | tf_op jit(solution)/shard_map/ppermute | solution.py:368
  35.8 1.9 %collective-permute-start.4 = (bf16[2,256,256]{2,1,0:T(8,128)(2,1)S(1)}, bf16[2,256,256]{2,1,0:T(8,128)(2,1)S(1)}, u32[]{:S(2)}, u32[]{:S(2)}) collective-permute-start(bf16[2,256,256]{2,1,0:T(8,128)(2,1)S(1)} %collective-permute-done.1.piece), channel_id=1, source_target_pairs={{0,64},{64,0},{128,192},{192,128},{1,65},{65,1},{129,193},{193,129... | collective-permute-start | bytes 786440 | tf_op jit(solution)/shard_map/ppermute | solution.py:368

commit v9 on v7

--- a/solution.py
+++ b/solution.py
@@ -360,8 +360,12 @@
 
 
 def along_y(value, steps):
-    pairs = [(b, b // PLANE * PLANE + (b + steps) % PLANE) for b in range(BLOCKS)]
-    return lax.ppermute(value, "blk", pairs)
+    pairs = [
+        (g * BLOCKS + b, g * BLOCKS + b // PLANE * PLANE + (b + steps[g % 2]) % PLANE)
+        for g in range(4)
+        for b in range(BLOCKS)
+    ]
+    return lax.ppermute(value, ("grp", "blk"), pairs)
 
 
 def other_core(value):
@@ -375,11 +379,11 @@
     got = planes_back(own)
     cols, rows = tables(place, shift_table, flip_table)
     sums, kept = open_sums(own, cols, rows, ph_in, pp_in)
-    right, left, middle = route(place, y, kept, got, (1, 3, 2))
-    right, left = along_y(right, 1), along_y(left, 3)
+    right, left, middle = route(place, y, kept, got, (3, 1, 2))
+    right, left = along_y(right, (1, 3)), along_y(left, (3, 1))
     (sums,) = spread([got], cols, rows, sums)
     middle, sums = lax.optimization_barrier((middle, sums))
-    middle = along_y(middle, 2)
+    middle = along_y(middle, (2, 2))
     right, sums = lax.optimization_barrier((right, sums))
     (sums,) = spread([right], cols, rows, sums)
     left, sums = lax.optimization_barrier((left, sums))

time: 39.3 us -> 44.4 us (1.13)
  waiting for transfers between devices: 5.17 us -> 10.3 us
    ppermute x3, waiting for transfers between devices: 0.01 us -> 4.47 us  [along_y(): return lax.ppermute(value, ('grp', 'blk'), pairs)]
    ppermute x2, waiting for transfers between devices: 0.09 us -> 0.73 us  [other_core(): return lax.ppermute(value, 'grp', [(s, s ^ 1) for s in range(4)])]
  transfers between devices with their start and end apart: 6 -> 6, of which waited for: 2 -> 3; matrix products, arithmetic and copies ran while one was open for 0% -> 0% of each run, Pallas kernels for 31% -> 27%
where the time goes in v9:
time: 44.4 us; the launch traced here: 44.2 us
  starting transfers between devices  16 us (36%)
  Pallas kernels  15.7 us (35%)
  waiting for transfers between devices  10.3 us (23%)
  local copies, waits for them, and re-layouts  1.38 us (3%)
  between operations  0.88 us (2%)
    ppermute x2, starting transfers between devices, other_core(): return lax.ppermute(value, 'grp', [(s, s ^ 1) for s in range(4)])  7.46 us
    pallas_call x3, Pallas kernels, spread(): pl.pallas_call(functools.partial(spread_kernel, count, fresh, send), out_...  5.78 us
    ppermute x1, waiting for transfers between devices, planes_back(): return lax.ppermute(value, ('grp', 'blk'), pairs)  5.07 us
    ppermute x3, starting transfers between devices, along_y(): return lax.ppermute(value, ('grp', 'blk'), pairs)  4.72 us
    ppermute x3, waiting for transfers between devices, along_y(): return lax.ppermute(value, ('grp', 'blk'), pairs)  4.47 us
    ppermute x1, starting transfers between devices, planes_back(): return lax.ppermute(value, ('grp', 'blk'), pairs)  3.82 us
    pallas_call x1, Pallas kernels, tables(): pl.pallas_call(table_kernel, out_shape=(jax.ShapeDtypeStruct((2 * TRANS +...  3.61 us
    pallas_call x1, Pallas kernels, close_sums(): pl.pallas_call(close_kernel, out_shape=(jax.ShapeDtypeStruct(SUMS, F32),)...  1.95 us
  transfers between devices with their start and end apart: 6, of which 3 were waited for; matrix products, arithmetic and copies ran while one was open for 0% of the time, Pallas kernels for 27%

profile of v9, /device:TPU:1, one launch (start us, length us, event | category | flops | bytes accessed | tf_op | source)
XLA Modules:
  0.0 44.2 jit_solution(12352133440187922977)
XLA Ops:
  0.6 1.7 %scale.1.piece = bf16[2,256,256]{2,1,0:T(8,128)(2,1)} custom-call(bf16[1,2,256,256]{3,2,1,0:T(8,128)(2,1)} %masses.1, s32[1,256]{1,0:T(1,128)} %spins.1), custom_call_target="tpu_custom_call" | custom-call | flops 1 | bytes 1 | tf_op jit(solution)/shard_map/scale/pallas_call | solution.py:306
  2.3 3.8 %collective-permute-start = (bf16[2,256,256]{2,1,0:T(8,128)(2,1)}, bf16[2,256,256]{2,1,0:T(8,128)(2,1)S(1)}, u32[]{:S(2)}, u32[]{:S(2)}) collective-permute-start(bf16[2,256,256]{2,1,0:T(8,128)(2,1)} %scale.1.piece), channel_id=1, source_target_pairs={{0,4},{1,5},{2,6},{3,7},{4,8},{5,9},{6,10},{7,11},{8,12},{9,13},{1... | collective-permute-start | bytes 786440 | tf_op jit(solution)/shard_map/ppermute | solution.py:359
  6.2 0.0 copy-start.3
  6.2 0.7 %copy-done.3 = s32[4,256]{1,0:T(4,128)S(1)} copy-done((s32[4,256]{1,0:T(4,128)S(1)}, s32[4,256]{1,0:T(4,128)}, u32[]{:S(2)}) %copy-start.3) | copy-done | bytes 4120
  6.8 0.0 copy-start.4
  6.8 0.7 %copy-done.4 = s32[4,256]{1,0:T(4,128)S(1)} copy-done((s32[4,256]{1,0:T(4,128)S(1)}, s32[4,256]{1,0:T(4,128)}, u32[]{:S(2)}) %copy-start.4) | copy-done | bytes 4120
  7.5 0.0 copy-start
  7.5 0.0 copy-start.1
  7.5 0.0 copy-start.2
  7.5 3.6 %tables.1 = (bf16[9,512,256]{2,1,0:T(8,128)(2,1)S(1)}, bf16[2,1152,256]{2,1,0:T(8,128)(2,1)S(1)}) custom-call(s32[1]{0:T(128)} %bitcast.place_ref.place, s32[4,256]{1,0:T(4,128)S(1)} %copy-done.3, s32[4,256]{1,0:T(4,128)S(1)} %copy-done.4), custom_call_target="tpu_custom_call" | custom-call | flops 4000000000 | bytes 1 | tf_op jit(solution)/shard_map/tables/pallas_call | solution.py:83
  11.2 0.0 copy-done
  11.2 0.0 copy-done.1
  11.2 0.0 copy-done.2
  11.2 1.5 %open_sums.1 = (f32[2,2,4,64,256]{4,3,2,1,0:T(8,128)S(1)}, bf16[2,256,256]{2,1,0:T(8,128)(2,1)S(1)}) custom-call(bf16[2,256,256]{2,1,0:T(8,128)(2,1)S(1)} %copy-done, bf16[9,512,256]{2,1,0:T(8,128)(2,1)S(1)} %get-tuple-element.19.cols.refs_1_, bf16[2,1152,256]{2,1,0:T(8,128)(2,1)S(1)} %get-tuple-element.20.rows.refs_2_, f32[2,4,64,256]{3,2,1,0:T(8,128)S(1)} %copy-done.1, ...), custom_call_target="tpu_custom_call" | custom-call | flops 4000000000 | bytes 1 | tf_op jit(solution)/shard_map/open_sums/pallas_call | solution.py:184
  12.7 5.1 %collective-permute-done.got.refs_0_ = bf16[2,256,256]{2,1,0:T(8,128)(2,1)S(1)} collective-permute-done((bf16[2,256,256]{2,1,0:T(8,128)(2,1)}, bf16[2,256,256]{2,1,0:T(8,128)(2,1)S(1)}, u32[]{:S(2)}, u32[]{:S(2)}) %collective-permute-start) | collective-permute-done | bytes 262176 | tf_op jit(solution)/shard_map/ppermute | solution.py:359
  17.8 0.1 route.1
  17.9 2.8 %collective-permute-start.3 = (bf16[2,256,256]{2,1,0:T(8,128)(2,1)S(1)}, bf16[2,256,256]{2,1,0:T(8,128)(2,1)S(1)}, u32[]{:S(2)}, u32[]{:S(2)}) collective-permute-start(bf16[2,256,256]{2,1,0:T(8,128)(2,1)S(1)} %get-tuple-element.26), channel_id=1, source_target_pairs={{0,1},{1,2},{2,3},{3,0},{4,5},{5,6},{6,7},{7,4},{8,9},{9,10},{10,1... | collective-permute-start | bytes 786440 | tf_op jit(solution)/shard_map/ppermute | solution.py:368
  20.7 0.0 collective-permute-start.2
  20.7 1.9 %spread.3.refs_3_ = f32[4,2,4,64,256]{4,3,2,1,0:T(8,128)S(1)} custom-call(bf16[2,256,256]{2,1,0:T(8,128)(2,1)S(1)} %collective-permute-done.got.refs_0_, bf16[9,512,256]{2,1,0:T(8,128)(2,1)S(1)} %get-tuple-element.19.cols.refs_1_, bf16[2,1152,256]{2,1,0:T(8,128)(2,1)S(1)} %get-tuple-element.20.rows.refs_2_, f32[2,2,4,64,256]{4,3,2,1,0:T(8,128)S(1)} %get-tuple-element.23.refs_3_), custom_call_target="tpu_custom_call" | custom-call | flops 1 | bytes 1 | tf_op jit(solution)/shard_map/spread/pallas_call | solution.py:230
  22.6 1.9 %collective-permute-start.1 = (bf16[2,256,256]{2,1,0:T(8,128)(2,1)S(1)}, bf16[2,256,256]{2,1,0:T(8,128)(2,1)S(1)}, u32[]{:S(2)}, u32[]{:S(2)}) collective-permute-start(bf16[2,256,256]{2,1,0:T(8,128)(2,1)S(1)} %get-tuple-element.24), channel_id=1, source_target_pairs={{0,2},{1,3},{2,0},{3,1},{4,6},{5,7},{6,4},{7,5},{8,10},{9,11},{10,... | collective-permute-start | bytes 786440 | tf_op jit(solution)/shard_map/ppermute | solution.py:368
  24.5 0.0 collective-permute-done.3.refs_0_
  24.5 1.9 %spread.4.refs_3_ = f32[4,2,4,64,256]{4,3,2,1,0:T(8,128)S(1)} custom-call(bf16[2,256,256]{2,1,0:T(8,128)(2,1)S(1)} %collective-permute-done.3.refs_0_, bf16[9,512,256]{2,1,0:T(8,128)(2,1)S(1)} %get-tuple-element.19.cols.refs_1_, bf16[2,1152,256]{2,1,0:T(8,128)(2,1)S(1)} %get-tuple-element.20.rows.refs_2_, f32[4,2,4,64,256]{4,3,2,1,0:T(8,128)S(1)} %spread.3.refs_3_), custom_call_target="tpu_custom_call" | custom-call | flops 1 | bytes 1 | tf_op jit(solution)/shard_map/spread/pallas_call | solution.py:230
  26.5 4.5 %collective-permute-done.2.refs_0_ = bf16[2,256,256]{2,1,0:T(8,128)(2,1)S(1)} collective-permute-done((bf16[2,256,256]{2,1,0:T(8,128)(2,1)S(1)}, bf16[2,256,256]{2,1,0:T(8,128)(2,1)S(1)}, u32[]{:S(2)}, u32[]{:S(2)}) %collective-permute-start.2) | collective-permute-done | bytes 262176 | tf_op jit(solution)/shard_map/ppermute | solution.py:368
  30.9 1.9 %spread.5 = (f32[2,2,4,64,256]{4,3,2,1,0:T(8,128)S(1)}, bf16[2,2,4,64,256]{4,3,2,1,0:T(8,128)(2,1)S(1)}) custom-call(bf16[2,256,256]{2,1,0:T(8,128)(2,1)S(1)} %collective-permute-done.2.refs_0_, bf16[9,512,256]{2,1,0:T(8,128)(2,1)S(1)} %get-tuple-element.19.cols.refs_1_, bf16[2,1152,256]{2,1,0:T(8,128)(2,1)S(1)} %get-tuple-element.20.rows.refs_2_, ...), custom_call_target="tpu_custom_call" | custom-call | flops 1 | bytes 1 | tf_op jit(solution)/shard_map/spread/pallas_call | solution.py:230
  32.9 7.4 %collective-permute-start.5 = (bf16[2,2,4,64,256]{4,3,2,1,0:T(8,128)(2,1)S(1)}, bf16[2,2,4,64,256]{4,3,2,1,0:T(8,128)(2,1)S(1)}, u32[]{:S(2)}, u32[]{:S(2)}) collective-permute-start(bf16[2,2,4,64,256]{4,3,2,1,0:T(8,128)(2,1)S(1)} %get-tuple-element.35), channel_id=1, source_target_pairs={{0,64},{64,0},{128,192},{192,128},{1,65},{65,1},{129,193},{193,129... | collective-permute-start | bytes 1572872 | tf_op jit(solution)/shard_map/ppermute | solution.py:372
  40.2 0.0 collective-permute-done.1.piece
  40.2 0.1 collective-permute-start.4
  40.3 1.1 %add.6.sums = f32[2,2,4,64,256]{4,3,2,1,0:T(8,128)S(1)} custom-call(bf16[2,256,256]{2,1,0:T(8,128)(2,1)S(1)} %collective-permute-done.1.piece, bf16[9,512,256]{2,1,0:T(8,128)(2,1)S(1)} %get-tuple-element.19.cols.refs_1_, bf16[2,1152,256]{2,1,0:T(8,128)(2,1)S(1)} %get-tuple-element.20.rows.refs_2_, f32[2,2,4,64,256]{4,3,2,1,0:T(8,128)S(1)} %get-tuple-element.34.before), custom_call_target="tpu_custom_call" | custom-call | flops 1 | bytes 1 | tf_op jit(solution)/shard_map/add/pallas_call | solution.py:252
  41.4 0.7 %collective-permute-done.4.piece = bf16[2,256,256]{2,1,0:T(8,128)(2,1)S(1)} collective-permute-done((bf16[2,256,256]{2,1,0:T(8,128)(2,1)S(1)}, bf16[2,256,256]{2,1,0:T(8,128)(2,1)S(1)}, u32[]{:S(2)}, u32[]{:S(2)}) %collective-permute-start.4) | collective-permute-done | bytes 262176 | tf_op jit(solution)/shard_map/ppermute | solution.py:372
  42.1 0.0 collective-permute-done.5.others
  42.1 1.9 %close_sums.1 = (f32[2,4,64,256]{3,2,1,0:T(8,128)}, f32[2,4,64,256]{3,2,1,0:T(8,128)}) custom-call(bf16[2,256,256]{2,1,0:T(8,128)(2,1)S(1)} %collective-permute-done.4.piece, bf16[9,512,256]{2,1,0:T(8,128)(2,1)S(1)} %get-tuple-element.19.cols.refs_1_, bf16[2,1152,256]{2,1,0:T(8,128)(2,1)S(1)} %get-tuple-element.20.rows.refs_2_, ...), custom_call_target="tpu_custom_call" | custom-call | flops 1 | bytes 1 | tf_op jit(solution)/shard_map/close_sums/pallas_call | solution.py:286
Async XLA Ops:
  2.3 15.4 %collective-permute-start = (bf16[2,256,256]{2,1,0:T(8,128)(2,1)}, bf16[2,256,256]{2,1,0:T(8,128)(2,1)S(1)}, u32[]{:S(2)}, u32[]{:S(2)}) collective-permute-start(bf16[2,256,256]{2,1,0:T(8,128)(2,1)} %scale.1.piece), channel_id=1, source_target_pairs={{0,4},{1,5},{2,6},{3,7},{4,8},{5,9},{6,10},{7,11},{8,12},{9,13},{1... | collective-permute-start | bytes 786440 | tf_op jit(solution)/shard_map/ppermute | solution.py:359
  6.2 0.7 %copy-start.3 = (s32[4,256]{1,0:T(4,128)S(1)}, s32[4,256]{1,0:T(4,128)}, u32[]{:S(2)}) copy-start(s32[4,256]{1,0:T(4,128)} %shift_in.1) | copy-start | bytes 12292
  6.8 0.7 %copy-start.4 = (s32[4,256]{1,0:T(4,128)S(1)}, s32[4,256]{1,0:T(4,128)}, u32[]{:S(2)}) copy-start(s32[4,256]{1,0:T(4,128)} %flip_in.1) | copy-start | bytes 12292
  7.5 3.6 %copy-start = (bf16[2,256,256]{2,1,0:T(8,128)(2,1)S(1)}, bf16[2,256,256]{2,1,0:T(8,128)(2,1)}, u32[]{:S(2)}) copy-start(bf16[2,256,256]{2,1,0:T(8,128)(2,1)} %scale.1.piece) | copy-start | bytes 786436
  7.5 3.6 %copy-start.1 = (f32[2,4,64,256]{3,2,1,0:T(8,128)S(1)}, f32[2,4,64,256]{3,2,1,0:T(8,128)}, u32[]{:S(2)}) copy-start(f32[2,4,64,256]{3,2,1,0:T(8,128)} %ph_in.1) | copy-start | bytes 1572868
  7.5 3.6 %copy-start.2 = (f32[2,4,64,256]{3,2,1,0:T(8,128)S(1)}, f32[2,4,64,256]{3,2,1,0:T(8,128)}, u32[]{:S(2)}) copy-start(f32[2,4,64,256]{3,2,1,0:T(8,128)} %pp_in.1) | copy-start | bytes 1572868
  17.9 6.6 %collective-permute-start.3 = (bf16[2,256,256]{2,1,0:T(8,128)(2,1)S(1)}, bf16[2,256,256]{2,1,0:T(8,128)(2,1)S(1)}, u32[]{:S(2)}, u32[]{:S(2)}) collective-permute-start(bf16[2,256,256]{2,1,0:T(8,128)(2,1)S(1)} %get-tuple-element.26), channel_id=1, source_target_pairs={{0,1},{1,2},{2,3},{3,0},{4,5},{5,6},{6,7},{7,4},{8,9},{9,10},{10,1... | collective-permute-start | bytes 786440 | tf_op jit(solution)/shard_map/ppermute | solution.py:368
  20.7 10.2 %collective-permute-start.2 = (bf16[2,256,256]{2,1,0:T(8,128)(2,1)S(1)}, bf16[2,256,256]{2,1,0:T(8,128)(2,1)S(1)}, u32[]{:S(2)}, u32[]{:S(2)}) collective-permute-start(bf16[2,256,256]{2,1,0:T(8,128)(2,1)S(1)} %get-tuple-element.25), channel_id=1, source_target_pairs={{0,3},{1,0},{2,1},{3,2},{4,7},{5,4},{6,5},{7,6},{8,11},{9,8},{10,9... | collective-permute-start | bytes 786440 | tf_op jit(solution)/shard_map/ppermute | solution.py:368
  22.6 17.6 %collective-permute-start.1 = (bf16[2,256,256]{2,1,0:T(8,128)(2,1)S(1)}, bf16[2,256,256]{2,1,0:T(8,128)(2,1)S(1)}, u32[]{:S(2)}, u32[]{:S(2)}) collective-permute-start(bf16[2,256,256]{2,1,0:T(8,128)(2,1)S(1)} %get-tuple-element.24), channel_id=1, source_target_pairs={{0,2},{1,3},{2,0},{3,1},{4,6},{5,7},{6,4},{7,5},{8,10},{9,11},{10,... | collective-permute-start | bytes 786440 | tf_op jit(solution)/shard_map/ppermute | solution.py:368
  32.9 9.3 %collective-permute-start.5 = (bf16[2,2,4,64,256]{4,3,2,1,0:T(8,128)(2,1)S(1)}, bf16[2,2,4,64,256]{4,3,2,1,0:T(8,128)(2,1)S(1)}, u32[]{:S(2)}, u32[]{:S(2)}) collective-permute-start(bf16[2,2,4,64,256]{4,3,2,1,0:T(8,128)(2,1)S(1)} %get-tuple-element.35), channel_id=1, source_target_pairs={{0,64},{64,0},{128,192},{192,128},{1,65},{65,1},{129,193},{193,129... | collective-permute-start | bytes 1572872 | tf_op jit(solution)/shard_map/ppermute | solution.py:372
  40.2 1.9 %collective-permute-start.4 = (bf16[2,256,256]{2,1,0:T(8,128)(2,1)S(1)}, bf16[2,256,256]{2,1,0:T(8,128)(2,1)S(1)}, u32[]{:S(2)}, u32[]{:S(2)}) collective-permute-start(bf16[2,256,256]{2,1,0:T(8,128)(2,1)S(1)} %collective-permute-done.1.piece), channel_id=1, source_target_pairs={{0,64},{64,0},{128,192},{192,128},{1,65},{65,1},{129,193},{193,129... | collective-permute-start | bytes 786440 | tf_op jit(solution)/shard_map/ppermute | solution.py:372

commit v10 on v7

--- a/solution.py
+++ b/solution.py
@@ -296,18 +296,27 @@
     )(piece, cols, rows, sums, others)
 
 
-def scale_kernel(masses, spins, out):
+def scale_kernel(masses, spins, out, raw, done, sems):
+    loads = [pltpu.make_async_copy(masses.at[0, s], raw.at[s], sems.at[0, s]) for s in range(2)]
+    stores = [pltpu.make_async_copy(done.at[s], out.at[s], sems.at[1, s]) for s in range(2)]
+    for load in loads:
+        load.start()
     signed = (2 * spins[...] - 1).astype(F32)
-    for spin, sign in enumerate((COUPLING, -COUPLING)):
-        out[spin] = (masses[0, spin].astype(F32) * jnp.exp(sign * signed)).astype(BF)
+    for s, sign in enumerate((COUPLING, -COUPLING)):
+        loads[s].wait()
+        done[s] = (raw[s].astype(F32) * jnp.exp(sign * signed)).astype(BF)
+        stores[s].start()
+    for store in stores:
+        store.wait()
 
 
 def scale(masses, spins):
     return pl.pallas_call(
         scale_kernel,
         out_shape=jax.ShapeDtypeStruct(PIECE, BF),
-        in_specs=[IN_VMEM] * 2,
-        out_specs=IN_VMEM,
+        in_specs=[ANYWHERE, IN_VMEM],
+        out_specs=ANYWHERE,
+        scratch_shapes=[pltpu.VMEM(PIECE, BF)] * 2 + [pltpu.SemaphoreType.DMA((2, 2))],
         cost_estimate=TINY,
         compiler_params=pltpu.CompilerParams(vmem_limit_bytes=56 * MIB),
         name="scale",

time: 39.3 us -> 40.9 us (1.041)
  the two profiles are of different devices: /device:TPU:1 before, /device:TPU:25 now
where the time goes in v10:
time: 40.9 us; the launch traced here: 40.7 us
  Pallas kernels  16.4 us (40%)
  starting transfers between devices  15.6 us (38%)
  waiting for transfers between devices  6.47 us (16%)
  local copies, waits for them, and re-layouts  1.38 us (3%)
  between operations  0.9 us (2%)
    ppermute x2, starting transfers between devices, other_core(): return lax.ppermute(value, 'grp', [(s, s ^ 1) for s in range(4)])  9.78 us
    pallas_call x3, Pallas kernels, spread(): pl.pallas_call(functools.partial(spread_kernel, count, fresh, send), out_...  5.78 us
    ppermute x1, waiting for transfers between devices, planes_back(): return lax.ppermute(value, ('grp', 'blk'), pairs)  5.11 us
    pallas_call x1, Pallas kernels, tables(): pl.pallas_call(table_kernel, out_shape=(jax.ShapeDtypeStruct((2 * TRANS +...  3.6 us
    ppermute x1, starting transfers between devices, planes_back(): return lax.ppermute(value, ('grp', 'blk'), pairs)  3.07 us
    ppermute x3, starting transfers between devices, along_y(): return lax.ppermute(value, 'blk', pairs)  2.75 us
    pallas_call x1, Pallas kernels, scale(): pl.pallas_call(scale_kernel, out_shape=jax.ShapeDtypeStruct(PIECE, BF), i...  2.36 us
    pallas_call x1, Pallas kernels, close_sums(): pl.pallas_call(close_kernel, out_shape=(jax.ShapeDtypeStruct(SUMS, F32),)...  1.95 us
  transfers between devices with their start and end apart: 6, of which 3 were waited for; matrix products, arithmetic and copies ran while one was open for 0% of the time, Pallas kernels for 29%

profile of v10, /device:TPU:25, one launch (start us, length us, event | category | flops | bytes accessed | tf_op | source)
XLA Modules:
  0.0 40.7 jit_solution(15925995864174859449)
XLA Ops:
  0.6 2.4 %scale.1.piece = bf16[2,256,256]{2,1,0:T(8,128)(2,1)} custom-call(bf16[1,2,256,256]{3,2,1,0:T(8,128)(2,1)} %masses.1, s32[1,256]{1,0:T(1,128)} %spins.1), custom_call_target="tpu_custom_call" | custom-call | flops 1 | bytes 1 | tf_op jit(solution)/shard_map/scale/pallas_call | solution.py:314
  3.0 3.1 %collective-permute-start = (bf16[2,256,256]{2,1,0:T(8,128)(2,1)}, bf16[2,256,256]{2,1,0:T(8,128)(2,1)S(1)}, u32[]{:S(2)}, u32[]{:S(2)}) collective-permute-start(bf16[2,256,256]{2,1,0:T(8,128)(2,1)} %scale.1.piece), channel_id=1, source_target_pairs={{0,4},{1,5},{2,6},{3,7},{4,8},{5,9},{6,10},{7,11},{8,12},{9,13},{1... | collective-permute-start | bytes 786440 | tf_op jit(solution)/shard_map/ppermute | solution.py:368
  6.1 0.0 copy-start.3
  6.1 0.7 %copy-done.3 = s32[4,256]{1,0:T(4,128)S(1)} copy-done((s32[4,256]{1,0:T(4,128)S(1)}, s32[4,256]{1,0:T(4,128)}, u32[]{:S(2)}) %copy-start.3) | copy-done | bytes 4120
  6.8 0.0 copy-start.4
  6.8 0.7 %copy-done.4 = s32[4,256]{1,0:T(4,128)S(1)} copy-done((s32[4,256]{1,0:T(4,128)S(1)}, s32[4,256]{1,0:T(4,128)}, u32[]{:S(2)}) %copy-start.4) | copy-done | bytes 4120
  7.4 0.0 copy-start
  7.4 0.0 copy-start.1
  7.4 0.0 copy-start.2
  7.4 3.6 %tables.1 = (bf16[9,512,256]{2,1,0:T(8,128)(2,1)S(1)}, bf16[2,1152,256]{2,1,0:T(8,128)(2,1)S(1)}) custom-call(s32[1]{0:T(128)} %bitcast.place_ref.place, s32[4,256]{1,0:T(4,128)S(1)} %copy-done.3, s32[4,256]{1,0:T(4,128)S(1)} %copy-done.4), custom_call_target="tpu_custom_call" | custom-call | flops 4000000000 | bytes 1 | tf_op jit(solution)/shard_map/tables/pallas_call | solution.py:83
  11.1 0.0 copy-done
  11.1 0.0 copy-done.1
  11.1 0.0 copy-done.2
  11.1 1.5 %open_sums.1 = (f32[2,2,4,64,256]{4,3,2,1,0:T(8,128)S(1)}, bf16[2,256,256]{2,1,0:T(8,128)(2,1)S(1)}) custom-call(bf16[2,256,256]{2,1,0:T(8,128)(2,1)S(1)} %copy-done, bf16[9,512,256]{2,1,0:T(8,128)(2,1)S(1)} %get-tuple-element.19.cols.refs_1_, bf16[2,1152,256]{2,1,0:T(8,128)(2,1)S(1)} %get-tuple-element.20.rows.refs_2_, f32[2,4,64,256]{3,2,1,0:T(8,128)S(1)} %copy-done.1, ...), custom_call_target="tpu_custom_call" | custom-call | flops 4000000000 | bytes 1 | tf_op jit(solution)/shard_map/open_sums/pallas_call | solution.py:184
  12.6 5.1 %collective-permute-done.got.refs_0_ = bf16[2,256,256]{2,1,0:T(8,128)(2,1)S(1)} collective-permute-done((bf16[2,256,256]{2,1,0:T(8,128)(2,1)}, bf16[2,256,256]{2,1,0:T(8,128)(2,1)S(1)}, u32[]{:S(2)}, u32[]{:S(2)}) %collective-permute-start) | collective-permute-done | bytes 262176 | tf_op jit(solution)/shard_map/ppermute | solution.py:368
  17.7 0.1 route.1
  17.8 0.1 collective-permute-start.3
  17.9 1.5 %collective-permute-start.2 = (bf16[2,256,256]{2,1,0:T(8,128)(2,1)S(1)}, bf16[2,256,256]{2,1,0:T(8,128)(2,1)S(1)}, u32[]{:S(2)}, u32[]{:S(2)}) collective-permute-start(bf16[2,256,256]{2,1,0:T(8,128)(2,1)S(1)} %get-tuple-element.25), channel_id=1, source_target_pairs={{0,3},{1,0},{2,1},{3,2},{4,7},{5,4},{6,5},{7,6},{8,11},{9,8},{10,9... | collective-permute-start | bytes 786440 | tf_op jit(solution)/shard_map/ppermute | solution.py:373
  19.4 1.9 %spread.3.refs_3_ = f32[4,2,4,64,256]{4,3,2,1,0:T(8,128)S(1)} custom-call(bf16[2,256,256]{2,1,0:T(8,128)(2,1)S(1)} %collective-permute-done.got.refs_0_, bf16[9,512,256]{2,1,0:T(8,128)(2,1)S(1)} %get-tuple-element.19.cols.refs_1_, bf16[2,1152,256]{2,1,0:T(8,128)(2,1)S(1)} %get-tuple-element.20.rows.refs_2_, f32[2,2,4,64,256]{4,3,2,1,0:T(8,128)S(1)} %get-tuple-element.23.refs_3_), custom_call_target="tpu_custom_call" | custom-call | flops 1 | bytes 1 | tf_op jit(solution)/shard_map/spread/pallas_call | solution.py:230
  21.3 1.2 %collective-permute-start.1 = (bf16[2,256,256]{2,1,0:T(8,128)(2,1)S(1)}, bf16[2,256,256]{2,1,0:T(8,128)(2,1)S(1)}, u32[]{:S(2)}, u32[]{:S(2)}) collective-permute-start(bf16[2,256,256]{2,1,0:T(8,128)(2,1)S(1)} %get-tuple-element.24), channel_id=1, source_target_pairs={{0,2},{1,3},{2,0},{3,1},{4,6},{5,7},{6,4},{7,5},{8,10},{9,11},{10,... | collective-permute-start | bytes 786440 | tf_op jit(solution)/shard_map/ppermute | solution.py:373
  22.5 0.6 %collective-permute-done.3.refs_0_ = bf16[2,256,256]{2,1,0:T(8,128)(2,1)S(1)} collective-permute-done((bf16[2,256,256]{2,1,0:T(8,128)(2,1)S(1)}, bf16[2,256,256]{2,1,0:T(8,128)(2,1)S(1)}, u32[]{:S(2)}, u32[]{:S(2)}) %collective-permute-start.3) | collective-permute-done | bytes 262176 | tf_op jit(solution)/shard_map/ppermute | solution.py:373
  23.1 1.9 %spread.4.refs_3_ = f32[4,2,4,64,256]{4,3,2,1,0:T(8,128)S(1)} custom-call(bf16[2,256,256]{2,1,0:T(8,128)(2,1)S(1)} %collective-permute-done.3.refs_0_, bf16[9,512,256]{2,1,0:T(8,128)(2,1)S(1)} %get-tuple-element.19.cols.refs_1_, bf16[2,1152,256]{2,1,0:T(8,128)(2,1)S(1)} %get-tuple-element.20.rows.refs_2_, f32[4,2,4,64,256]{4,3,2,1,0:T(8,128)S(1)} %spread.3.refs_3_), custom_call_target="tpu_custom_call" | custom-call | flops 1 | bytes 1 | tf_op jit(solution)/shard_map/spread/pallas_call | solution.py:230
  25.1 0.0 collective-permute-done.2.refs_0_
  25.1 1.9 %spread.5 = (f32[2,2,4,64,256]{4,3,2,1,0:T(8,128)S(1)}, bf16[2,2,4,64,256]{4,3,2,1,0:T(8,128)(2,1)S(1)}) custom-call(bf16[2,256,256]{2,1,0:T(8,128)(2,1)S(1)} %collective-permute-done.2.refs_0_, bf16[9,512,256]{2,1,0:T(8,128)(2,1)S(1)} %get-tuple-element.19.cols.refs_1_, bf16[2,1152,256]{2,1,0:T(8,128)(2,1)S(1)} %get-tuple-element.20.rows.refs_2_, ...), custom_call_target="tpu_custom_call" | custom-call | flops 1 | bytes 1 | tf_op jit(solution)/shard_map/spread/pallas_call | solution.py:230
  27.0 9.7 %collective-permute-start.5 = (bf16[2,2,4,64,256]{4,3,2,1,0:T(8,128)(2,1)S(1)}, bf16[2,2,4,64,256]{4,3,2,1,0:T(8,128)(2,1)S(1)}, u32[]{:S(2)}, u32[]{:S(2)}) collective-permute-start(bf16[2,2,4,64,256]{4,3,2,1,0:T(8,128)(2,1)S(1)} %get-tuple-element.35), channel_id=1, source_target_pairs={{0,64},{64,0},{128,192},{192,128},{1,65},{65,1},{129,193},{193,129... | collective-permute-start | bytes 1572872 | tf_op jit(solution)/shard_map/ppermute | solution.py:377
  36.7 0.0 collective-permute-done.1.piece
  36.7 0.1 collective-permute-start.4
  36.8 1.1 %add.6.sums = f32[2,2,4,64,256]{4,3,2,1,0:T(8,128)S(1)} custom-call(bf16[2,256,256]{2,1,0:T(8,128)(2,1)S(1)} %collective-permute-done.1.piece, bf16[9,512,256]{2,1,0:T(8,128)(2,1)S(1)} %get-tuple-element.19.cols.refs_1_, bf16[2,1152,256]{2,1,0:T(8,128)(2,1)S(1)} %get-tuple-element.20.rows.refs_2_, f32[2,2,4,64,256]{4,3,2,1,0:T(8,128)S(1)} %get-tuple-element.34.before), custom_call_target="tpu_custom_call" | custom-call | flops 1 | bytes 1 | tf_op jit(solution)/shard_map/add/pallas_call | solution.py:252
  37.9 0.7 %collective-permute-done.4.piece = bf16[2,256,256]{2,1,0:T(8,128)(2,1)S(1)} collective-permute-done((bf16[2,256,256]{2,1,0:T(8,128)(2,1)S(1)}, bf16[2,256,256]{2,1,0:T(8,128)(2,1)S(1)}, u32[]{:S(2)}, u32[]{:S(2)}) %collective-permute-start.4) | collective-permute-done | bytes 262176 | tf_op jit(solution)/shard_map/ppermute | solution.py:377
  38.6 0.0 collective-permute-done.5.others
  38.6 2.0 %close_sums.1 = (f32[2,4,64,256]{3,2,1,0:T(8,128)}, f32[2,4,64,256]{3,2,1,0:T(8,128)}) custom-call(bf16[2,256,256]{2,1,0:T(8,128)(2,1)S(1)} %collective-permute-done.4.piece, bf16[9,512,256]{2,1,0:T(8,128)(2,1)S(1)} %get-tuple-element.19.cols.refs_1_, bf16[2,1152,256]{2,1,0:T(8,128)(2,1)S(1)} %get-tuple-element.20.rows.refs_2_, ...), custom_call_target="tpu_custom_call" | custom-call | flops 1 | bytes 1 | tf_op jit(solution)/shard_map/close_sums/pallas_call | solution.py:286
Async XLA Ops:
  3.0 14.7 %collective-permute-start = (bf16[2,256,256]{2,1,0:T(8,128)(2,1)}, bf16[2,256,256]{2,1,0:T(8,128)(2,1)S(1)}, u32[]{:S(2)}, u32[]{:S(2)}) collective-permute-start(bf16[2,256,256]{2,1,0:T(8,128)(2,1)} %scale.1.piece), channel_id=1, source_target_pairs={{0,4},{1,5},{2,6},{3,7},{4,8},{5,9},{6,10},{7,11},{8,12},{9,13},{1... | collective-permute-start | bytes 786440 | tf_op jit(solution)/shard_map/ppermute | solution.py:368
  6.1 0.7 %copy-start.3 = (s32[4,256]{1,0:T(4,128)S(1)}, s32[4,256]{1,0:T(4,128)}, u32[]{:S(2)}) copy-start(s32[4,256]{1,0:T(4,128)} %shift_in.1) | copy-start | bytes 12292
  6.8 0.7 %copy-start.4 = (s32[4,256]{1,0:T(4,128)S(1)}, s32[4,256]{1,0:T(4,128)}, u32[]{:S(2)}) copy-start(s32[4,256]{1,0:T(4,128)} %flip_in.1) | copy-start | bytes 12292
  7.4 3.6 %copy-start = (bf16[2,256,256]{2,1,0:T(8,128)(2,1)S(1)}, bf16[2,256,256]{2,1,0:T(8,128)(2,1)}, u32[]{:S(2)}) copy-start(bf16[2,256,256]{2,1,0:T(8,128)(2,1)} %scale.1.piece) | copy-start | bytes 786436
  7.4 3.6 %copy-start.1 = (f32[2,4,64,256]{3,2,1,0:T(8,128)S(1)}, f32[2,4,64,256]{3,2,1,0:T(8,128)}, u32[]{:S(2)}) copy-start(f32[2,4,64,256]{3,2,1,0:T(8,128)} %ph_in.1) | copy-start | bytes 1572868
  7.4 3.6 %copy-start.2 = (f32[2,4,64,256]{3,2,1,0:T(8,128)S(1)}, f32[2,4,64,256]{3,2,1,0:T(8,128)}, u32[]{:S(2)}) copy-start(f32[2,4,64,256]{3,2,1,0:T(8,128)} %pp_in.1) | copy-start | bytes 1572868
  17.8 5.3 %collective-permute-start.3 = (bf16[2,256,256]{2,1,0:T(8,128)(2,1)S(1)}, bf16[2,256,256]{2,1,0:T(8,128)(2,1)S(1)}, u32[]{:S(2)}, u32[]{:S(2)}) collective-permute-start(bf16[2,256,256]{2,1,0:T(8,128)(2,1)S(1)} %get-tuple-element.26), channel_id=1, source_target_pairs={{0,1},{1,2},{2,3},{3,0},{4,5},{5,6},{6,7},{7,4},{8,9},{9,10},{10,1... | collective-permute-start | bytes 786440 | tf_op jit(solution)/shard_map/ppermute | solution.py:373
  17.9 7.2 %collective-permute-start.2 = (bf16[2,256,256]{2,1,0:T(8,128)(2,1)S(1)}, bf16[2,256,256]{2,1,0:T(8,128)(2,1)S(1)}, u32[]{:S(2)}, u32[]{:S(2)}) collective-permute-start(bf16[2,256,256]{2,1,0:T(8,128)(2,1)S(1)} %get-tuple-element.25), channel_id=1, source_target_pairs={{0,3},{1,0},{2,1},{3,2},{4,7},{5,4},{6,5},{7,6},{8,11},{9,8},{10,9... | collective-permute-start | bytes 786440 | tf_op jit(solution)/shard_map/ppermute | solution.py:373
  21.3 15.4 %collective-permute-start.1 = (bf16[2,256,256]{2,1,0:T(8,128)(2,1)S(1)}, bf16[2,256,256]{2,1,0:T(8,128)(2,1)S(1)}, u32[]{:S(2)}, u32[]{:S(2)}) collective-permute-start(bf16[2,256,256]{2,1,0:T(8,128)(2,1)S(1)} %get-tuple-element.24), channel_id=1, source_target_pairs={{0,2},{1,3},{2,0},{3,1},{4,6},{5,7},{6,4},{7,5},{8,10},{9,11},{10,... | collective-permute-start | bytes 786440 | tf_op jit(solution)/shard_map/ppermute | solution.py:373
  27.0 11.6 %collective-permute-start.5 = (bf16[2,2,4,64,256]{4,3,2,1,0:T(8,128)(2,1)S(1)}, bf16[2,2,4,64,256]{4,3,2,1,0:T(8,128)(2,1)S(1)}, u32[]{:S(2)}, u32[]{:S(2)}) collective-permute-start(bf16[2,2,4,64,256]{4,3,2,1,0:T(8,128)(2,1)S(1)} %get-tuple-element.35), channel_id=1, source_target_pairs={{0,64},{64,0},{128,192},{192,128},{1,65},{65,1},{129,193},{193,129... | collective-permute-start | bytes 1572872 | tf_op jit(solution)/shard_map/ppermute | solution.py:377
  36.7 1.9 %collective-permute-start.4 = (bf16[2,256,256]{2,1,0:T(8,128)(2,1)S(1)}, bf16[2,256,256]{2,1,0:T(8,128)(2,1)S(1)}, u32[]{:S(2)}, u32[]{:S(2)}) collective-permute-start(bf16[2,256,256]{2,1,0:T(8,128)(2,1)S(1)} %collective-permute-done.1.piece), channel_id=1, source_target_pairs={{0,64},{64,0},{128,192},{192,128},{1,65},{65,1},{129,193},{193,129... | collective-permute-start | bytes 786440 | tf_op jit(solution)/shard_map/ppermute | solution.py:377
